TPU v7x, 32 devices: a whole 2x2x4 slice. The times are simulated.
32 devices in a mesh: queue: 16 (over z, y, x), tok: 2 (over core).
Axes of the slice: x: 2, y: 2, z: 4, core: 2. Of those that a mesh axis runs over, the one named last changes fastest.
Arguments:
- latent: float32 [16, 64, 64], P('queue', 'tok'), may hold values from -1.5 to 1.5
- fresh_noise: float32 [3, 64, 64], P(None, 'tok'), may hold values from -1.5 to 1.5
- frame_slot: int32 [16], replicated, may hold values from 0 to 15
- frame_reach: int32 [16], replicated, may hold values from 0 to 3, as said below
- level_embed: bfloat16 [19, 3072], P(None, 'tok'), may hold values from -0.59765625 to 0.59765625
- embed_weight: bfloat16 [64, 3072], P(None, 'tok'), may hold values from -0.75 to 0.75
- qkv_weight: bfloat16 [3, 1536, 3072], P(None, 'tok'), may hold values from -0.1100574 to 0.1100574
- qk_gain: float32 [2, 1536], P(None, 'tok'), may hold values from 0.5 to 6
- out_weight: bfloat16 [1536, 3072], P('tok'), may hold values from -0.5 to 0.5
- vel_weight: bfloat16 [3072, 64], P('tok'), may hold values from -0.5390625 to 0.5390625
Outputs:
- velocity: float32 [3, 16, 64, 64], P(None, 'queue', 'tok')
- queue_out: float32 [16, 64, 64], P('queue', 'tok')
Inputs may be any that keep to these rules, and one draw needn't show every extreme that they name: `frame_reach`: some position has width 3.
All inputs are finite; a program needn't handle non-finite values.
Results may differ from a plain program's by a relative error of at most 0.024.
Values may be sent and summed in bfloat16 or wider, within the bound.
No kernel may reach another device: no remote copies, remote signals or barrier semaphores. Data moves between devices by JAX's collectives and lax.ppermute only.
A program may use at most 64 MiB of HBM per device.

v0:
```python
import jax
import jax.numpy as jnp
from jax import lax
from jax.sharding import PartitionSpec as P

HD = 64
STEPS = 3
HALO = 3


EPS = 1e-06


def shifted(value, axis, steps):
    count = lax.axis_size(axis)
    initial, last = (max(0, -steps), min(count, count - steps))
    return lax.ppermute(value, axis, [(source, source + steps) for source in range(initial, last)])


def head_norm(projection, gain_row):
    row_count = projection.shape[0]
    head_count = gain_row.shape[0] // HD
    per_head = projection.reshape(row_count, head_count, HD)
    scaled = per_head * lax.rsqrt(jnp.mean(per_head * per_head, axis=-1, keepdims=True) + EPS)
    return (scaled * gain_row.reshape(head_count, HD)).astype(jnp.bfloat16)


def normalize(hidden):
    return (hidden * lax.rsqrt(jnp.mean(hidden * hidden, axis=-1, keepdims=True) + EPS)).astype(
        jnp.bfloat16
    )


def pick_entry(lookup, wanted):
    positions = jnp.arange(lookup.shape[0], dtype=jnp.int32)
    return jnp.sum(jnp.where(positions == wanted, lookup, 0))


def body(
    latent,
    fresh_noise,
    frame_slot,
    frame_reach,
    level_embed,
    embed_weight,
    qkv_weight,
    qk_gain,
    out_weight,
    vel_weight,
):
    full_embed, full_levels, full_vel = (
        lax.all_gather(embed_weight, "tok", axis=1, tiled=True),
        lax.all_gather(level_embed, "tok", axis=1, tiled=True),
        lax.all_gather(vel_weight, "tok", axis=0, tiled=True),
    )
    level_count = full_levels.shape[0]
    queue_count = lax.axis_size("queue")
    position = lax.axis_index("queue")
    tok_rows = latent.shape[1]
    frame_rows = tok_rows * lax.axis_size("tok")
    local_width = qkv_weight.shape[1]
    head_count = local_width // HD
    window_len = 2 * HALO + 1
    offsets = jnp.arange(window_len, dtype=jnp.int32) - HALO
    own_reach = pick_entry(frame_reach, position)
    target = position + offsets
    usable = (jnp.abs(offsets) <= own_reach) & (target >= 0) & (target < queue_count)
    vel_f = full_vel.astype(jnp.float32)
    queue_state = latent
    outputs = []
    for step_index in range(STEPS):
        arrived = shifted(queue_state, "queue", 1)
        queue_state = jnp.where(position == 0, fresh_noise[step_index][None], arrived)
        anchor = pick_entry(frame_slot, position - step_index - 1)
        noise_level = jnp.where(position >= step_index + 1, anchor + step_index, position)
        level_row = lax.dynamic_slice_in_dim(full_levels, noise_level, 1, 0).astype(jnp.float32)
        own_hidden = (
            jnp.dot(
                queue_state[0].astype(jnp.bfloat16), full_embed, preferred_element_type=jnp.float32
            )
            + level_row
        )
        projected = jnp.einsum(
            "td,ihd->ith",
            lax.all_gather(normalize(own_hidden), "tok", axis=0, tiled=True),
            qkv_weight,
            preferred_element_type=jnp.float32,
        )
        queries = head_norm(projected[0], qk_gain[0])
        key_rows = head_norm(projected[1], qk_gain[1]).reshape(frame_rows, local_width)
        values = projected[2].astype(jnp.bfloat16)
        key_value = jnp.stack([key_rows, values])
        window = []
        for offset_value in range(-HALO, HALO + 1):
            if offset_value == 0:
                window.append(key_value)
            else:
                window.append(shifted(key_value, "queue", -offset_value))
        stacked = jnp.stack(window)
        key_all = stacked[:, 0].reshape(window_len, frame_rows, head_count, HD)
        value_all = stacked[:, 1].reshape(window_len, frame_rows, head_count, HD)
        scores = jnp.einsum(
            "qhc,jkhc->hqjk", queries, key_all, preferred_element_type=jnp.float32
        ) * HD ** (-0.5)
        scores = jnp.where(usable[None, None, :, None], scores, -1e30)
        row_max = jnp.max(scores, axis=(2, 3), keepdims=True)
        expo = jnp.exp(scores - row_max)
        row_total = jnp.sum(expo, axis=(2, 3), keepdims=True)
        weights = (expo / row_total).astype(jnp.bfloat16)
        attended = jnp.einsum(
            "hqjk,jkhc->qhc", weights, value_all, preferred_element_type=jnp.float32
        )
        attended = attended.astype(jnp.bfloat16).reshape(frame_rows, local_width)
        widened = jnp.dot(attended, out_weight, preferred_element_type=jnp.float32)
        result = jnp.dot(widened, vel_f, precision=lax.Precision.HIGHEST)
        partial_value = lax.psum_scatter(
            result.astype(jnp.bfloat16), "tok", scatter_dimension=0, tiled=True
        ).astype(jnp.float32)
        velocity = partial_value + jnp.dot(own_hidden, vel_f, precision=lax.Precision.HIGHEST)
        queue_state = queue_state - (velocity / level_count)[None]
        outputs.append(velocity[None])
    return (jnp.stack(outputs), queue_state)


def solution(mesh):
    return jax.shard_map(
        body,
        mesh=mesh,
        in_specs=(
            P("queue", "tok", None),
            P(None, "tok", None),
            P(),
            P(),
            P(None, "tok"),
            P(None, "tok"),
            P(None, "tok", None),
            P(None, "tok"),
            P("tok", None),
            P("tok", None),
        ),
        out_specs=(P(None, "queue", "tok", None), P("queue", "tok", None)),
        check_vma=False,
    )
```

profile of v0, /device:TPU:0, one launch (start us, length us, event | category | flops | bytes accessed | tf_op | source)
XLA Modules:
  0.0 235.4 jit_solution(17513362828256787658)
XLA Ops:
  7.2 4.8 %collective-permute-start = (f32[1,32,64]{2,1,0:T(8,128)}, f32[1,32,64]{2,1,0:T(8,128)S(1)}, u32[]{:S(2)}, u32[]{:S(2)}) collective-permute-start(f32[1,32,64]{2,1,0:T(8,128)} %param.10), channel_id=1, source_target_pairs={{0,2},{2,4},{4,6},{6,8},{8,10},{10,12},{12,14},{14,16},{16,18},{18... | collective-permute-start | bytes 24584 | tf_op jit(solution)/shard_map/ppermute | solution.py:17
  22.1 3.7 %all_gather.21 = bf16[3072,64]{0,1:T(8,128)(2,1)} all-gather(bf16[1536,64]{0,1:T(8,128)(2,1)} %param.19), channel_id=1, replica_groups=mesh['queue'=16,'tok'=2] {'tok'}, dimensions={0}, use_global_device_ids=true | all-gather | bytes 589824 | tf_op jit(solution)/shard_map/all_gather | solution.py:54
  29.9 9.4 %convolution_bitcast_fusion.2 = f32[3,64,768]{2,1,0:T(8,128)S(1)} fusion(bf16[3,768,3072]{2,1,0:T(8,128)(2,1)} %param.16, bf16[64,3072]{1,0:T(8,128)(2,1)S(1)} %all_gather.20), kind=kOutput, calls=%fused_computation.29 | convolution fusion | flops 905969664 | bytes 15138816 | tf_op jit(solution)/shard_map/td,ihd->ith/dot_general | solution.py:83
  40.1 4.4 %collective-permute-start.1 = (bf16[2,64,768]{2,1,0:T(8,128)(2,1)S(1)}, bf16[2,64,768]{2,1,0:T(8,128)(2,1)S(1)}, u32[]{:S(2)}, u32[]{:S(2)}) collective-permute-start(bf16[2,64,768]{2,1,0:T(8,128)(2,1)S(1)} %pad_maximum_fusion), channel_id=1, source_target_pairs={{0,6},{2,8},{4,10},{6,12},{8,14},{10,16},{12,18},{14,20},{16,22},{... | collective-permute-start | bytes 589832 | tf_op jit(solution)/shard_map/ppermute | solution.py:17
  44.5 3.4 %collective-permute-start.2 = (bf16[2,64,768]{2,1,0:T(8,128)(2,1)S(1)}, bf16[2,64,768]{2,1,0:T(8,128)(2,1)S(1)}, u32[]{:S(2)}, u32[]{:S(2)}) collective-permute-start(bf16[2,64,768]{2,1,0:T(8,128)(2,1)S(1)} %pad_maximum_fusion), channel_id=1, source_target_pairs={{0,4},{2,6},{4,8},{6,10},{8,12},{10,14},{12,16},{14,18},{16,20},{1... | collective-permute-start | bytes 589832 | tf_op jit(solution)/shard_map/ppermute | solution.py:17
  55.0 6.5 %collective-permute-done.4 = bf16[2,64,768]{2,1,0:T(8,128)(2,1)S(1)} collective-permute-done((bf16[2,64,768]{2,1,0:T(8,128)(2,1)S(1)}, bf16[2,64,768]{2,1,0:T(8,128)(2,1)S(1)}, u32[]{:S(2)}, u32[]{:S(2)}) %collective-permute-start.4) | collective-permute-done | bytes 196640 | tf_op jit(solution)/shard_map/ppermute | solution.py:17
  61.6 5.0 %collective-permute-done.5 = bf16[2,64,768]{2,1,0:T(8,128)(2,1)S(1)} collective-permute-done((bf16[2,64,768]{2,1,0:T(8,128)(2,1)S(1)}, bf16[2,64,768]{2,1,0:T(8,128)(2,1)S(1)}, u32[]{:S(2)}, u32[]{:S(2)}) %collective-permute-start.5) | collective-permute-done | bytes 196640 | tf_op jit(solution)/shard_map/ppermute | solution.py:17
  70.7 3.4 %reshape_squeeze.30 = bf16[7,64,12,64]{3,2,1,0:T(8,128)(2,1)} reshape(bf16[7,1,64,768]{3,2,1,0:T(8,128)(2,1)} %get-tuple-element.11) | data formatting | bytes 1376256 | tf_op jit(solution)/shard_map/reshape;squeeze | solution.py:101
  79.1 9.0 %reduce-scatter.4.cloned.1.call-done = bf16[32,64]{1,0:T(8,128)(2,1)} async-done(((bf16[64,64]{1,0:T(8,128)(2,1)}), bf16[32,64]{1,0:T(8,128)(2,1)}) %reduce-scatter.4.cloned.1.call-update) | async-done | bytes 4112 | tf_op jit(solution)/shard_map/reduce_scatter | solution.py:116
  89.9 3.8 %collective-permute-start.7 = (f32[1,32,64]{2,1,0:T(8,128)S(1)}, f32[1,32,64]{2,1,0:T(8,128)S(1)}, u32[]{:S(2)}, u32[]{:S(2)}) collective-permute-start(f32[1,32,64]{2,1,0:T(8,128)S(1)} %get-tuple-element.24), channel_id=1, source_target_pairs={{0,2},{2,4},{4,6},{6,8},{8,10},{10,12},{12,14},{14,16},{16,18},{18... | collective-permute-start | bytes 24584 | tf_op jit(solution)/shard_map/ppermute | solution.py:17
  98.2 9.4 %convolution_bitcast_fusion.1 = f32[3,64,768]{2,1,0:T(8,128)S(1)} fusion(bf16[3,768,3072]{2,1,0:T(8,128)(2,1)} %param.16, bf16[64,3072]{1,0:T(8,128)(2,1)S(1)} %all_gather.22), kind=kOutput, calls=%fused_computation.28 | convolution fusion | flops 905969664 | bytes 15138816 | tf_op jit(solution)/shard_map/td,ihd->ith/dot_general | solution.py:83
  108.5 5.1 %collective-permute-start.8 = (bf16[2,64,768]{2,1,0:T(8,128)(2,1)S(1)}, bf16[2,64,768]{2,1,0:T(8,128)(2,1)S(1)}, u32[]{:S(2)}, u32[]{:S(2)}) collective-permute-start(bf16[2,64,768]{2,1,0:T(8,128)(2,1)S(1)} %pad_maximum_fusion.1), channel_id=1, source_target_pairs={{0,6},{2,8},{4,10},{6,12},{8,14},{10,16},{12,18},{14,20},{16,22},{... | collective-permute-start | bytes 589832 | tf_op jit(solution)/shard_map/ppermute | solution.py:17
  125.0 5.4 %collective-permute-done.11 = bf16[2,64,768]{2,1,0:T(8,128)(2,1)S(1)} collective-permute-done((bf16[2,64,768]{2,1,0:T(8,128)(2,1)S(1)}, bf16[2,64,768]{2,1,0:T(8,128)(2,1)S(1)}, u32[]{:S(2)}, u32[]{:S(2)}) %collective-permute-start.11) | collective-permute-done | bytes 196640 | tf_op jit(solution)/shard_map/ppermute | solution.py:17
  130.4 5.0 %collective-permute-done.12 = bf16[2,64,768]{2,1,0:T(8,128)(2,1)S(1)} collective-permute-done((bf16[2,64,768]{2,1,0:T(8,128)(2,1)S(1)}, bf16[2,64,768]{2,1,0:T(8,128)(2,1)S(1)}, u32[]{:S(2)}, u32[]{:S(2)}) %collective-permute-start.12) | collective-permute-done | bytes 196640 | tf_op jit(solution)/shard_map/ppermute | solution.py:17
  139.6 3.4 %reshape_squeeze.33 = bf16[7,64,12,64]{3,2,1,0:T(8,128)(2,1)} reshape(bf16[7,1,64,768]{3,2,1,0:T(8,128)(2,1)} %get-tuple-element.9) | data formatting | bytes 1376256 | tf_op jit(solution)/shard_map/reshape;squeeze | solution.py:101
  147.9 9.3 %reduce-scatter.6.cloned.1.call-done = bf16[32,64]{1,0:T(8,128)(2,1)} async-done(((bf16[64,64]{1,0:T(8,128)(2,1)}), bf16[32,64]{1,0:T(8,128)(2,1)}) %reduce-scatter.6.cloned.1.call-update) | async-done | bytes 4112 | tf_op jit(solution)/shard_map/reduce_scatter | solution.py:116
  159.0 3.6 %collective-permute-start.14 = (f32[1,32,64]{2,1,0:T(8,128)S(1)}, f32[1,32,64]{2,1,0:T(8,128)S(1)}, u32[]{:S(2)}, u32[]{:S(2)}) collective-permute-start(f32[1,32,64]{2,1,0:T(8,128)S(1)} %get-tuple-element.28), channel_id=1, source_target_pairs={{0,2},{2,4},{4,6},{6,8},{8,10},{10,12},{12,14},{14,16},{16,18},{18... | collective-permute-start | bytes 24584 | tf_op jit(solution)/shard_map/ppermute | solution.py:17
  167.5 9.4 %convolution_bitcast_fusion = f32[3,64,768]{2,1,0:T(8,128)S(1)} fusion(bf16[3,768,3072]{2,1,0:T(8,128)(2,1)} %param.16, bf16[64,3072]{1,0:T(8,128)(2,1)S(1)} %all_gather.23), kind=kOutput, calls=%fused_computation.27 | convolution fusion | flops 905969664 | bytes 15138816 | tf_op jit(solution)/shard_map/td,ihd->ith/dot_general | solution.py:83
  177.7 5.1 %collective-permute-start.15 = (bf16[2,64,768]{2,1,0:T(8,128)(2,1)S(1)}, bf16[2,64,768]{2,1,0:T(8,128)(2,1)S(1)}, u32[]{:S(2)}, u32[]{:S(2)}) collective-permute-start(bf16[2,64,768]{2,1,0:T(8,128)(2,1)S(1)} %pad_maximum_fusion.2), channel_id=1, source_target_pairs={{0,6},{2,8},{4,10},{6,12},{8,14},{10,16},{12,18},{14,20},{16,22},{... | collective-permute-start | bytes 589832 | tf_op jit(solution)/shard_map/ppermute | solution.py:17
  186.2 3.4 %collective-permute-start.17 = (bf16[2,64,768]{2,1,0:T(8,128)(2,1)S(1)}, bf16[2,64,768]{2,1,0:T(8,128)(2,1)S(1)}, u32[]{:S(2)}, u32[]{:S(2)}) collective-permute-start(bf16[2,64,768]{2,1,0:T(8,128)(2,1)S(1)} %pad_maximum_fusion.2), channel_id=1, source_target_pairs={{0,2},{2,4},{4,6},{6,8},{8,10},{10,12},{12,14},{14,16},{16,18},{18... | collective-permute-start | bytes 589832 | tf_op jit(solution)/shard_map/ppermute | solution.py:17
  194.2 5.4 %collective-permute-done.18 = bf16[2,64,768]{2,1,0:T(8,128)(2,1)S(1)} collective-permute-done((bf16[2,64,768]{2,1,0:T(8,128)(2,1)S(1)}, bf16[2,64,768]{2,1,0:T(8,128)(2,1)S(1)}, u32[]{:S(2)}, u32[]{:S(2)}) %collective-permute-start.18) | collective-permute-done | bytes 196640 | tf_op jit(solution)/shard_map/ppermute | solution.py:17
  199.7 5.0 %collective-permute-done.19 = bf16[2,64,768]{2,1,0:T(8,128)(2,1)S(1)} collective-permute-done((bf16[2,64,768]{2,1,0:T(8,128)(2,1)S(1)}, bf16[2,64,768]{2,1,0:T(8,128)(2,1)S(1)}, u32[]{:S(2)}, u32[]{:S(2)}) %collective-permute-start.19) | collective-permute-done | bytes 196640 | tf_op jit(solution)/shard_map/ppermute | solution.py:17
  208.8 3.4 %reshape_squeeze.36 = bf16[7,64,12,64]{3,2,1,0:T(8,128)(2,1)} reshape(bf16[7,1,64,768]{3,2,1,0:T(8,128)(2,1)} %get-tuple-element.7) | data formatting | bytes 1376256 | tf_op jit(solution)/shard_map/reshape;squeeze | solution.py:101
  217.1 9.3 %reduce-scatter.8.cloned.1.call-done = bf16[32,64]{1,0:T(8,128)(2,1)} async-done(((bf16[64,64]{1,0:T(8,128)(2,1)}), bf16[32,64]{1,0:T(8,128)(2,1)}) %reduce-scatter.8.cloned.1.call-update) | async-done | bytes 4112 | tf_op jit(solution)/shard_map/reduce_scatter | solution.py:116
  (207 shorter events, 82.8 us)
Async XLA Ops:
  7.2 81.0 %reduce-scatter.4.cloned.1.call-start = ((), (), s32[]{:S(2)}) async-start(), calls=%async_computation.3 | async-start | bytes 24576 | tf_op jit(solution)/shard_map/reduce_scatter | solution.py:116
  7.2 18.7 %collective-permute-start = (f32[1,32,64]{2,1,0:T(8,128)}, f32[1,32,64]{2,1,0:T(8,128)S(1)}, u32[]{:S(2)}, u32[]{:S(2)}) collective-permute-start(f32[1,32,64]{2,1,0:T(8,128)} %param.10), channel_id=1, source_target_pairs={{0,2},{2,4},{4,6},{6,8},{8,10},{10,12},{12,14},{14,16},{16,18},{18... | collective-permute-start | bytes 24584 | tf_op jit(solution)/shard_map/ppermute | solution.py:17
  40.1 13.5 %collective-permute-start.1 = (bf16[2,64,768]{2,1,0:T(8,128)(2,1)S(1)}, bf16[2,64,768]{2,1,0:T(8,128)(2,1)S(1)}, u32[]{:S(2)}, u32[]{:S(2)}) collective-permute-start(bf16[2,64,768]{2,1,0:T(8,128)(2,1)S(1)} %pad_maximum_fusion), channel_id=1, source_target_pairs={{0,6},{2,8},{4,10},{6,12},{8,14},{10,16},{12,18},{14,20},{16,22},{... | collective-permute-start | bytes 589832 | tf_op jit(solution)/shard_map/ppermute | solution.py:17
  44.5 10.5 %collective-permute-start.2 = (bf16[2,64,768]{2,1,0:T(8,128)(2,1)S(1)}, bf16[2,64,768]{2,1,0:T(8,128)(2,1)S(1)}, u32[]{:S(2)}, u32[]{:S(2)}) collective-permute-start(bf16[2,64,768]{2,1,0:T(8,128)(2,1)S(1)} %pad_maximum_fusion), channel_id=1, source_target_pairs={{0,4},{2,6},{4,8},{6,10},{8,12},{10,14},{12,16},{14,18},{16,20},{1... | collective-permute-start | bytes 589832 | tf_op jit(solution)/shard_map/ppermute | solution.py:17
  47.9 7.1 %collective-permute-start.3 = (bf16[2,64,768]{2,1,0:T(8,128)(2,1)S(1)}, bf16[2,64,768]{2,1,0:T(8,128)(2,1)S(1)}, u32[]{:S(2)}, u32[]{:S(2)}) collective-permute-start(bf16[2,64,768]{2,1,0:T(8,128)(2,1)S(1)} %pad_maximum_fusion), channel_id=1, source_target_pairs={{0,2},{2,4},{4,6},{6,8},{8,10},{10,12},{12,14},{14,16},{16,18},{18... | collective-permute-start | bytes 589832 | tf_op jit(solution)/shard_map/ppermute | solution.py:17
  50.4 11.1 %collective-permute-start.4 = (bf16[2,64,768]{2,1,0:T(8,128)(2,1)S(1)}, bf16[2,64,768]{2,1,0:T(8,128)(2,1)S(1)}, u32[]{:S(2)}, u32[]{:S(2)}) collective-permute-start(bf16[2,64,768]{2,1,0:T(8,128)(2,1)S(1)} %pad_maximum_fusion), channel_id=1, source_target_pairs={{2,0},{4,2},{6,4},{8,6},{10,8},{12,10},{14,12},{16,14},{18,16},{20... | collective-permute-start | bytes 589832 | tf_op jit(solution)/shard_map/ppermute | solution.py:17
  51.7 14.8 %collective-permute-start.5 = (bf16[2,64,768]{2,1,0:T(8,128)(2,1)S(1)}, bf16[2,64,768]{2,1,0:T(8,128)(2,1)S(1)}, u32[]{:S(2)}, u32[]{:S(2)}) collective-permute-start(bf16[2,64,768]{2,1,0:T(8,128)(2,1)S(1)} %pad_maximum_fusion), channel_id=1, source_target_pairs={{4,0},{6,2},{8,4},{10,6},{12,8},{14,10},{16,12},{18,14},{20,16},{2... | collective-permute-start | bytes 589832 | tf_op jit(solution)/shard_map/ppermute | solution.py:17
  53.6 13.0 %collective-permute-start.6 = (bf16[2,64,768]{2,1,0:T(8,128)(2,1)S(1)}, bf16[2,64,768]{2,1,0:T(8,128)(2,1)S(1)}, u32[]{:S(2)}, u32[]{:S(2)}) collective-permute-start(bf16[2,64,768]{2,1,0:T(8,128)(2,1)S(1)} %pad_maximum_fusion), channel_id=1, source_target_pairs={{6,0},{8,2},{10,4},{12,6},{14,8},{16,10},{18,12},{20,14},{22,16},{... | collective-permute-start | bytes 589832 | tf_op jit(solution)/shard_map/ppermute | solution.py:17
  79.1 78.1 %reduce-scatter.6.cloned.1.call-start = ((), (), s32[]{:S(2)}) async-start(), calls=%async_computation.4 | async-start | bytes 24576 | tf_op jit(solution)/shard_map/reduce_scatter | solution.py:116
  89.9 5.0 %collective-permute-start.7 = (f32[1,32,64]{2,1,0:T(8,128)S(1)}, f32[1,32,64]{2,1,0:T(8,128)S(1)}, u32[]{:S(2)}, u32[]{:S(2)}) collective-permute-start(f32[1,32,64]{2,1,0:T(8,128)S(1)} %get-tuple-element.24), channel_id=1, source_target_pairs={{0,2},{2,4},{4,6},{6,8},{8,10},{10,12},{12,14},{14,16},{16,18},{18... | collective-permute-start | bytes 24584 | tf_op jit(solution)/shard_map/ppermute | solution.py:17
  108.5 15.1 %collective-permute-start.8 = (bf16[2,64,768]{2,1,0:T(8,128)(2,1)S(1)}, bf16[2,64,768]{2,1,0:T(8,128)(2,1)S(1)}, u32[]{:S(2)}, u32[]{:S(2)}) collective-permute-start(bf16[2,64,768]{2,1,0:T(8,128)(2,1)S(1)} %pad_maximum_fusion.1), channel_id=1, source_target_pairs={{0,6},{2,8},{4,10},{6,12},{8,14},{10,16},{12,18},{14,20},{16,22},{... | collective-permute-start | bytes 589832 | tf_op jit(solution)/shard_map/ppermute | solution.py:17
  113.6 11.3 %collective-permute-start.9 = (bf16[2,64,768]{2,1,0:T(8,128)(2,1)S(1)}, bf16[2,64,768]{2,1,0:T(8,128)(2,1)S(1)}, u32[]{:S(2)}, u32[]{:S(2)}) collective-permute-start(bf16[2,64,768]{2,1,0:T(8,128)(2,1)S(1)} %pad_maximum_fusion.1), channel_id=1, source_target_pairs={{0,4},{2,6},{4,8},{6,10},{8,12},{10,14},{12,16},{14,18},{16,20},{1... | collective-permute-start | bytes 589832 | tf_op jit(solution)/shard_map/ppermute | solution.py:17
  117.0 7.9 %collective-permute-start.10 = (bf16[2,64,768]{2,1,0:T(8,128)(2,1)S(1)}, bf16[2,64,768]{2,1,0:T(8,128)(2,1)S(1)}, u32[]{:S(2)}, u32[]{:S(2)}) collective-permute-start(bf16[2,64,768]{2,1,0:T(8,128)(2,1)S(1)} %pad_maximum_fusion.1), channel_id=1, source_target_pairs={{0,2},{2,4},{4,6},{6,8},{8,10},{10,12},{12,14},{14,16},{16,18},{18... | collective-permute-start | bytes 589832 | tf_op jit(solution)/shard_map/ppermute | solution.py:17
  120.4 10.0 %collective-permute-start.11 = (bf16[2,64,768]{2,1,0:T(8,128)(2,1)S(1)}, bf16[2,64,768]{2,1,0:T(8,128)(2,1)S(1)}, u32[]{:S(2)}, u32[]{:S(2)}) collective-permute-start(bf16[2,64,768]{2,1,0:T(8,128)(2,1)S(1)} %pad_maximum_fusion.1), channel_id=1, source_target_pairs={{2,0},{4,2},{6,4},{8,6},{10,8},{12,10},{14,12},{16,14},{18,16},{20... | collective-permute-start | bytes 589832 | tf_op jit(solution)/shard_map/ppermute | solution.py:17
  121.7 13.7 %collective-permute-start.12 = (bf16[2,64,768]{2,1,0:T(8,128)(2,1)S(1)}, bf16[2,64,768]{2,1,0:T(8,128)(2,1)S(1)}, u32[]{:S(2)}, u32[]{:S(2)}) collective-permute-start(bf16[2,64,768]{2,1,0:T(8,128)(2,1)S(1)} %pad_maximum_fusion.1), channel_id=1, source_target_pairs={{4,0},{6,2},{8,4},{10,6},{12,8},{14,10},{16,12},{18,14},{20,16},{2... | collective-permute-start | bytes 589832 | tf_op jit(solution)/shard_map/ppermute | solution.py:17
  123.5 11.9 %collective-permute-start.13 = (bf16[2,64,768]{2,1,0:T(8,128)(2,1)S(1)}, bf16[2,64,768]{2,1,0:T(8,128)(2,1)S(1)}, u32[]{:S(2)}, u32[]{:S(2)}) collective-permute-start(bf16[2,64,768]{2,1,0:T(8,128)(2,1)S(1)} %pad_maximum_fusion.1), channel_id=1, source_target_pairs={{6,0},{8,2},{10,4},{12,6},{14,8},{16,10},{18,12},{20,14},{22,16},{... | collective-permute-start | bytes 589832 | tf_op jit(solution)/shard_map/ppermute | solution.py:17
  147.9 78.5 %reduce-scatter.8.cloned.1.call-start = ((), (), s32[]{:S(2)}) async-start(), calls=%async_computation.5 | async-start | bytes 24576 | tf_op jit(solution)/shard_map/reduce_scatter | solution.py:116
  159.0 5.0 %collective-permute-start.14 = (f32[1,32,64]{2,1,0:T(8,128)S(1)}, f32[1,32,64]{2,1,0:T(8,128)S(1)}, u32[]{:S(2)}, u32[]{:S(2)}) collective-permute-start(f32[1,32,64]{2,1,0:T(8,128)S(1)} %get-tuple-element.28), channel_id=1, source_target_pairs={{0,2},{2,4},{4,6},{6,8},{8,10},{10,12},{12,14},{14,16},{16,18},{18... | collective-permute-start | bytes 24584 | tf_op jit(solution)/shard_map/ppermute | solution.py:17
  177.7 15.1 %collective-permute-start.15 = (bf16[2,64,768]{2,1,0:T(8,128)(2,1)S(1)}, bf16[2,64,768]{2,1,0:T(8,128)(2,1)S(1)}, u32[]{:S(2)}, u32[]{:S(2)}) collective-permute-start(bf16[2,64,768]{2,1,0:T(8,128)(2,1)S(1)} %pad_maximum_fusion.2), channel_id=1, source_target_pairs={{0,6},{2,8},{4,10},{6,12},{8,14},{10,16},{12,18},{14,20},{16,22},{... | collective-permute-start | bytes 589832 | tf_op jit(solution)/shard_map/ppermute | solution.py:17
  182.8 11.3 %collective-permute-start.16 = (bf16[2,64,768]{2,1,0:T(8,128)(2,1)S(1)}, bf16[2,64,768]{2,1,0:T(8,128)(2,1)S(1)}, u32[]{:S(2)}, u32[]{:S(2)}) collective-permute-start(bf16[2,64,768]{2,1,0:T(8,128)(2,1)S(1)} %pad_maximum_fusion.2), channel_id=1, source_target_pairs={{0,4},{2,6},{4,8},{6,10},{8,12},{10,14},{12,16},{14,18},{16,20},{1... | collective-permute-start | bytes 589832 | tf_op jit(solution)/shard_map/ppermute | solution.py:17
  186.2 8.0 %collective-permute-start.17 = (bf16[2,64,768]{2,1,0:T(8,128)(2,1)S(1)}, bf16[2,64,768]{2,1,0:T(8,128)(2,1)S(1)}, u32[]{:S(2)}, u32[]{:S(2)}) collective-permute-start(bf16[2,64,768]{2,1,0:T(8,128)(2,1)S(1)} %pad_maximum_fusion.2), channel_id=1, source_target_pairs={{0,2},{2,4},{4,6},{6,8},{8,10},{10,12},{12,14},{14,16},{16,18},{18... | collective-permute-start | bytes 589832 | tf_op jit(solution)/shard_map/ppermute | solution.py:17
  189.6 10.0 %collective-permute-start.18 = (bf16[2,64,768]{2,1,0:T(8,128)(2,1)S(1)}, bf16[2,64,768]{2,1,0:T(8,128)(2,1)S(1)}, u32[]{:S(2)}, u32[]{:S(2)}) collective-permute-start(bf16[2,64,768]{2,1,0:T(8,128)(2,1)S(1)} %pad_maximum_fusion.2), channel_id=1, source_target_pairs={{2,0},{4,2},{6,4},{8,6},{10,8},{12,10},{14,12},{16,14},{18,16},{20... | collective-permute-start | bytes 589832 | tf_op jit(solution)/shard_map/ppermute | solution.py:17
  190.9 13.7 %collective-permute-start.19 = (bf16[2,64,768]{2,1,0:T(8,128)(2,1)S(1)}, bf16[2,64,768]{2,1,0:T(8,128)(2,1)S(1)}, u32[]{:S(2)}, u32[]{:S(2)}) collective-permute-start(bf16[2,64,768]{2,1,0:T(8,128)(2,1)S(1)} %pad_maximum_fusion.2), channel_id=1, source_target_pairs={{4,0},{6,2},{8,4},{10,6},{12,8},{14,10},{16,12},{18,14},{20,16},{2... | collective-permute-start | bytes 589832 | tf_op jit(solution)/shard_map/ppermute | solution.py:17
  192.8 11.8 %collective-permute-start.20 = (bf16[2,64,768]{2,1,0:T(8,128)(2,1)S(1)}, bf16[2,64,768]{2,1,0:T(8,128)(2,1)S(1)}, u32[]{:S(2)}, u32[]{:S(2)}) collective-permute-start(bf16[2,64,768]{2,1,0:T(8,128)(2,1)S(1)} %pad_maximum_fusion.2), channel_id=1, source_target_pairs={{6,0},{8,2},{10,4},{12,6},{14,8},{16,10},{18,12},{20,14},{22,16},{... | collective-permute-start | bytes 589832 | tf_op jit(solution)/shard_map/ppermute | solution.py:17
  (30 other events, 239.8 us)
Sparse Core Ops, SparseCore 0:
  79.2 8.8 reduce-scatter.3
  148.0 9.1 reduce-scatter.5
  217.2 9.1 reduce-scatter.7
where the time goes:
time: 237 us; the launch traced here: 235 us
  waiting for transfers between devices  62.7 us (26%)
  starting transfers between devices  58.1 us (25%)
  matrix products  51 us (22%)
  local copies, waits for them, and re-layouts  22.7 us (10%)
  between operations  16.9 us (7%)
  blocking collectives  14.8 us (6%)
  other arithmetic  9.25 us (4%)
    ppermute x21, starting transfers between devices, shifted(): lax.ppermute(value, axis, [(source, source + steps) for source in range(i...  57.9 us
    ppermute x21, waiting for transfers between devices, shifted(): lax.ppermute(value, axis, [(source, source + steps) for source in range(i...  35 us
    dot_general x3, matrix products, body(): jnp.einsum('td,ihd->ith', lax.all_gather(normalize(own_hidden), 'tok', ax...  28.2 us
    reduce_scatter x3, waiting for transfers between devices, body(): lax.psum_scatter(result.astype(jnp.bfloat16), 'tok', scatter_dimension=0,...  27.6 us
    another operation x3, local copies, waits for them, and re-layouts, body(): value_all = stacked[:, 1].reshape(window_len, frame_rows, head_count, HD)  10.2 us
    dot_general x3, matrix products, body(): jnp.einsum('hqjk,jkhc->qhc', weights, value_all, preferred_element_type=j...  8.17 us
    all_gather x3, blocking collectives, body(): lax.all_gather(normalize(own_hidden), 'tok', axis=0, tiled=True)  6.48 us
    dot_general x3, matrix products, body(): jnp.dot(own_hidden, vel_f, precision=lax.Precision.HIGHEST)  5.29 us
  transfers between devices with their start and end apart: 24, of which 11 were waited for; matrix products, arithmetic and copies ran while one was open for 2% of the time, Pallas kernels for 0%

commit v1 on v0

v1 whole, which is shorter than its diff:
```python
import functools
import math

import jax
import jax.numpy as jnp
from jax import lax
from jax.experimental import pallas as pl
from jax.experimental.pallas import tpu as pltpu
from jax.sharding import PartitionSpec as P

HD = 64
STEPS = 3
HALO = 3
LANES = 128
EPS = 1e-06
F32, BF16 = jnp.float32, jnp.bfloat16


def round_up(value, unit):
    return -(-value // unit) * unit


def dot(a, b):
    return jnp.dot(a, b, preferred_element_type=F32)


def dot_nt(a, b):
    return lax.dot_general(a, b, (((1,), (1,)), ((), ())), preferred_element_type=F32)


def halves(value, axis):
    high = value.astype(BF16)
    low = (value - high.astype(F32)).astype(BF16)
    return jnp.concatenate([high, low], axis=axis)


def weights_kernel(rows, base, g_ref, qkv_hbm, out_hbm, mq_ref, mk_ref, mv_ref, wo_ref, gram_ref, buf, sems):
    width = out_hbm.shape[0]
    per = width // rows
    parts, _, depth = g_ref.shape
    copies = []
    for chunk in range(4 * per):
        source = qkv_hbm.at[chunk // per] if chunk < 3 * per else out_hbm
        copy = pltpu.make_async_copy(
            source.at[pl.ds((chunk % per) * rows, rows)], buf.at[chunk], sems.at[chunk]
        )
        copy.start()
        copies.append(copy)
    gram = sum(dot_nt(g_ref[t], g_ref[t, :base]) for t in range(parts))
    gram_ref[...] = halves(gram, 1)
    for chunk in range(4 * per):
        copies[chunk].wait()
        where = pl.ds((chunk % per) * rows, rows)
        blocks = [buf[chunk, :, t * depth : (t + 1) * depth] for t in range(parts)]
        kind = chunk // per
        if kind in (0, 2):
            target = mq_ref if kind == 0 else mv_ref
            target[where, :] = halves(sum(dot_nt(blocks[t], g_ref[t, :base]) for t in range(parts)), 1)
        elif kind == 1:
            mk_ref[:, where] = halves(sum(dot_nt(g_ref[t, :base], blocks[t]) for t in range(parts)), 0)
        else:
            wo_ref[:, where] = halves(sum(dot_nt(g_ref[t, base:], blocks[t]) for t in range(parts)), 0)


def advance(level_count, tok, first, g_ref, hpart_ref, xq_ref):
    shared = g_ref[0]
    for t in range(1, g_ref.shape[0]):
        shared = shared + g_ref[t]
    velocity = shared + hpart_ref[...]
    moved = xq_ref[...] - velocity * (1.0 / level_count)
    if first is None:
        return velocity, moved
    lane_frame = lax.broadcasted_iota(jnp.int32, (1, shared.shape[1]), 1) // tok
    return velocity, jnp.where(lane_frame + first == -1, shared, moved)


def own_rows(block, tok, part_rows, index, scratch):
    scratch[...] = block.T
    return scratch[pl.ds(pl.multiple_of(index * part_rows, 8), part_rows), :]


def step_kernel(step, cfg, *refs):
    tok, frames, channels, base, depth, level_count, heads, part_rows = cfg
    query_block = max(1, LANES // tok)
    n_query = query_block + 2 * HALO * (STEPS - 1 - step)
    n_key = n_query + 2 * HALO
    key_lanes, query_lanes = n_key * tok, n_query * tok
    width = heads * HD
    window = (2 * HALO + query_block) * tok
    position, tok_index = lax.axis_index("queue"), lax.axis_index("tok")
    first_key = position - HALO - (HALO + 1) * (STEPS - 1 - step)
    refs = list(refs)
    slot_ref, reach_ref = refs[0], refs[1]
    if step == 0:
        lat_ref = refs[2]
        refs = refs[3:]
    else:
        g_ref, hprev_ref, xprev_ref = refs[2:5]
        refs = refs[5:]
    fresh_ref = None
    if step < STEPS - 1:
        fresh_ref = refs.pop(0)
    gain_ref, mq_ref, mk_ref, mv_ref, wo_ref, gram_ref = refs[:6]
    refs = refs[6:]
    part_ref, hpart_ref, xq_ref = refs[:3]
    refs = refs[3:]
    own_ref = None
    if step > 0:
        own_ref = refs.pop(0)
    kbuf, vbuf, qbuf, att, tbuf = refs

    if step == 0:
        pieces = []
        for w in range(n_key):
            source = lax.rem(first_key - 1 + w + 2 * frames, frames)
            pieces.append(lat_ref[pl.ds(pl.multiple_of(source * tok, 8), tok), :])
        state = jnp.concatenate(pieces, axis=0).T
    else:
        velocity, state = advance(level_count, tok, first_key - 1, g_ref, hprev_ref, xprev_ref)
        mine = (HALO + 1) * (STEPS - step)
        own_ref[...] = own_rows(velocity[:, mine * tok : (mine + 1) * tok], tok, part_rows, tok_index, tbuf)

    key_frame = lax.broadcasted_iota(jnp.int32, (1, key_lanes), 1) // tok
    level_row = jnp.full((1, key_lanes), -1, jnp.int32)
    for w in range(n_key):
        frame = first_key + w
        known = slot_ref[jnp.clip(frame - step - 1, 0, frames - 1)] + step
        level_row = jnp.where(key_frame == w, jnp.where(frame >= step + 1, known, frame), level_row)
    row = lax.broadcasted_iota(jnp.int32, (base - channels, key_lanes), 0)
    aug_t = jnp.concatenate([state, jnp.where(row == level_row, 1.0, 0.0)], axis=0)
    aug_t = aug_t.astype(BF16).astype(F32)
    aug = aug_t.T
    aug_b, aug_tb = aug.astype(BF16), aug_t.astype(BF16)
    aug_q = aug_t[:, HALO * tok : HALO * tok + query_lanes]
    aug_qb = aug_q.astype(BF16)
    both = jnp.concatenate([aug_b, aug_b], axis=1)
    both_t = jnp.concatenate([aug_tb, aug_tb], axis=0)
    both_q = jnp.concatenate([aug_qb, aug_qb], axis=0)
    gram = gram_ref[:base, :]
    mean_t = jnp.sum(dot(gram, both_t) * aug_t, axis=0, keepdims=True) * (1.0 / depth)
    mean_q = jnp.sum(dot(gram, both_q) * aug_q, axis=0, keepdims=True) * (1.0 / depth)
    mean_c = jnp.sum(dot_nt(both, gram) * aug, axis=1, keepdims=True) * (1.0 / depth)
    mean_t, mean_q, mean_c = (jnp.maximum(m, 0.0) + EPS for m in (mean_t, mean_q, mean_c))

    hpart_ref[...] = dot(gram_ref[base:, :], both_q)
    xq_ref[...] = state[:, HALO * tok : HALO * tok + query_lanes]

    gain = gain_ref[0:1, :] * gain_ref[1:2, :] * (HD ** -0.5 * math.log2(math.e))
    span = 256 if width % 256 == 0 else 128
    head_of = lambda axis: lax.broadcasted_iota(jnp.int32, (span, span), axis) // HD
    average = jnp.where(head_of(0) == head_of(1), 1.0 / HD, 0.0).astype(BF16)
    for at in range(0, width, span):
        raw = dot(both, mk_ref[:, at : at + span])
        spread = dot((raw * raw).astype(BF16), average)
        kbuf[:, at : at + span] = (raw * lax.rsqrt(spread + EPS * mean_c) * gain[:, at : at + span]).astype(BF16)
    vbuf[...] = (dot(mv_ref[...], both_t) * lax.rsqrt(mean_t)).astype(BF16)
    raw = dot(mq_ref[...], both_q).reshape(heads, HD, query_lanes)
    spread = jnp.sum(raw * raw, axis=1, keepdims=True) * (1.0 / HD)
    qbuf[...] = (raw * lax.rsqrt(spread + EPS * mean_q)[:, :, :]).reshape(width, query_lanes).astype(BF16)

    def block(b, carry):
        lead = (b * LANES) // tok
        keys = pl.ds(pl.multiple_of(lead * tok, LANES), window)
        lanes = pl.ds(pl.multiple_of(b * LANES, LANES), LANES)
        lane = lax.broadcasted_iota(jnp.int32, (1, 2 * LANES), 1)
        within = lax.rem(lane, LANES) // tok
        bias_rows = []
        reach = []
        for j in range(query_block):
            frame = first_key + HALO + lead + j
            reach.append(reach_ref[jnp.clip(frame, 0, frames - 1)])
        for k in range(2 * HALO + query_block):
            target = first_key + lead + k
            inside = (target >= 0) & (target < frames)
            bias = jnp.zeros((1, 2 * LANES), F32)
            for j in range(query_block):
                counted = inside & (abs(k - HALO - j) <= reach[j])
                value = jnp.where(counted, 0.0, -1e30)
                bias = jnp.where(within == j, value, bias) if query_block > 1 else bias + value
            bias_rows.append(bias)
        ones = jnp.ones((16, window), BF16)
        upper = lax.broadcasted_iota(jnp.int32, (2 * HD, LANES), 0) < HD
        for pair in range(heads // 2):
            cols = slice(pair * 2 * HD, (pair + 1) * 2 * HD)
            query = qbuf[cols, lanes]
            zero = jnp.zeros_like(query)
            query = jnp.concatenate([jnp.where(upper, query, zero), jnp.where(upper, zero, query)], axis=1)
            score = dot(kbuf[keys, cols], query)
            score = jnp.concatenate(
                [score[k * tok : (k + 1) * tok] + bias_rows[k] for k in range(len(bias_rows))], axis=0
            )
            weight = jnp.exp2(score - jnp.max(score, axis=0, keepdims=True)).astype(BF16)
            mixed = dot(jnp.concatenate([vbuf[cols, keys], ones], axis=0), weight)
            total = 1.0 / mixed[2 * HD : 2 * HD + 1, :]
            top = mixed[:HD, :LANES] * total[:, :LANES]
            bottom = mixed[HD : 2 * HD, LANES:] * total[:, LANES:]
            att[cols, lanes] = jnp.concatenate([top, bottom], axis=0).astype(BF16)
        return carry

    blocks = query_lanes // LANES
    if blocks == 1:
        block(0, 0)
    else:
        lax.fori_loop(0, blocks, block, 0)
    mixed = dot(wo_ref[...], att[...])
    partial = mixed[:channels] + mixed[channels:]
    if step < STEPS - 1:
        tbuf[...] = jnp.zeros_like(tbuf)
        tbuf[pl.ds(pl.multiple_of(tok_index * part_rows, 8), part_rows), :] = fresh_ref[step + 1]
        fresh_t = tbuf[...].T
        fresh_t = jnp.concatenate([fresh_t] * n_query, axis=1)
        slot = lax.broadcasted_iota(jnp.int32, (1, query_lanes), 1) // tok + first_key + HALO
        partial = jnp.where(slot == -1, fresh_t, partial)
    part_ref[...] = partial[:, : part_ref.shape[1]]


def last_kernel(cfg, *refs):
    tok, frames, channels, base, depth, level_count, heads, part_rows = cfg
    g_ref, hpart_ref, xq_ref = refs[:3]
    own = refs[3 : 3 + STEPS - 1]
    velocity_ref, queue_ref, tbuf = refs[3 + STEPS - 1 :]
    tok_index = lax.axis_index("tok")
    velocity, moved = advance(level_count, tok, None, g_ref, hpart_ref, xq_ref)
    for s in range(STEPS - 1):
        velocity_ref[s, 0] = own[s][...]
    velocity_ref[STEPS - 1, 0] = own_rows(velocity[:, :tok], tok, part_rows, tok_index, tbuf)
    queue_ref[0] = own_rows(moved[:, :tok], tok, part_rows, tok_index, tbuf)


def body(
    latent,
    fresh_noise,
    frame_slot,
    frame_reach,
    level_embed,
    embed_weight,
    qkv_weight,
    qk_gain,
    out_weight,
    vel_weight,
):
    frames, parts = lax.axis_size("queue"), lax.axis_size("tok")
    position = lax.axis_index("queue")
    part_rows, channels = latent.shape[1], latent.shape[2]
    tok = part_rows * parts
    level_count = level_embed.shape[0]
    depth = qkv_weight.shape[2]
    width = qkv_weight.shape[1]
    spare = round_up(width, 2 * LANES) - width
    if spare:
        qkv_weight = jnp.pad(qkv_weight, ((0, 0), (0, spare), (0, 0)))
        qk_gain = jnp.pad(qk_gain, ((0, 0), (0, spare)))
        out_weight = jnp.pad(out_weight, ((0, spare), (0, 0)))
        width += spare
    heads = width // HD
    base = round_up(channels + level_count, LANES)
    cfg = (tok, frames, channels, base, depth, level_count, heads, part_rows)
    vmem, smem, anywhere = (
        pl.BlockSpec(memory_space=pltpu.VMEM),
        pl.BlockSpec(memory_space=pltpu.SMEM),
        pl.BlockSpec(memory_space=pl.ANY),
    )
    shape = jax.ShapeDtypeStruct

    sent = jnp.where(position == frames - 1, fresh_noise[0], latent[0])
    latents = lax.all_gather(sent, ("queue", "tok"), axis=0, tiled=True)

    filler = jnp.zeros((base - channels - level_count, embed_weight.shape[1]), BF16)
    table = jnp.concatenate([embed_weight, level_embed, filler, vel_weight.T], axis=0)
    table = lax.all_gather(table, "tok", axis=0, tiled=False)

    rows = 256
    chunks = 4 * width // rows
    mq, mk, mv, wo, gram = pl.pallas_call(
        functools.partial(weights_kernel, rows, base),
        out_shape=(
            shape((width, 2 * base), BF16),
            shape((2 * base, width), BF16),
            shape((width, 2 * base), BF16),
            shape((2 * channels, width), BF16),
            shape((base + channels, 2 * base), BF16),
        ),
        in_specs=[vmem, anywhere, anywhere],
        out_specs=(vmem,) * 5,
        scratch_shapes=[
            pltpu.VMEM((chunks, rows, depth), BF16),
            pltpu.SemaphoreType.DMA((chunks,)),
        ],
        compiler_params=pltpu.CompilerParams(vmem_limit_bytes=40 * 2**20),
        cost_estimate=pl.CostEstimate(
            flops=2 * base * 4 * width * depth, bytes_accessed=8 * width * depth, transcendentals=0
        ),
        name="weights",
    )(table, qkv_weight, out_weight)

    query_block = max(1, LANES // tok)
    owned = []
    for step in range(STEPS):
        n_query = query_block + 2 * HALO * (STEPS - 1 - step)
        query_lanes, key_lanes = n_query * tok, (n_query + 2 * HALO) * tok
        args = [frame_slot, frame_reach]
        specs = [smem, smem]
        if step == 0:
            args += [latents]
            specs += [vmem]
        else:
            args += [gathered, hpart, xq]
            specs += [vmem] * 3
        if step < STEPS - 1:
            args += [fresh_noise]
            specs += [vmem]
        args += [qk_gain, mq, mk, mv, wo, gram]
        specs += [vmem] * 6
        outs = [shape((channels, query_lanes), F32)] * 3
        if step > 0:
            outs += [shape((part_rows, channels), F32)]
        window = (2 * HALO + query_block) * tok
        result = pl.pallas_call(
            functools.partial(step_kernel, step, cfg),
            out_shape=tuple(outs),
            in_specs=specs,
            out_specs=(vmem,) * len(outs),
            scratch_shapes=[
                pltpu.VMEM((key_lanes, width), BF16),
                pltpu.VMEM((width, key_lanes), BF16),
                pltpu.VMEM((width, query_lanes), BF16),
                pltpu.VMEM((width, query_lanes), BF16),
                pltpu.VMEM((tok, channels), F32),
            ],
            compiler_params=pltpu.CompilerParams(vmem_limit_bytes=48 * 2**20),
            cost_estimate=pl.CostEstimate(
                flops=4 * query_lanes * window * width + 12 * key_lanes * base * width,
                bytes_accessed=8 * width * base,
                transcendentals=query_lanes * window * heads,
            ),
            name="step%d" % step,
        )(*args)
        part, hpart, xq = result[:3]
        owned += list(result[3:])
        gathered = lax.all_gather(part, "tok", axis=0, tiled=False)

    return tuple(
        pl.pallas_call(
            functools.partial(last_kernel, cfg),
            out_shape=(
                shape((STEPS, 1, part_rows, channels), F32),
                shape((1, part_rows, channels), F32),
            ),
            in_specs=[vmem] * (3 + len(owned)),
            out_specs=(vmem, vmem),
            scratch_shapes=[pltpu.VMEM((tok, channels), F32)],
            name="last",
        )(gathered, hpart, xq, *owned)
    )


def solution(mesh):
    return jax.shard_map(
        body,
        mesh=mesh,
        in_specs=(
            P("queue", "tok", None),
            P(None, "tok", None),
            P(),
            P(),
            P(None, "tok"),
            P(None, "tok"),
            P(None, "tok", None),
            P(None, "tok"),
            P("tok", None),
            P("tok", None),
        ),
        out_specs=(P(None, "queue", "tok", None), P("queue", "tok", None)),
        check_vma=False,
    )
```

time: 237 us -> 125 us (0.53)
  waiting for transfers between devices: 62.7 us -> 0.02 us
  starting transfers between devices: 58.1 us -> 0.04 us
  Pallas kernels: 0 us -> 52.4 us
  matrix products: 51 us -> 0 us
  blocking collectives: 14.8 us -> 50.9 us
  local copies, waits for them, and re-layouts: 22.7 us -> 4.91 us
  other arithmetic: 9.25 us -> 2.05 us
  between operations: 16.9 us -> 14.2 us
    ppermute x21 -> x0, starting transfers between devices: 57.9 us -> none  [shifted(): lax.ppermute(value, axis, [(source, source + steps) for source in range(i...]
    pallas_call x0 -> x5, Pallas kernels: none -> 52.4 us  [the longest x3 38 us: body(): pl.pallas_call(functools.partial(step_kernel, step, cfg), out_shape=tuple...]
    dot_general x18 -> x0, matrix products: 49.5 us -> none  [the longest x3 28.2 us: body(): jnp.einsum('td,ihd->ith', lax.all_gather(normalize(own_hidden), 'tok', ax...]
    all_gather x6 -> x4, blocking collectives: 14.8 us -> 50.9 us  [the longest x1 44.6 us: body(): latents = lax.all_gather(sent, ('queue', 'tok'), axis=0, tiled=True)]
    ppermute x21 -> x0, waiting for transfers between devices: 35 us -> none  [shifted(): lax.ppermute(value, axis, [(source, source + steps) for source in range(i...]
    reduce_scatter x3 -> x0, waiting for transfers between devices: 27.6 us -> none  [body(): lax.psum_scatter(result.astype(jnp.bfloat16), 'tok', scatter_dimension=0,...]
    another operation x15 -> x0, local copies, waits for them, and re-layouts: 15 us -> none  [the longest x3 10.2 us: body(): value_all = stacked[:, 1].reshape(window_len, frame_rows, head_count, HD)]
    reduce_sum x10 -> x0, other arithmetic: 4.76 us -> none  [the longest x3 2.1 us: body(): row_total = jnp.sum(expo, axis=(2, 3), keepdims=True)]
  transfers between devices with their start and end apart: 24 -> 1, of which waited for: 11 -> 0; matrix products, arithmetic and copies ran while one was open for 2% -> 0% of each run, Pallas kernels for 0% -> 0%
where the time goes in v1:
time: 125 us
  Pallas kernels  52.4 us (42%)
  blocking collectives  50.9 us (41%)
  between operations  14.2 us (11%)
  local copies, waits for them, and re-layouts  4.91 us (4%)
  other arithmetic  2.05 us (2%)
    all_gather x1, blocking collectives, body(): latents = lax.all_gather(sent, ('queue', 'tok'), axis=0, tiled=True)  44.6 us
    pallas_call x3, Pallas kernels, body(): pl.pallas_call(functools.partial(step_kernel, step, cfg), out_shape=tuple...  38 us
    pallas_call x1, Pallas kernels, body(): pl.pallas_call(functools.partial(weights_kernel, rows, base), out_shape=(...  12.9 us
    all_gather x3, blocking collectives, body(): gathered = lax.all_gather(part, 'tok', axis=0, tiled=False)  6.28 us
    unnamed x22, local copies, waits for them, and re-layouts  4.83 us
  transfers between devices with their start and end apart: 1, of which 0 were waited for; matrix products, arithmetic and copies ran while one was open for 0% of the time, Pallas kernels for 0%

profile of v1, /device:TPU:0, one launch (start us, length us, event | category | flops | bytes accessed | tf_op | source)
XLA Modules:
  0.0 124.5 jit_solution(7740539015870640188)
XLA Ops:
  7.2 0.0 copy-start.10
  7.2 0.0 copy-start.6
  7.2 0.0 all-gather.7.cloned.1.call-start
  7.2 0.1 pad.2.clone
  7.3 2.0 %pad_maximum_fusion = bf16[192,1536]{1,0:T(8,128)(2,1)} fusion(bf16[64,1536]{1,0:T(8,128)(2,1)} %bitcast.11, bf16[19,1536]{1,0:T(8,128)(2,1)} %param.14, bf16[64,1536]{1,0:T(8,128)(2,1)} %param.15, bf16[192]{0:T(256)(128)(2,1)S(1)} %pad.2.clone), kind=kLoop, calls=%fused_computation | loop fusion | flops 2359296 | bytes 1041792 | tf_op jit(solution)/shard_map/concatenate | solution.py:269
  9.4 0.0 all-gather.7.cloned.1.call-update
  9.4 0.0 copy-done.10
  9.4 0.0 copy-done.6
  9.4 44.6 %all-gather = f32[1,1024,64]{2,1,0:T(8,128)S(1)} all-gather(f32[1,32,64]{2,1,0:T(8,128)S(1)} %slice_select_fusion), channel_id=2, replica_groups=mesh['queue'=16,'tok'=2] {'queue','tok'}, dimensions={1}, use_global_device_ids=true | all-gather | bytes 270336 | tf_op jit(solution)/shard_map/all_gather | solution.py:266
  54.1 2.3 %copy-done = bf16[768,3072]{1,0:T(8,128)(2,1)S(1)} copy-done((bf16[768,3072]{1,0:T(8,128)(2,1)S(1)}, bf16[768,3072]{1,0:T(8,128)(2,1)}, u32[]{:S(2)}) %copy-start) | copy-done | bytes 4718616
  56.4 1.3 %copy-done.1 = bf16[384,1536]{1,0:T(8,128)(2,1)S(1)} copy-done((bf16[384,1536]{1,0:T(8,128)(2,1)S(1)}, bf16[384,1536]{1,0:T(8,128)(2,1)}, u32[]{:S(2)}) %copy-start.1) | copy-done | bytes 1179672
  57.7 12.9 %weights.1 = (bf16[768,256]{1,0:T(8,128)(2,1)S(1)}, bf16[256,768]{1,0:T(8,128)(2,1)S(1)}, bf16[768,256]{1,0:T(8,128)(2,1)S(1)}, bf16[128,768]{1,0:T(8,128)(2,1)S(1)}, bf16[192,256]{1,0:T(8,128)(2,1)S(1)}) custom-call(bf16[2,192,1536]{2,1,0:T(8,128)(2,1)S(1)} %bitcast.6, bf16[3,768,3072]{2,1,0:T(8,128)(2,1)} %qkv_hbm.1, bf16[768,3072]{1,0:T(8,128)(2,1)S(1)} %copy-done), custom_call_target="tpu_custom_call" | custom-call | flops 2415919104 | bytes 18874368 | tf_op jit(solution)/shard_map/weights/pallas_call | solution.py:274
  70.6 0.0 copy-done.7
  70.6 0.0 copy-done.8
  70.6 21.4 %step0.1 = (f32[64,896]{1,0:T(8,128)S(1)}, f32[64,896]{1,0:T(8,128)S(1)}, f32[64,896]{1,0:T(8,128)S(1)}) custom-call(s32[16]{0:T(128)S(1)} %copy-done.8, s32[16]{0:T(128)S(1)} %copy-done.9, f32[1024,64]{1,0:T(8,128)S(1)} %bitcast.7, f32[3,32,64]{2,1,0:T(8,128)S(1)} %copy-done.6, f32[2,768]{1,0:T(2,128)S(1)} %copy-done.7, ...), custom_call_target="tpu_custom_call" | custom-call | flops 2919235584 | bytes 786432 | tf_op jit(solution)/shard_map/step0/pallas_call | solution.py:318
  92.0 2.3 %all-gather.2 = f32[128,896]{1,0:T(8,128)S(1)} all-gather(f32[64,896]{1,0:T(8,128)S(1)} %get-tuple-element.23), channel_id=4, replica_groups=mesh['queue'=16,'tok'=2] {'tok'}, dimensions={0}, use_global_device_ids=true | all-gather | bytes 688128 | tf_op jit(solution)/shard_map/all_gather | solution.py:340
  94.3 12.8 %step1.1 = (f32[64,512]{1,0:T(8,128)S(1)}, f32[64,512]{1,0:T(8,128)S(1)}, f32[64,512]{1,0:T(8,128)S(1)}, f32[32,64]{1,0:T(8,128)S(1)}) custom-call(s32[16]{0:T(128)S(1)} %copy-done.8, s32[16]{0:T(128)S(1)} %copy-done.9, f32[2,64,896]{2,1,0:T(8,128)S(1)} %bitcast.8, f32[64,896]{1,0:T(8,128)S(1)} %get-tuple-element.24.refs_3_, ...), custom_call_target="tpu_custom_call" | custom-call | flops 1862270976 | bytes 786432 | tf_op jit(solution)/shard_map/step1/pallas_call | solution.py:318
  107.1 2.0 %all-gather.3 = f32[128,512]{1,0:T(8,128)S(1)} all-gather(f32[64,512]{1,0:T(8,128)S(1)} %get-tuple-element.26), channel_id=5, replica_groups=mesh['queue'=16,'tok'=2] {'tok'}, dimensions={0}, use_global_device_ids=true | all-gather | bytes 393216 | tf_op jit(solution)/shard_map/all_gather | solution.py:340
  109.1 3.8 %step2.1 = (f32[64,128]{1,0:T(8,128)S(1)}, f32[64,128]{1,0:T(8,128)S(1)}, f32[64,128]{1,0:T(8,128)S(1)}, f32[32,64]{1,0:T(8,128)S(1)}) custom-call(s32[16]{0:T(128)S(1)} %copy-done.8, s32[16]{0:T(128)S(1)} %copy-done.9, f32[2,64,512]{2,1,0:T(8,128)S(1)} %bitcast.9, f32[64,512]{1,0:T(8,128)S(1)} %get-tuple-element.27.refs_3_, ...), custom_call_target="tpu_custom_call" | custom-call | flops 805306368 | bytes 786432 | tf_op jit(solution)/shard_map/step2/pallas_call | solution.py:318
  112.9 0.6 copy-done.2
  113.5 0.6 copy-done.3
  114.1 2.0 %all-gather.4 = f32[128,128]{1,0:T(8,128)} all-gather(f32[64,128]{1,0:T(8,128)S(1)} %get-tuple-element.29), channel_id=6, replica_groups=mesh['queue'=16,'tok'=2] {'tok'}, dimensions={0}, use_global_device_ids=true | all-gather | bytes 98304 | tf_op jit(solution)/shard_map/all_gather | solution.py:340
  116.1 0.0 copy-done.5
  116.1 1.6 %last.1 = (f32[3,1,32,64]{3,2,1,0:T(8,128)}, f32[1,32,64]{2,1,0:T(8,128)}) custom-call(f32[2,64,128]{2,1,0:T(8,128)} %bitcast.10, f32[64,128]{1,0:T(8,128)} %copy-done.2, f32[64,128]{1,0:T(8,128)} %copy-done.3, f32[32,64]{1,0:T(8,128)} %copy-done.4, f32[32,64]{1,0:T(8,128)} %copy-done.5), custom_call_target="tpu_custom_call" | custom-call | tf_op jit(solution)/shard_map/last/pallas_call | solution.py:343
  (14 shorter events, 0.0 us)
Async XLA Ops:
  7.2 2.2 %copy-start.10 = (f32[1,32,64]{2,1,0:T(8,128)S(1)}, f32[1,32,64]{2,1,0:T(8,128)}, u32[]{:S(2)}) copy-start(f32[1,32,64]{2,1,0:T(8,128)} %param.10) | copy-start | bytes 24580
  7.2 2.2 %copy-start.6 = (f32[3,32,64]{2,1,0:T(8,128)S(1)}, f32[3,32,64]{2,1,0:T(8,128)}, u32[]{:S(2)}) copy-start(f32[3,32,64]{2,1,0:T(8,128)} %refs_5_.2) | copy-start | bytes 73732
  7.2 46.9 %all-gather.7.cloned.1.call-start = ((), (), s32[]{:S(2)}) async-start(), calls=%async_computation | async-start | bytes 1769472 | tf_op jit(solution)/shard_map/all_gather | solution.py:270
  54.1 2.3 %copy-start = (bf16[768,3072]{1,0:T(8,128)(2,1)S(1)}, bf16[768,3072]{1,0:T(8,128)(2,1)}, u32[]{:S(2)}) copy-start(bf16[768,3072]{1,0:T(8,128)(2,1)} %out_hbm.1) | copy-start | bytes 14155780
  56.4 1.3 %copy-start.1 = (bf16[384,1536]{1,0:T(8,128)(2,1)S(1)}, bf16[384,1536]{1,0:T(8,128)(2,1)}, u32[]{:S(2)}) copy-start(bf16[384,1536]{1,0:T(8,128)(2,1)} %all-gather.7.cloned.1.call-done) | copy-start | bytes 3538948
  57.7 12.9 %copy-start.7 = (f32[2,768]{1,0:T(2,128)S(1)}, f32[2,768]{1,0:T(2,128)}, u32[]{:S(2)}) copy-start(f32[2,768]{1,0:T(2,128)} %refs_5_.3) | copy-start | bytes 18436
  57.7 12.9 %copy-start.8 = (s32[16]{0:T(128)S(1)}, s32[16]{0:T(128)}, u32[]{:S(2)}) copy-start(s32[16]{0:T(128)} %refs_0_.5) | copy-start | bytes 196
  57.7 12.9 %copy-start.9 = (s32[16]{0:T(128)S(1)}, s32[16]{0:T(128)}, u32[]{:S(2)}) copy-start(s32[16]{0:T(128)} %refs_1_.5) | copy-start | bytes 196
  107.1 5.8 %copy-start.4 = (f32[32,64]{1,0:T(8,128)}, f32[32,64]{1,0:T(8,128)S(1)}, u32[]{:S(2)}) copy-start(f32[32,64]{1,0:T(8,128)S(1)} %get-tuple-element.32.refs_3_) | copy-start | bytes 24580
  112.9 0.6 copy-start.2
  113.5 0.6 copy-start.3
  114.1 2.0 %copy-start.5 = (f32[32,64]{1,0:T(8,128)}, f32[32,64]{1,0:T(8,128)S(1)}, u32[]{:S(2)}) copy-start(f32[32,64]{1,0:T(8,128)S(1)} %get-tuple-element.33.refs_4_) | copy-start | bytes 24580
Sparse Core Ops, SparseCore 0:
  9.6 11.9 all-gather.6

commit v2 on v1

--- a/solution.py
+++ b/solution.py
@@ -34,32 +34,80 @@
     return jnp.concatenate([high, low], axis=axis)
 
 
-def weights_kernel(rows, base, g_ref, qkv_hbm, out_hbm, mq_ref, mk_ref, mv_ref, wo_ref, gram_ref, buf, sems):
-    width = out_hbm.shape[0]
-    per = width // rows
-    parts, _, depth = g_ref.shape
+def table_kernel(channels, embed_ref, level_ref, vel_ref, out_ref):
+    count, base = level_ref.shape[0], out_ref.shape[0] - vel_ref.shape[0]
+    out_ref[:channels] = embed_ref[...]
+    filler = jnp.zeros((base - channels - count, out_ref.shape[1]), F32)
+    out_ref[channels:base] = jnp.concatenate([level_ref[...].astype(F32), filler], axis=0).astype(BF16)
+    out_ref[base:] = vel_ref[...]
+
+
+def start_chunks(rows, parts, qkv_hbm, out_hbm, buf, sems):
+    per = out_hbm.shape[0] // rows
+    depth = buf.shape[-1]
+    index, count = lax.axis_index("tok"), lax.axis_size("tok")
     copies = []
     for chunk in range(4 * per):
         source = qkv_hbm.at[chunk // per] if chunk < 3 * per else out_hbm
-        copy = pltpu.make_async_copy(
-            source.at[pl.ds((chunk % per) * rows, rows)], buf.at[chunk], sems.at[chunk]
-        )
-        copy.start()
-        copies.append(copy)
-    gram = sum(dot_nt(g_ref[t], g_ref[t, :base]) for t in range(parts))
+        for at, part in enumerate(parts):
+            columns = pl.ds(pl.multiple_of(lax.rem(index + part, count) * depth, LANES), depth)
+            copy = pltpu.make_async_copy(
+                source.at[pl.ds((chunk % per) * rows, rows), columns],
+                buf.at[at, chunk],
+                sems.at[at, chunk],
+            )
+            copy.start()
+            copies.append(copy)
+    return copies
+
+
+def turned(table):
+    return table.astype(F32).T.astype(BF16)
+
+
+def own_weights_kernel(rows, base, g_ref, qkv_hbm, out_hbm, acc_ref, wo_ref, gram_ref, buf, sems):
+    copies = start_chunks(rows, (0,), qkv_hbm, out_hbm, buf, sems)
+    per = out_hbm.shape[0] // rows
+    right = turned(g_ref[...])
+    gram_ref[...] = dot(g_ref[...], right[:, :base])
+    for chunk in range(4 * per):
+        copies[chunk].wait()
+        if chunk < 3 * per:
+            acc_ref[chunk * rows : (chunk + 1) * rows, :] = dot(buf[0, chunk], right[:, :base])
+        else:
+            at = (chunk - 3 * per) * rows
+            wo_ref[at : at + rows, :] = dot(buf[0, chunk], right[:, base:])
+
+
+def other_weights_kernel(rows, base, count, *refs):
+    tables, refs = refs[: count - 1], refs[count - 1 :]
+    acc_ref, wo_acc, gram_acc, qkv_hbm, out_hbm, mq_ref, mk_ref, mv_ref, wo_ref, gram_ref, buf, sems = refs
+    copies = start_chunks(rows, range(1, count), qkv_hbm, out_hbm, buf, sems)
+    per = out_hbm.shape[0] // rows
+    rights = [turned(table[...]) for table in tables]
+    gram = gram_acc[...]
+    for table, right in zip(tables, rights):
+        gram = gram + dot(table[...], right[:, :base])
     gram_ref[...] = halves(gram, 1)
     for chunk in range(4 * per):
-        copies[chunk].wait()
+        for at in range(count - 1):
+            copies[chunk * (count - 1) + at].wait()
+        kind = chunk // per
         where = pl.ds((chunk % per) * rows, rows)
-        blocks = [buf[chunk, :, t * depth : (t + 1) * depth] for t in range(parts)]
-        kind = chunk // per
-        if kind in (0, 2):
-            target = mq_ref if kind == 0 else mv_ref
-            target[where, :] = halves(sum(dot_nt(blocks[t], g_ref[t, :base]) for t in range(parts)), 1)
+        if kind < 3:
+            total = acc_ref[chunk * rows : (chunk + 1) * rows, :]
+        else:
+            total = wo_acc[where, :]
+        for at, right in enumerate(rights):
+            total = total + dot(buf[at, chunk], right[:, :base] if kind < 3 else right[:, base:])
+        if kind == 0:
+            mq_ref[where, :] = halves(total, 1)
         elif kind == 1:
-            mk_ref[:, where] = halves(sum(dot_nt(g_ref[t, :base], blocks[t]) for t in range(parts)), 0)
+            mk_ref[:, where] = halves(total.T, 0)
+        elif kind == 2:
+            mv_ref[where, :] = halves(total, 1)
         else:
-            wo_ref[:, where] = halves(sum(dot_nt(g_ref[t, base:], blocks[t]) for t in range(parts)), 0)
+            wo_ref[:, where] = halves(total.T, 0)
 
 
 def advance(level_count, tok, first, g_ref, hpart_ref, xq_ref):
@@ -113,7 +161,7 @@
         pieces = []
         for w in range(n_key):
             source = lax.rem(first_key - 1 + w + 2 * frames, frames)
-            pieces.append(lat_ref[pl.ds(pl.multiple_of(source * tok, 8), tok), :])
+            pieces += [lat_ref[source, t, 0] for t in range(tok // part_rows)]
         state = jnp.concatenate(pieces, axis=0).T
     else:
         velocity, state = advance(level_count, tok, first_key - 1, g_ref, hprev_ref, xprev_ref)
@@ -255,24 +303,62 @@
     heads = width // HD
     base = round_up(channels + level_count, LANES)
     cfg = (tok, frames, channels, base, depth, level_count, heads, part_rows)
-    vmem, smem, anywhere = (
+    vmem, smem, hbm = (
         pl.BlockSpec(memory_space=pltpu.VMEM),
         pl.BlockSpec(memory_space=pltpu.SMEM),
-        pl.BlockSpec(memory_space=pl.ANY),
+        pl.BlockSpec(memory_space=pltpu.HBM),
     )
     shape = jax.ShapeDtypeStruct
 
-    sent = jnp.where(position == frames - 1, fresh_noise[0], latent[0])
-    latents = lax.all_gather(sent, ("queue", "tok"), axis=0, tiled=True)
-
-    filler = jnp.zeros((base - channels - level_count, embed_weight.shape[1]), BF16)
-    table = jnp.concatenate([embed_weight, level_embed, filler, vel_weight.T], axis=0)
-    table = lax.all_gather(table, "tok", axis=0, tiled=False)
-
-    rows = 256
+    sent = jnp.where(position == frames - 1, fresh_noise[0], latent[0])[None]
+    if frames * tok * channels < 2**18 + 1:
+        sent = jnp.concatenate([sent, fresh_noise], axis=0)
+    latents = lax.all_gather(sent.reshape(-1, channels), ("queue", "tok"), axis=0, tiled=True)
+    latents = latents.reshape(frames, parts, -1, part_rows, channels)
+
+    share = depth // parts
+    table = pl.pallas_call(
+        functools.partial(table_kernel, channels),
+        out_shape=shape((base + channels, share), BF16),
+        in_specs=[vmem] * 3,
+        out_specs=vmem,
+        name="table",
+    )(embed_weight, level_embed, vel_weight.T)
+    tables = [
+        lax.ppermute(table, "tok", [(source, (source - k) % parts) for source in range(parts)])
+        for k in range(1, parts)
+    ]
+
+    rows = 384 if width % 384 == 0 else 256
     chunks = 4 * width // rows
+    limit = pltpu.CompilerParams(vmem_limit_bytes=40 * 2**20)
+
+    def estimate(share_count):
+        return pl.CostEstimate(
+            flops=8 * base * width * share * share_count,
+            bytes_accessed=8 * width * share * share_count,
+            transcendentals=0,
+        )
+
+    sums = pl.pallas_call(
+        functools.partial(own_weights_kernel, rows, base),
+        out_shape=(
+            shape((3 * width, base), F32),
+            shape((width, channels), F32),
+            shape((base + channels, base), F32),
+        ),
+        in_specs=[vmem, hbm, hbm],
+        out_specs=(vmem,) * 3,
+        scratch_shapes=[
+            pltpu.VMEM((1, chunks, rows, share), BF16),
+            pltpu.SemaphoreType.DMA((1, chunks)),
+        ],
+        compiler_params=limit,
+        cost_estimate=estimate(1),
+        name="own_weights",
+    )(table, qkv_weight, out_weight)
     mq, mk, mv, wo, gram = pl.pallas_call(
-        functools.partial(weights_kernel, rows, base),
+        functools.partial(other_weights_kernel, rows, base, parts),
         out_shape=(
             shape((width, 2 * base), BF16),
             shape((2 * base, width), BF16),
@@ -280,18 +366,16 @@
             shape((2 * channels, width), BF16),
             shape((base + channels, 2 * base), BF16),
         ),
-        in_specs=[vmem, anywhere, anywhere],
+        in_specs=[vmem] * (parts + 2) + [hbm, hbm],
         out_specs=(vmem,) * 5,
         scratch_shapes=[
-            pltpu.VMEM((chunks, rows, depth), BF16),
-            pltpu.SemaphoreType.DMA((chunks,)),
+            pltpu.VMEM((parts - 1, chunks, rows, share), BF16),
+            pltpu.SemaphoreType.DMA((parts - 1, chunks)),
         ],
-        compiler_params=pltpu.CompilerParams(vmem_limit_bytes=40 * 2**20),
-        cost_estimate=pl.CostEstimate(
-            flops=2 * base * 4 * width * depth, bytes_accessed=8 * width * depth, transcendentals=0
-        ),
-        name="weights",
-    )(table, qkv_weight, out_weight)
+        compiler_params=limit,
+        cost_estimate=estimate(parts - 1),
+        name="other_weights",
+    )(*tables, *sums, qkv_weight, out_weight)
 
     query_block = max(1, LANES // tok)
     owned = []

time: 125 us -> 126 us (level)
  blocking collectives: 50.9 us -> 6.28 us
  waiting for transfers between devices: 0.02 us -> 41.7 us
  Pallas kernels: 52.4 us -> 54.5 us
  local copies, waits for them, and re-layouts: 4.91 us -> 6.25 us
    all_gather x1 -> x0, blocking collectives: 44.6 us -> none  [body(): latents = lax.all_gather(sent, ('queue', 'tok'), axis=0, tiled=True)]
    all_gather x1, waiting for transfers between devices: 0.01 us -> 41.7 us  [body(): lax.all_gather(sent.reshape(-1, channels), ('queue', 'tok'), axis=0, tile...]
    pallas_call x1 -> x3, Pallas kernels: 12.9 us -> 14.9 us  [the longest x1 7.53 us: body(): pl.pallas_call(functools.partial(own_weights_kernel, rows, base), out_sha...]
    unnamed x22 -> x24, local copies, waits for them, and re-layouts: 4.83 us -> 6.25 us
  transfers between devices with their start and end apart: 1 -> 2, of which waited for: 0 -> 1; matrix products, arithmetic and copies ran while one was open for 0% -> 0% of each run, Pallas kernels for 0% -> 12%
where the time goes in v2:
time: 126 us
  Pallas kernels  54.5 us (43%)
  waiting for transfers between devices  41.7 us (33%)
  between operations  14.2 us (11%)
  blocking collectives  6.28 us (5%)
  local copies, waits for them, and re-layouts  6.25 us (5%)
  other arithmetic  2.18 us (2%)
    all_gather x1, waiting for transfers between devices, body(): lax.all_gather(sent.reshape(-1, channels), ('queue', 'tok'), axis=0, tile...  41.7 us
    pallas_call x3, Pallas kernels, body(): pl.pallas_call(functools.partial(step_kernel, step, cfg), out_shape=tuple...  38 us
    pallas_call x1, Pallas kernels, body(): pl.pallas_call(functools.partial(own_weights_kernel, rows, base), out_sha...  7.53 us
    all_gather x3, blocking collectives, body(): gathered = lax.all_gather(part, 'tok', axis=0, tiled=False)  6.28 us
    unnamed x24, local copies, waits for them, and re-layouts  6.25 us
    pallas_call x1, Pallas kernels, body(): pl.pallas_call(functools.partial(other_weights_kernel, rows, base, parts)...  5.45 us
  transfers between devices with their start and end apart: 2, of which 1 were waited for; matrix products, arithmetic and copies ran while one was open for 0% of the time, Pallas kernels for 12%

profile of v2, /device:TPU:0, one launch (start us, length us, event | category | flops | bytes accessed | tf_op | source)
XLA Modules:
  0.0 125.5 jit_solution(8903954632181016273)
XLA Ops:
  7.2 0.0 all-gather.5.cloned.1.call-start
  7.2 0.7 slice_select_fusion
  8.0 1.4 %pad_maximum_fusion = f32[4,32,64]{2,1,0:T(8,128)} fusion(f32[3,32,64]{2,1,0:T(8,128)} %refs_5_.4, f32[1,32,64]{2,1,0:T(8,128)S(1)} %slice_select_fusion), kind=kLoop, calls=%fused_computation | loop fusion | flops 8192 | bytes 65536 | tf_op jit(solution)/shard_map/concatenate | solution.py:315
  9.4 0.0 all-gather.5.cloned.1.call-update
  9.4 1.9 %table.1.g_ref = bf16[192,1536]{1,0:T(8,128)(2,1)} custom-call(bf16[64,1536]{1,0:T(8,128)(2,1)} %embed_ref.1, bf16[19,1536]{1,0:T(8,128)(2,1)} %level_ref.1, bf16[64,1536]{1,0:T(8,128)(2,1)} %bitcast.11), custom_call_target="tpu_custom_call" | custom-call | tf_op jit(solution)/shard_map/table/pallas_call | solution.py:320
  11.3 0.5 collective-permute-start
  11.8 2.3 %copy-done = bf16[768,3072]{1,0:T(8,128)(2,1)S(1)} copy-done((bf16[768,3072]{1,0:T(8,128)(2,1)S(1)}, bf16[768,3072]{1,0:T(8,128)(2,1)}, u32[]{:S(2)}) %copy-start) | copy-done | bytes 4718616
  14.1 1.1 copy-done.2
  15.2 7.5 %own_weights.1 = (f32[2304,128]{1,0:T(8,128)S(1)}, f32[768,64]{1,0:T(8,128)S(1)}, f32[192,128]{1,0:T(8,128)S(1)}) custom-call(bf16[192,1536]{1,0:T(8,128)(2,1)S(1)} %copy-done.2, bf16[3,768,3072]{2,1,0:T(8,128)(2,1)} %refs_4_.2, bf16[768,3072]{1,0:T(8,128)(2,1)S(1)} %copy-done), custom_call_target="tpu_custom_call" | custom-call | flops 1207959552 | bytes 9437184 | tf_op jit(solution)/shard_map/own_weights/pallas_call | solution.py:343
  22.8 0.0 copy-start.3
  22.8 0.0 copy-start.10
  22.8 0.0 copy-start.11
  22.8 5.4 %other_weights.1 = (bf16[768,256]{1,0:T(8,128)(2,1)S(1)}, bf16[256,768]{1,0:T(8,128)(2,1)S(1)}, bf16[768,256]{1,0:T(8,128)(2,1)S(1)}, bf16[128,768]{1,0:T(8,128)(2,1)S(1)}, bf16[192,256]{1,0:T(8,128)(2,1)S(1)}) custom-call(bf16[192,1536]{1,0:T(8,128)(2,1)S(1)} %collective-permute-done.refs_0_, f32[2304,128]{1,0:T(8,128)S(1)} %get-tuple-element.21.refs_1_, ...), custom_call_target="tpu_custom_call" | custom-call | flops 1207959552 | bytes 9437184 | tf_op jit(solution)/shard_map/other_weights/pallas_call | solution.py:360
  28.3 41.7 %all-gather.5.cloned.1.call-done = f32[4096,64]{1,0:T(8,128)} async-done(((f32[128,64]{1,0:T(8,128)}), f32[4096,64]{1,0:T(8,128)}) %all-gather.5.cloned.1.call-update) | async-done | bytes 1048592 | tf_op jit(solution)/shard_map/all_gather | solution.py:316
  70.0 1.6 %copy-done.8 = f32[4096,64]{1,0:T(8,128)S(1)} copy-done((f32[4096,64]{1,0:T(8,128)S(1)}, f32[4096,64]{1,0:T(8,128)}, u32[]{:S(2)}) %copy-start.8) | copy-done | bytes 1048600
  71.6 21.4 %step0.1 = (f32[64,896]{1,0:T(8,128)S(1)}, f32[64,896]{1,0:T(8,128)S(1)}, f32[64,896]{1,0:T(8,128)S(1)}) custom-call(s32[16]{0:T(128)S(1)} %copy-done.10, s32[16]{0:T(128)S(1)} %copy-done.11, f32[16,2,4,32,64]{4,3,2,1,0:T(8,128)S(1)} %bitcast.8, f32[3,32,64]{2,1,0:T(8,128)S(1)} %copy-done.3, f32[2,768]{1,0:T(2,128)S(1)} %copy-done.9, ...), custom_call_target="tpu_custom_call" | custom-call | flops 2919235584 | bytes 786432 | tf_op jit(solution)/shard_map/step0/pallas_call | solution.py:402
  92.9 2.3 %all-gather = f32[128,896]{1,0:T(8,128)S(1)} all-gather(f32[64,896]{1,0:T(8,128)S(1)} %get-tuple-element.29), channel_id=2, replica_groups=mesh['queue'=16,'tok'=2] {'tok'}, dimensions={0}, use_global_device_ids=true | all-gather | bytes 688128 | tf_op jit(solution)/shard_map/all_gather | solution.py:424
  95.3 12.8 %step1.1 = (f32[64,512]{1,0:T(8,128)S(1)}, f32[64,512]{1,0:T(8,128)S(1)}, f32[64,512]{1,0:T(8,128)S(1)}, f32[32,64]{1,0:T(8,128)S(1)}) custom-call(s32[16]{0:T(128)S(1)} %copy-done.10, s32[16]{0:T(128)S(1)} %copy-done.11, f32[2,64,896]{2,1,0:T(8,128)S(1)} %bitcast.6, f32[64,896]{1,0:T(8,128)S(1)} %get-tuple-element.30.refs_3_, ...), custom_call_target="tpu_custom_call" | custom-call | flops 1862270976 | bytes 786432 | tf_op jit(solution)/shard_map/step1/pallas_call | solution.py:402
  108.1 2.0 %all-gather.1 = f32[128,512]{1,0:T(8,128)S(1)} all-gather(f32[64,512]{1,0:T(8,128)S(1)} %get-tuple-element.32), channel_id=3, replica_groups=mesh['queue'=16,'tok'=2] {'tok'}, dimensions={0}, use_global_device_ids=true | all-gather | bytes 393216 | tf_op jit(solution)/shard_map/all_gather | solution.py:424
  110.1 3.8 %step2.1 = (f32[64,128]{1,0:T(8,128)S(1)}, f32[64,128]{1,0:T(8,128)S(1)}, f32[64,128]{1,0:T(8,128)S(1)}, f32[32,64]{1,0:T(8,128)S(1)}) custom-call(s32[16]{0:T(128)S(1)} %copy-done.10, s32[16]{0:T(128)S(1)} %copy-done.11, f32[2,64,512]{2,1,0:T(8,128)S(1)} %bitcast.7, f32[64,512]{1,0:T(8,128)S(1)} %get-tuple-element.33.refs_3_, ...), custom_call_target="tpu_custom_call" | custom-call | flops 805306368 | bytes 786432 | tf_op jit(solution)/shard_map/step2/pallas_call | solution.py:402
  113.9 0.6 copy-done.4
  114.5 0.6 copy-done.5
  115.1 2.0 %all-gather.2 = f32[128,128]{1,0:T(8,128)} all-gather(f32[64,128]{1,0:T(8,128)S(1)} %get-tuple-element.35), channel_id=4, replica_groups=mesh['queue'=16,'tok'=2] {'tok'}, dimensions={0}, use_global_device_ids=true | all-gather | bytes 98304 | tf_op jit(solution)/shard_map/all_gather | solution.py:424
  117.1 1.6 %last.1 = (f32[3,1,32,64]{3,2,1,0:T(8,128)}, f32[1,32,64]{2,1,0:T(8,128)}) custom-call(f32[2,64,128]{2,1,0:T(8,128)} %bitcast.10, f32[64,128]{1,0:T(8,128)} %copy-done.4, f32[64,128]{1,0:T(8,128)} %copy-done.5, f32[32,64]{1,0:T(8,128)} %copy-done.6, f32[32,64]{1,0:T(8,128)} %copy-done.7), custom_call_target="tpu_custom_call" | custom-call | tf_op jit(solution)/shard_map/last/pallas_call | solution.py:427
  (17 shorter events, 0.0 us)
Async XLA Ops:
  7.2 62.8 %all-gather.5.cloned.1.call-start = ((), (), s32[]{:S(2)}) async-start(), calls=%async_computation | async-start | bytes 2162688 | tf_op jit(solution)/shard_map/all_gather | solution.py:316
  11.3 11.4 %collective-permute-start = (bf16[192,1536]{1,0:T(8,128)(2,1)}, bf16[192,1536]{1,0:T(8,128)(2,1)S(1)}, u32[]{:S(2)}, u32[]{:S(2)}) collective-permute-start(bf16[192,1536]{1,0:T(8,128)(2,1)} %table.1.g_ref), channel_id=1, source_target_pairs={{0,1},{1,0},{2,3},{3,2},{4,5},{5,4},{6,7},{7,6},{8,9},{9,8},{10,11... | collective-permute-start | bytes 1769480 | tf_op jit(solution)/shard_map/ppermute | solution.py:328
  11.8 2.3 %copy-start = (bf16[768,3072]{1,0:T(8,128)(2,1)S(1)}, bf16[768,3072]{1,0:T(8,128)(2,1)}, u32[]{:S(2)}) copy-start(bf16[768,3072]{1,0:T(8,128)(2,1)} %refs_5_.3) | copy-start | bytes 14155780
  14.1 1.1 copy-start.2
  15.2 7.5 %copy-start.1 = (bf16[768,3072]{1,0:T(8,128)(2,1)S(1)}, bf16[768,3072]{1,0:T(8,128)(2,1)}, u32[]{:S(2)}) copy-start(bf16[768,3072]{1,0:T(8,128)(2,1)} %refs_5_.3) | copy-start | bytes 14155780
  22.8 47.2 %copy-start.3 = (f32[3,32,64]{2,1,0:T(8,128)S(1)}, f32[3,32,64]{2,1,0:T(8,128)}, u32[]{:S(2)}) copy-start(f32[3,32,64]{2,1,0:T(8,128)} %refs_5_.4) | copy-start | bytes 73732
  22.8 47.2 %copy-start.9 = (f32[2,768]{1,0:T(2,128)S(1)}, f32[2,768]{1,0:T(2,128)}, u32[]{:S(2)}) copy-start(f32[2,768]{1,0:T(2,128)} %refs_5_.5) | copy-start | bytes 18436
  22.8 47.2 %copy-start.10 = (s32[16]{0:T(128)S(1)}, s32[16]{0:T(128)}, u32[]{:S(2)}) copy-start(s32[16]{0:T(128)} %refs_0_.5) | copy-start | bytes 196
  22.8 47.2 %copy-start.11 = (s32[16]{0:T(128)S(1)}, s32[16]{0:T(128)}, u32[]{:S(2)}) copy-start(s32[16]{0:T(128)} %refs_1_.5) | copy-start | bytes 196
  70.0 1.6 %copy-start.8 = (f32[4096,64]{1,0:T(8,128)S(1)}, f32[4096,64]{1,0:T(8,128)}, u32[]{:S(2)}) copy-start(f32[4096,64]{1,0:T(8,128)} %all-gather.5.cloned.1.call-done) | copy-start | bytes 3145732
  108.1 9.0 %copy-start.6 = (f32[32,64]{1,0:T(8,128)}, f32[32,64]{1,0:T(8,128)S(1)}, u32[]{:S(2)}) copy-start(f32[32,64]{1,0:T(8,128)S(1)} %get-tuple-element.38.refs_3_) | copy-start | bytes 24580
  113.9 0.6 copy-start.4
  114.5 0.6 copy-start.5
  115.1 2.0 %copy-start.7 = (f32[32,64]{1,0:T(8,128)}, f32[32,64]{1,0:T(8,128)S(1)}, u32[]{:S(2)}) copy-start(f32[32,64]{1,0:T(8,128)S(1)} %get-tuple-element.39.refs_4_) | copy-start | bytes 24580
Sparse Core Ops, SparseCore 0:
  10.9 59.0 all-gather.4

commit v3 on v2

--- a/solution.py
+++ b/solution.py
@@ -34,80 +34,82 @@
     return jnp.concatenate([high, low], axis=axis)
 
 
-def table_kernel(channels, embed_ref, level_ref, vel_ref, out_ref):
-    count, base = level_ref.shape[0], out_ref.shape[0] - vel_ref.shape[0]
-    out_ref[:channels] = embed_ref[...]
-    filler = jnp.zeros((base - channels - count, out_ref.shape[1]), F32)
-    out_ref[channels:base] = jnp.concatenate([level_ref[...].astype(F32), filler], axis=0).astype(BF16)
-    out_ref[base:] = vel_ref[...]
-
-
-def start_chunks(rows, parts, qkv_hbm, out_hbm, buf, sems):
+def start_chunks(rows, chunks, parts, qkv_hbm, out_hbm, buf, sems):
     per = out_hbm.shape[0] // rows
     depth = buf.shape[-1]
     index, count = lax.axis_index("tok"), lax.axis_size("tok")
     copies = []
-    for chunk in range(4 * per):
+    for place, chunk in enumerate(chunks):
         source = qkv_hbm.at[chunk // per] if chunk < 3 * per else out_hbm
         for at, part in enumerate(parts):
             columns = pl.ds(pl.multiple_of(lax.rem(index + part, count) * depth, LANES), depth)
             copy = pltpu.make_async_copy(
                 source.at[pl.ds((chunk % per) * rows, rows), columns],
-                buf.at[at, chunk],
-                sems.at[at, chunk],
+                buf.at[at, place],
+                sems.at[at, place],
             )
             copy.start()
             copies.append(copy)
     return copies
 
 
-def turned(table):
-    return table.astype(F32).T.astype(BF16)
-
-
-def own_weights_kernel(rows, base, g_ref, qkv_hbm, out_hbm, acc_ref, wo_ref, gram_ref, buf, sems):
-    copies = start_chunks(rows, (0,), qkv_hbm, out_hbm, buf, sems)
+def stack_rows(base, embed_ref, level_ref):
+    filler = base - embed_ref.shape[0] - level_ref.shape[0]
+    rows = [embed_ref[...].astype(F32), level_ref[...].astype(F32)]
+    return jnp.concatenate(rows + [jnp.zeros((filler, embed_ref.shape[1]), F32)], axis=0)
+
+
+def turned(base, embed_ref, level_ref, vel_ref):
+    left = stack_rows(base, embed_ref, level_ref)
+    return left.astype(BF16), left.T.astype(BF16), vel_ref[...].astype(F32).T.astype(BF16)
+
+
+def own_weights_kernel(rows, base, *refs):
+    qkv_hbm, out_hbm, acc_ref, wo_ref, gram_ref, gv_ref, buf, sems = refs[3:]
     per = out_hbm.shape[0] // rows
-    right = turned(g_ref[...])
-    gram_ref[...] = dot(g_ref[...], right[:, :base])
+    copies = start_chunks(rows, range(4 * per), (0,), qkv_hbm, out_hbm, buf, sems)
+    left, right, vel = turned(base, *refs[:3])
+    gram_ref[...] = dot(left, right)
+    gv_ref[...] = dot(refs[2][...], right)
     for chunk in range(4 * per):
         copies[chunk].wait()
         if chunk < 3 * per:
-            acc_ref[chunk * rows : (chunk + 1) * rows, :] = dot(buf[0, chunk], right[:, :base])
+            acc_ref[chunk * rows : (chunk + 1) * rows, :] = dot(buf[0, chunk], right)
         else:
             at = (chunk - 3 * per) * rows
-            wo_ref[at : at + rows, :] = dot(buf[0, chunk], right[:, base:])
-
-
-def other_weights_kernel(rows, base, count, *refs):
-    tables, refs = refs[: count - 1], refs[count - 1 :]
-    acc_ref, wo_acc, gram_acc, qkv_hbm, out_hbm, mq_ref, mk_ref, mv_ref, wo_ref, gram_ref, buf, sems = refs
-    copies = start_chunks(rows, range(1, count), qkv_hbm, out_hbm, buf, sems)
+            wo_ref[at : at + rows, :] = dot(buf[0, chunk], vel)
+
+
+def other_weights_kernel(rows, base, count, second, *refs):
+    tables, refs = refs[: 3 * (count - 1)], refs[3 * (count - 1) :]
+    acc_ref, wo_acc, gram_acc, gv_acc, qkv_hbm, out_hbm, _ = refs[:7]
+    outs, buf, sems = refs[7:-2], refs[-2], refs[-1]
     per = out_hbm.shape[0] // rows
-    rights = [turned(table[...]) for table in tables]
-    gram = gram_acc[...]
-    for table, right in zip(tables, rights):
-        gram = gram + dot(table[...], right[:, :base])
-    gram_ref[...] = halves(gram, 1)
-    for chunk in range(4 * per):
+    chunks = range(2 * per, 4 * per) if second else range(2 * per)
+    copies = start_chunks(rows, chunks, range(1, count), qkv_hbm, out_hbm, buf, sems)
+    rights = [turned(base, *tables[3 * at : 3 * at + 3]) for at in range(count - 1)]
+    if second:
+        gram, gv = gram_acc[...], gv_acc[...]
+        for at, (left, right, _) in enumerate(rights):
+            gram = gram + dot(left, right)
+            gv = gv + dot(tables[3 * at + 2][...], right)
+        outs[2][:base] = halves(gram, 1)
+        outs[2][base:] = halves(gv, 1)
+    for place, chunk in enumerate(chunks):
         for at in range(count - 1):
-            copies[chunk * (count - 1) + at].wait()
+            copies[place * (count - 1) + at].wait()
         kind = chunk // per
         where = pl.ds((chunk % per) * rows, rows)
         if kind < 3:
             total = acc_ref[chunk * rows : (chunk + 1) * rows, :]
         else:
             total = wo_acc[where, :]
-        for at, right in enumerate(rights):
-            total = total + dot(buf[at, chunk], right[:, :base] if kind < 3 else right[:, base:])
-        if kind == 0:
-            mq_ref[where, :] = halves(total, 1)
-        elif kind == 1:
-            mk_ref[:, where] = halves(total.T, 0)
-        elif kind == 2:
-            mv_ref[where, :] = halves(total, 1)
+        for at, (_, right, vel) in enumerate(rights):
+            total = total + dot(buf[at, place], right if kind < 3 else vel)
+        if kind % 2:
+            outs[1][:, where] = halves(total.T, 0)
         else:
-            wo_ref[:, where] = halves(total.T, 0)
+            outs[0][where, :] = halves(total, 1)
 
 
 def advance(level_count, tok, first, g_ref, hpart_ref, xq_ref):
@@ -140,8 +142,9 @@
     refs = list(refs)
     slot_ref, reach_ref = refs[0], refs[1]
     if step == 0:
-        lat_ref = refs[2]
-        refs = refs[3:]
+        count = tok // part_rows
+        lat_refs = refs[2 : 2 + count]
+        refs = refs[2 + count :]
     else:
         g_ref, hprev_ref, xprev_ref = refs[2:5]
         refs = refs[5:]
@@ -155,14 +158,15 @@
     own_ref = None
     if step > 0:
         own_ref = refs.pop(0)
-    kbuf, vbuf, qbuf, att, tbuf = refs
+    kbuf, vbuf, qbuf, att, tbuf, xbuf = refs
 
     if step == 0:
-        pieces = []
         for w in range(n_key):
             source = lax.rem(first_key - 1 + w + 2 * frames, frames)
-            pieces += [lat_ref[source, t, 0] for t in range(tok // part_rows)]
-        state = jnp.concatenate(pieces, axis=0).T
+            for t in range(count):
+                at = lax.rem(tok_index + t, count) * part_rows + w * tok
+                xbuf[pl.ds(pl.multiple_of(at, 8), part_rows), :] = lat_refs[t][position ^ source]
+        state = xbuf[...].T
     else:
         velocity, state = advance(level_count, tok, first_key - 1, g_ref, hprev_ref, xprev_ref)
         mine = (HALO + 1) * (STEPS - step)
@@ -310,33 +314,36 @@
     )
     shape = jax.ShapeDtypeStruct
 
-    sent = jnp.where(position == frames - 1, fresh_noise[0], latent[0])[None]
-    if frames * tok * channels < 2**18 + 1:
-        sent = jnp.concatenate([sent, fresh_noise], axis=0)
-    latents = lax.all_gather(sent.reshape(-1, channels), ("queue", "tok"), axis=0, tiled=True)
-    latents = latents.reshape(frames, parts, -1, part_rows, channels)
+    def swapped(value, axis, distance):
+        count = lax.axis_size(axis)
+        return lax.ppermute(value, axis, [(source, source ^ distance) for source in range(count)])
+
+    def from_ahead(value, distance):
+        return lax.ppermute(value, "tok", [(source, (source - distance) % parts) for source in range(parts)])
+
+    state = jnp.where(position == frames - 1, fresh_noise[0], latent[0])[None]
+    rounds = []
+    reached = 1
+    while reached < frames:
+        group = min(4, frames // reached)
+        moved = [swapped(state, "queue", reached * d) for d in range(1, group)]
+        state = jnp.concatenate([state] + moved, axis=0)
+        rounds.append(state)
+        reached *= group
+    latents = [state] + [from_ahead(state, d) for d in range(1, parts)]
 
     share = depth // parts
-    table = pl.pallas_call(
-        functools.partial(table_kernel, channels),
-        out_shape=shape((base + channels, share), BF16),
-        in_specs=[vmem] * 3,
-        out_specs=vmem,
-        name="table",
-    )(embed_weight, level_embed, vel_weight.T)
-    tables = [
-        lax.ppermute(table, "tok", [(source, (source - k) % parts) for source in range(parts)])
-        for k in range(1, parts)
-    ]
+    table = (embed_weight, level_embed, vel_weight.T)
+    tables = [from_ahead(piece, d) for d in range(1, parts) for piece in table]
 
     rows = 384 if width % 384 == 0 else 256
     chunks = 4 * width // rows
-    limit = pltpu.CompilerParams(vmem_limit_bytes=40 * 2**20)
+    limit = pltpu.CompilerParams(vmem_limit_bytes=60 * 2**20)
 
     def estimate(share_count):
         return pl.CostEstimate(
-            flops=8 * base * width * share * share_count,
-            bytes_accessed=8 * width * share * share_count,
+            flops=int(8 * base * width * share * share_count),
+            bytes_accessed=int(8 * width * share * share_count),
             transcendentals=0,
         )
 
@@ -345,10 +352,11 @@
         out_shape=(
             shape((3 * width, base), F32),
             shape((width, channels), F32),
-            shape((base + channels, base), F32),
+            shape((base, base), F32),
+            shape((channels, base), F32),
         ),
-        in_specs=[vmem, hbm, hbm],
-        out_specs=(vmem,) * 3,
+        in_specs=[vmem] * 3 + [hbm] * 2,
+        out_specs=(vmem,) * 4,
         scratch_shapes=[
             pltpu.VMEM((1, chunks, rows, share), BF16),
             pltpu.SemaphoreType.DMA((1, chunks)),
@@ -356,26 +364,30 @@
         compiler_params=limit,
         cost_estimate=estimate(1),
         name="own_weights",
-    )(table, qkv_weight, out_weight)
-    mq, mk, mv, wo, gram = pl.pallas_call(
-        functools.partial(other_weights_kernel, rows, base, parts),
-        out_shape=(
-            shape((width, 2 * base), BF16),
-            shape((2 * base, width), BF16),
-            shape((width, 2 * base), BF16),
-            shape((2 * channels, width), BF16),
-            shape((base + channels, 2 * base), BF16),
-        ),
-        in_specs=[vmem] * (parts + 2) + [hbm, hbm],
-        out_specs=(vmem,) * 5,
-        scratch_shapes=[
-            pltpu.VMEM((parts - 1, chunks, rows, share), BF16),
-            pltpu.SemaphoreType.DMA((parts - 1, chunks)),
-        ],
-        compiler_params=limit,
-        cost_estimate=estimate(parts - 1),
-        name="other_weights",
-    )(*tables, *sums, qkv_weight, out_weight)
+    )(*table, qkv_weight, out_weight)
+
+    def other_weights(second, after):
+        outs = [shape((width, 2 * base), BF16)]
+        if second:
+            outs += [shape((2 * channels, width), BF16), shape((base + channels, 2 * base), BF16)]
+        else:
+            outs += [shape((2 * base, width), BF16)]
+        return pl.pallas_call(
+            functools.partial(other_weights_kernel, rows, base, parts, second),
+            out_shape=tuple(outs),
+            in_specs=[vmem] * (3 * (parts - 1) + 4) + [hbm] * 2 + [pl.BlockSpec(memory_space=pl.ANY)],
+            out_specs=(vmem,) * len(outs),
+            scratch_shapes=[
+                pltpu.VMEM((parts - 1, chunks // 2, rows, share), BF16),
+                pltpu.SemaphoreType.DMA((parts - 1, chunks // 2)),
+            ],
+            compiler_params=limit,
+            cost_estimate=estimate(0.5 * (parts - 1)),
+            name="other_weights",
+        )(*tables, *sums, qkv_weight, out_weight, after)
+
+    mq, mk = other_weights(False, rounds[0])
+    mv, wo, gram = other_weights(True, rounds[-1])
 
     query_block = max(1, LANES // tok)
     owned = []
@@ -385,8 +397,8 @@
         args = [frame_slot, frame_reach]
         specs = [smem, smem]
         if step == 0:
-            args += [latents]
-            specs += [vmem]
+            args += latents
+            specs += [vmem] * parts
         else:
             args += [gathered, hpart, xq]
             specs += [vmem] * 3
@@ -410,6 +422,7 @@
                 pltpu.VMEM((width, query_lanes), BF16),
                 pltpu.VMEM((width, query_lanes), BF16),
                 pltpu.VMEM((tok, channels), F32),
+                pltpu.VMEM((key_lanes if step == 0 else tok, channels), F32),
             ],
             compiler_params=pltpu.CompilerParams(vmem_limit_bytes=48 * 2**20),
             cost_estimate=pl.CostEstimate(
@@ -433,6 +446,7 @@
             in_specs=[vmem] * (3 + len(owned)),
             out_specs=(vmem, vmem),
             scratch_shapes=[pltpu.VMEM((tok, channels), F32)],
+            compiler_params=pltpu.CompilerParams(vmem_limit_bytes=8 * 2**20),
             name="last",
         )(gathered, hpart, xq, *owned)
     )

time: 126 us -> 91.8 us (0.73)
  waiting for transfers between devices: 41.7 us -> 6.78 us
  between operations: 14.2 us -> 0.9 us
  starting transfers between devices: 0.49 us -> 12.8 us
  Pallas kernels: 54.5 us -> 59.5 us
  local copies, waits for them, and re-layouts: 6.25 us -> 4.56 us
  other arithmetic: 2.18 us -> 0.75 us
    all_gather x1 -> x0, waiting for transfers between devices: 41.7 us -> none  [body(): lax.all_gather(sent.reshape(-1, channels), ('queue', 'tok'), axis=0, tile...]
    ppermute x1 -> x10, starting transfers between devices: 0.45 us -> 12.8 us  [the longest x6 12.2 us: swapped(): lax.ppermute(value, axis, [(source, source ^ distance) for source in rang...]
    ppermute x1 -> x10, waiting for transfers between devices: 0.01 us -> 6.78 us  [the longest x6 6.77 us: swapped(): lax.ppermute(value, axis, [(source, source ^ distance) for source in rang...]
    pallas_call x2, Pallas kernels: 7.36 us -> 11.3 us  [other_weights(): pl.pallas_call(functools.partial(other_weights_kernel, rows, base, parts,...]
    unnamed x24 -> x41, local copies, waits for them, and re-layouts: 6.25 us -> 4.55 us
    pallas_call x1, Pallas kernels: 7.53 us -> 9.21 us  [body(): pl.pallas_call(functools.partial(own_weights_kernel, rows, base), out_sha...]
    concatenate x1, other arithmetic: 1.44 us -> 0.01 us  [body(): state = jnp.concatenate([state] + moved, axis=0)]
  transfers between devices with their start and end apart: 2 -> 10, of which waited for: 1 -> 5; matrix products, arithmetic and copies ran while one was open for 0% -> 0% of each run, Pallas kernels for 12% -> 22%
where the time goes in v3:
time: 91.8 us; the launch traced here: 91.4 us
  Pallas kernels  59.5 us (65%)
  starting transfers between devices  12.8 us (14%)
  waiting for transfers between devices  6.78 us (7%)
  blocking collectives  6.14 us (7%)
  local copies, waits for them, and re-layouts  4.56 us (5%)
    pallas_call x3, Pallas kernels, body(): pl.pallas_call(functools.partial(step_kernel, step, cfg), out_shape=tuple...  38.2 us
    ppermute x6, starting transfers between devices, swapped(): lax.ppermute(value, axis, [(source, source ^ distance) for source in rang...  12.2 us
    pallas_call x2, Pallas kernels, other_weights(): pl.pallas_call(functools.partial(other_weights_kernel, rows, base, parts,...  11.3 us
    pallas_call x1, Pallas kernels, body(): pl.pallas_call(functools.partial(own_weights_kernel, rows, base), out_sha...  9.21 us
    ppermute x6, waiting for transfers between devices, swapped(): lax.ppermute(value, axis, [(source, source ^ distance) for source in rang...  6.77 us
    all_gather x3, blocking collectives, body(): gathered = lax.all_gather(part, 'tok', axis=0, tiled=False)  6.14 us
    unnamed x41, local copies, waits for them, and re-layouts  4.55 us
  transfers between devices with their start and end apart: 10, of which 5 were waited for; matrix products, arithmetic and copies ran while one was open for 0% of the time, Pallas kernels for 22%

profile of v3, /device:TPU:0, one launch (start us, length us, event | category | flops | bytes accessed | tf_op | source)
XLA Modules:
  0.0 91.4 jit_solution(1235628025812565342)
XLA Ops:
  0.6 0.7 constant_dynamic-update-slice_fusion.6
  1.4 2.9 %collective-permute-start = (f32[1,32,64]{2,1,0:T(8,128)S(1)}, f32[1,32,64]{2,1,0:T(8,128)S(1)}, u32[]{:S(2)}, u32[]{:S(2)}) collective-permute-start(f32[1,32,64]{2,1,0:T(8,128)S(1)} %get-tuple-element.43), channel_id=1, source_target_pairs={{0,2},{2,0},{4,6},{6,4},{8,10},{10,8},{12,14},{14,12},{16,18},{18,... | collective-permute-start | bytes 24584 | tf_op jit(solution)/shard_map/ppermute | solution.py:319
  4.3 1.5 %collective-permute-start.1 = (f32[1,32,64]{2,1,0:T(8,128)S(1)}, f32[1,32,64]{2,1,0:T(8,128)S(1)}, u32[]{:S(2)}, u32[]{:S(2)}) collective-permute-start(f32[1,32,64]{2,1,0:T(8,128)S(1)} %get-tuple-element.43), channel_id=1, source_target_pairs={{0,4},{2,6},{4,0},{6,2},{8,12},{10,14},{12,8},{14,10},{16,20},{18,... | collective-permute-start | bytes 24584 | tf_op jit(solution)/shard_map/ppermute | solution.py:319
  6.4 1.7 %collective-permute-done.1 = f32[1,32,64]{2,1,0:T(8,128)S(1)} collective-permute-done((f32[1,32,64]{2,1,0:T(8,128)S(1)}, f32[1,32,64]{2,1,0:T(8,128)S(1)}, u32[]{:S(2)}, u32[]{:S(2)}) %collective-permute-start.1) | collective-permute-done | bytes 8224 | tf_op jit(solution)/shard_map/ppermute | solution.py:319
  8.1 2.4 %collective-permute-done.2 = f32[1,32,64]{2,1,0:T(8,128)S(1)} collective-permute-done((f32[1,32,64]{2,1,0:T(8,128)S(1)}, f32[1,32,64]{2,1,0:T(8,128)S(1)}, u32[]{:S(2)}, u32[]{:S(2)}) %collective-permute-start.2) | collective-permute-done | bytes 8224 | tf_op jit(solution)/shard_map/ppermute | solution.py:319
  10.5 1.6 %collective-permute-start.3 = (f32[4,32,64]{2,1,0:T(8,128)S(1)}, f32[4,32,64]{2,1,0:T(8,128)S(1)}, u32[]{:S(2)}, u32[]{:S(2)}) collective-permute-start(f32[4,32,64]{2,1,0:T(8,128)S(1)} %pad_maximum_fusion.refs_9_), channel_id=1, source_target_pairs={{0,8},{2,10},{4,12},{6,14},{8,0},{10,2},{12,4},{14,6},{16,24},{18,... | collective-permute-start | bytes 98312 | tf_op jit(solution)/shard_map/ppermute | solution.py:319
  12.1 2.6 %collective-permute-start.4 = (f32[4,32,64]{2,1,0:T(8,128)S(1)}, f32[4,32,64]{2,1,0:T(8,128)S(1)}, u32[]{:S(2)}, u32[]{:S(2)}) collective-permute-start(f32[4,32,64]{2,1,0:T(8,128)S(1)} %pad_maximum_fusion.refs_9_), channel_id=1, source_target_pairs={{0,16},{2,18},{4,20},{6,22},{8,24},{10,26},{12,28},{14,30},{16,0},... | collective-permute-start | bytes 98312 | tf_op jit(solution)/shard_map/ppermute | solution.py:319
  14.8 3.6 %collective-permute-start.5 = (f32[4,32,64]{2,1,0:T(8,128)S(1)}, f32[4,32,64]{2,1,0:T(8,128)S(1)}, u32[]{:S(2)}, u32[]{:S(2)}) collective-permute-start(f32[4,32,64]{2,1,0:T(8,128)S(1)} %pad_maximum_fusion.refs_9_), channel_id=1, source_target_pairs={{0,24},{2,26},{4,28},{6,30},{8,16},{10,18},{12,20},{14,22},{16,8},... | collective-permute-start | bytes 98312 | tf_op jit(solution)/shard_map/ppermute | solution.py:319
  18.7 2.2 %collective-permute-done.5 = f32[4,32,64]{2,1,0:T(8,128)S(1)} collective-permute-done((f32[4,32,64]{2,1,0:T(8,128)S(1)}, f32[4,32,64]{2,1,0:T(8,128)S(1)}, u32[]{:S(2)}, u32[]{:S(2)}) %collective-permute-start.5) | collective-permute-done | bytes 32800 | tf_op jit(solution)/shard_map/ppermute | solution.py:319
  21.1 9.2 %own_weights.1 = (f32[2304,128]{1,0:T(8,128)}, f32[768,64]{1,0:T(8,128)}, f32[128,128]{1,0:T(8,128)}, f32[64,128]{1,0:T(8,128)}) custom-call(bf16[64,1536]{1,0:T(8,128)(2,1)} %refs_0_.4, bf16[19,1536]{1,0:T(8,128)(2,1)} %refs_1_.4, bf16[64,1536]{1,0:T(8,128)(2,1)} %bitcast.8, bf16[3,768,3072]{2,1,0:T(8,128)(2,1)} %refs_7_.3, bf16[768,3072]{1,0:T(8,128)(2,1)} %refs_8_.3), custom_call_target="tpu_custom_call" | custom-call | flops 1207959552 | bytes 9437184 | tf_op jit(solution)/shard_map/own_weights/pallas_call | solution.py:350
  30.3 0.6 copy-done.16
  31.1 5.7 %other_weights.2 = (bf16[768,256]{1,0:T(8,128)(2,1)}, bf16[256,768]{1,0:T(8,128)(2,1)}) custom-call(bf16[64,1536]{1,0:T(8,128)(2,1)} %copy-done.14, bf16[19,1536]{1,0:T(8,128)(2,1)} %copy-done.16, bf16[64,1536]{1,0:T(8,128)(2,1)} %copy-done.15, f32[2304,128]{1,0:T(8,128)} %get-tuple-element.22.refs_3_, f32[768,64]{1,0:T(8,128)} %get-tuple-element.23.refs_4_, ...), custom_call_target="tpu_custom_call" | custom-call | flops 603979776 | bytes 4718592 | tf_op jit(solution)/shard_map/other_weights/pallas_call | solution.py:375
  36.8 5.6 %other_weights.3 = (bf16[768,256]{1,0:T(8,128)(2,1)}, bf16[128,768]{1,0:T(8,128)(2,1)}, bf16[192,256]{1,0:T(8,128)(2,1)}) custom-call(bf16[64,1536]{1,0:T(8,128)(2,1)} %copy-done.14, bf16[19,1536]{1,0:T(8,128)(2,1)} %copy-done.16, bf16[64,1536]{1,0:T(8,128)(2,1)} %copy-done.15, f32[2304,128]{1,0:T(8,128)} %get-tuple-element.22.refs_3_, ...), custom_call_target="tpu_custom_call" | custom-call | flops 603979776 | bytes 4718592 | tf_op jit(solution)/shard_map/other_weights/pallas_call | solution.py:375
  42.5 0.9 %copy-done.1 = f32[16,32,64]{2,1,0:T(8,128)S(1)} copy-done((f32[16,32,64]{2,1,0:T(8,128)S(1)}, f32[16,32,64]{2,1,0:T(8,128)}, u32[]{:S(2)}) %copy-start.1) | copy-done | bytes 131096
  43.5 1.0 %copy-done.5 = bf16[768,256]{1,0:T(8,128)(2,1)S(1)} copy-done((bf16[768,256]{1,0:T(8,128)(2,1)S(1)}, bf16[768,256]{1,0:T(8,128)(2,1)}, u32[]{:S(2)}) %copy-start.5) | copy-done | bytes 393240
  44.5 0.9 %copy-done.7 = bf16[128,768]{1,0:T(8,128)(2,1)S(1)} copy-done((bf16[128,768]{1,0:T(8,128)(2,1)S(1)}, bf16[128,768]{1,0:T(8,128)(2,1)}, u32[]{:S(2)}) %copy-start.7) | copy-done | bytes 196632
  45.4 0.9 copy-done.9
  46.3 21.6 %step0.1 = (f32[64,896]{1,0:T(8,128)S(1)}, f32[64,896]{1,0:T(8,128)S(1)}, f32[64,896]{1,0:T(8,128)S(1)}) custom-call(s32[16]{0:T(128)S(1)} %copy-done.12, s32[16]{0:T(128)S(1)} %copy-done.13, f32[16,32,64]{2,1,0:T(8,128)S(1)} %copy-done.1, f32[16,32,64]{2,1,0:T(8,128)S(1)} %collective-permute-done.6.refs_3_, f32[3,32,64]{2,1,0:T(8,128)S(1)} %copy-done.2, ...), custom_call_target="tpu_custom_call" | custom-call | flops 2919235584 | bytes 786432 | tf_op jit(solution)/shard_map/step0/pallas_call | solution.py:414
  68.0 2.2 %all-gather = f32[128,896]{1,0:T(8,128)S(1)} all-gather(f32[64,896]{1,0:T(8,128)S(1)} %get-tuple-element.31), channel_id=2, replica_groups=mesh['queue'=16,'tok'=2] {'tok'}, dimensions={0}, use_global_device_ids=true | all-gather | bytes 688128 | tf_op jit(solution)/shard_map/all_gather | solution.py:437
  70.2 12.8 %step1.1 = (f32[64,512]{1,0:T(8,128)S(1)}, f32[64,512]{1,0:T(8,128)S(1)}, f32[64,512]{1,0:T(8,128)S(1)}, f32[32,64]{1,0:T(8,128)S(1)}) custom-call(s32[16]{0:T(128)S(1)} %copy-done.12, s32[16]{0:T(128)S(1)} %copy-done.13, f32[2,64,896]{2,1,0:T(8,128)S(1)} %bitcast.4, f32[64,896]{1,0:T(8,128)S(1)} %get-tuple-element.32.refs_3_, ...), custom_call_target="tpu_custom_call" | custom-call | flops 1862270976 | bytes 786432 | tf_op jit(solution)/shard_map/step1/pallas_call | solution.py:414
  83.0 2.0 %all-gather.1 = f32[128,512]{1,0:T(8,128)S(1)} all-gather(f32[64,512]{1,0:T(8,128)S(1)} %get-tuple-element.34), channel_id=3, replica_groups=mesh['queue'=16,'tok'=2] {'tok'}, dimensions={0}, use_global_device_ids=true | all-gather | bytes 393216 | tf_op jit(solution)/shard_map/all_gather | solution.py:437
  85.1 3.8 %step2.1 = (f32[64,128]{1,0:T(8,128)S(1)}, f32[64,128]{1,0:T(8,128)S(1)}, f32[64,128]{1,0:T(8,128)S(1)}, f32[32,64]{1,0:T(8,128)S(1)}) custom-call(s32[16]{0:T(128)S(1)} %copy-done.12, s32[16]{0:T(128)S(1)} %copy-done.13, f32[2,64,512]{2,1,0:T(8,128)S(1)} %bitcast.5, f32[64,512]{1,0:T(8,128)S(1)} %get-tuple-element.35.refs_3_, ...), custom_call_target="tpu_custom_call" | custom-call | flops 805306368 | bytes 786432 | tf_op jit(solution)/shard_map/step2/pallas_call | solution.py:414
  88.8 1.9 %all-gather.2 = f32[128,128]{1,0:T(8,128)S(1)} all-gather(f32[64,128]{1,0:T(8,128)S(1)} %get-tuple-element.37), channel_id=4, replica_groups=mesh['queue'=16,'tok'=2] {'tok'}, dimensions={0}, use_global_device_ids=true | all-gather | bytes 98304 | tf_op jit(solution)/shard_map/all_gather | solution.py:437
  90.7 0.7 last.1
  (50 shorter events, 1.2 us)
Async XLA Ops:
  1.4 5.0 %collective-permute-start = (f32[1,32,64]{2,1,0:T(8,128)S(1)}, f32[1,32,64]{2,1,0:T(8,128)S(1)}, u32[]{:S(2)}, u32[]{:S(2)}) collective-permute-start(f32[1,32,64]{2,1,0:T(8,128)S(1)} %get-tuple-element.43), channel_id=1, source_target_pairs={{0,2},{2,0},{4,6},{6,4},{8,10},{10,8},{12,14},{14,12},{16,18},{18,... | collective-permute-start | bytes 24584 | tf_op jit(solution)/shard_map/ppermute | solution.py:319
  4.3 3.7 %collective-permute-start.1 = (f32[1,32,64]{2,1,0:T(8,128)S(1)}, f32[1,32,64]{2,1,0:T(8,128)S(1)}, u32[]{:S(2)}, u32[]{:S(2)}) collective-permute-start(f32[1,32,64]{2,1,0:T(8,128)S(1)} %get-tuple-element.43), channel_id=1, source_target_pairs={{0,4},{2,6},{4,0},{6,2},{8,12},{10,14},{12,8},{14,10},{16,20},{18,... | collective-permute-start | bytes 24584 | tf_op jit(solution)/shard_map/ppermute | solution.py:319
  5.8 4.6 %collective-permute-start.2 = (f32[1,32,64]{2,1,0:T(8,128)S(1)}, f32[1,32,64]{2,1,0:T(8,128)S(1)}, u32[]{:S(2)}, u32[]{:S(2)}) collective-permute-start(f32[1,32,64]{2,1,0:T(8,128)S(1)} %get-tuple-element.43), channel_id=1, source_target_pairs={{0,6},{2,4},{4,2},{6,0},{8,14},{10,12},{12,10},{14,8},{16,22},{18,... | collective-permute-start | bytes 24584 | tf_op jit(solution)/shard_map/ppermute | solution.py:319
  5.8 24.5 %collective-permute-start.7 = (bf16[64,1536]{1,0:T(8,128)(2,1)}, bf16[64,1536]{1,0:T(8,128)(2,1)S(1)}, u32[]{:S(2)}, u32[]{:S(2)}) collective-permute-start(bf16[64,1536]{1,0:T(8,128)(2,1)} %refs_0_.4), channel_id=1, source_target_pairs={{0,1},{1,0},{2,3},{3,2},{4,5},{5,4},{6,7},{7,6},{8,9},{9,8},{10,11... | collective-permute-start | bytes 589832 | tf_op jit(solution)/shard_map/ppermute | solution.py:322
  5.8 24.4 %collective-permute-start.8 = (bf16[19,1536]{1,0:T(8,128)(2,1)}, bf16[19,1536]{1,0:T(8,128)(2,1)S(1)}, u32[]{:S(2)}, u32[]{:S(2)}) collective-permute-start(bf16[19,1536]{1,0:T(8,128)(2,1)} %refs_1_.4), channel_id=1, source_target_pairs={{0,1},{1,0},{2,3},{3,2},{4,5},{5,4},{6,7},{7,6},{8,9},{9,8},{10,11... | collective-permute-start | bytes 175112 | tf_op jit(solution)/shard_map/ppermute | solution.py:322
  6.4 24.0 %collective-permute-start.9 = (bf16[64,1536]{1,0:T(8,128)(2,1)}, bf16[64,1536]{1,0:T(8,128)(2,1)S(1)}, u32[]{:S(2)}, u32[]{:S(2)}) collective-permute-start(bf16[64,1536]{1,0:T(8,128)(2,1)} %bitcast.7), channel_id=1, source_target_pairs={{0,1},{1,0},{2,3},{3,2},{4,5},{5,4},{6,7},{7,6},{8,9},{9,8},{10,11... | collective-permute-start | bytes 589832 | tf_op jit(solution)/shard_map/ppermute | solution.py:322
  10.5 19.8 %copy-start.17 = (f32[4,32,64]{2,1,0:T(8,128)}, f32[4,32,64]{2,1,0:T(8,128)S(1)}, u32[]{:S(2)}) copy-start(f32[4,32,64]{2,1,0:T(8,128)S(1)} %pad_maximum_fusion.refs_9_) | copy-start | bytes 98308
  10.5 4.3 %collective-permute-start.3 = (f32[4,32,64]{2,1,0:T(8,128)S(1)}, f32[4,32,64]{2,1,0:T(8,128)S(1)}, u32[]{:S(2)}, u32[]{:S(2)}) collective-permute-start(f32[4,32,64]{2,1,0:T(8,128)S(1)} %pad_maximum_fusion.refs_9_), channel_id=1, source_target_pairs={{0,8},{2,10},{4,12},{6,14},{8,0},{10,2},{12,4},{14,6},{16,24},{18,... | collective-permute-start | bytes 98312 | tf_op jit(solution)/shard_map/ppermute | solution.py:319
  12.1 6.6 %collective-permute-start.4 = (f32[4,32,64]{2,1,0:T(8,128)S(1)}, f32[4,32,64]{2,1,0:T(8,128)S(1)}, u32[]{:S(2)}, u32[]{:S(2)}) collective-permute-start(f32[4,32,64]{2,1,0:T(8,128)S(1)} %pad_maximum_fusion.refs_9_), channel_id=1, source_target_pairs={{0,16},{2,18},{4,20},{6,22},{8,24},{10,26},{12,28},{14,30},{16,0},... | collective-permute-start | bytes 98312 | tf_op jit(solution)/shard_map/ppermute | solution.py:319
  14.8 6.1 %collective-permute-start.5 = (f32[4,32,64]{2,1,0:T(8,128)S(1)}, f32[4,32,64]{2,1,0:T(8,128)S(1)}, u32[]{:S(2)}, u32[]{:S(2)}) collective-permute-start(f32[4,32,64]{2,1,0:T(8,128)S(1)} %pad_maximum_fusion.refs_9_), channel_id=1, source_target_pairs={{0,24},{2,26},{4,28},{6,30},{8,16},{10,18},{12,20},{14,22},{16,8},... | collective-permute-start | bytes 98312 | tf_op jit(solution)/shard_map/ppermute | solution.py:319
  21.0 15.8 %copy-start = (f32[16,32,64]{2,1,0:T(8,128)}, f32[16,32,64]{2,1,0:T(8,128)S(1)}, u32[]{:S(2)}) copy-start(f32[16,32,64]{2,1,0:T(8,128)S(1)} %constant_dynamic-update-slice_fusion.refs_9_.refs_2_) | copy-start | bytes 393220
  21.0 21.5 %collective-permute-start.6 = (f32[16,32,64]{2,1,0:T(8,128)S(1)}, f32[16,32,64]{2,1,0:T(8,128)S(1)}, u32[]{:S(2)}, u32[]{:S(2)}) collective-permute-start(f32[16,32,64]{2,1,0:T(8,128)S(1)} %constant_dynamic-update-slice_fusion.refs_9_.refs_2_), channel_id=1, source_target_pairs={{0,1},{1,0},{2,3},{3,2},{4,5},{5,4},{6,7},{7,6},{8,9},{9,8},{10,11... | collective-permute-start | bytes 393224 | tf_op jit(solution)/shard_map/ppermute | solution.py:322
  36.7 5.7 %copy-start.2 = (f32[3,32,64]{2,1,0:T(8,128)S(1)}, f32[3,32,64]{2,1,0:T(8,128)}, u32[]{:S(2)}) copy-start(f32[3,32,64]{2,1,0:T(8,128)} %refs_5_.4) | copy-start | bytes 73732
  36.8 5.7 %copy-start.3 = (bf16[768,256]{1,0:T(8,128)(2,1)S(1)}, bf16[768,256]{1,0:T(8,128)(2,1)}, u32[]{:S(2)}) copy-start(bf16[768,256]{1,0:T(8,128)(2,1)} %get-tuple-element.26.refs_6_.refs_7_) | copy-start | bytes 1179652
  36.8 5.7 %copy-start.4 = (bf16[256,768]{1,0:T(8,128)(2,1)S(1)}, bf16[256,768]{1,0:T(8,128)(2,1)}, u32[]{:S(2)}) copy-start(bf16[256,768]{1,0:T(8,128)(2,1)} %get-tuple-element.27.refs_7_.refs_8_) | copy-start | bytes 1179652
  36.8 5.7 %copy-start.11 = (f32[2,768]{1,0:T(2,128)S(1)}, f32[2,768]{1,0:T(2,128)}, u32[]{:S(2)}) copy-start(f32[2,768]{1,0:T(2,128)} %refs_5_.5) | copy-start | bytes 18436
  36.8 5.7 %copy-start.12 = (s32[16]{0:T(128)S(1)}, s32[16]{0:T(128)}, u32[]{:S(2)}) copy-start(s32[16]{0:T(128)} %refs_0_.7) | copy-start | bytes 196
  36.8 5.7 %copy-start.13 = (s32[16]{0:T(128)S(1)}, s32[16]{0:T(128)}, u32[]{:S(2)}) copy-start(s32[16]{0:T(128)} %refs_1_.7) | copy-start | bytes 196
  42.5 1.0 %copy-start.1 = (f32[16,32,64]{2,1,0:T(8,128)S(1)}, f32[16,32,64]{2,1,0:T(8,128)}, u32[]{:S(2)}) copy-start(f32[16,32,64]{2,1,0:T(8,128)} %copy-done) | copy-start | bytes 393220
  43.5 1.0 %copy-start.5 = (bf16[768,256]{1,0:T(8,128)(2,1)S(1)}, bf16[768,256]{1,0:T(8,128)(2,1)}, u32[]{:S(2)}) copy-start(bf16[768,256]{1,0:T(8,128)(2,1)} %get-tuple-element.28.refs_8_.refs_9_) | copy-start | bytes 1179652
  44.5 0.9 %copy-start.7 = (bf16[128,768]{1,0:T(8,128)(2,1)S(1)}, bf16[128,768]{1,0:T(8,128)(2,1)}, u32[]{:S(2)}) copy-start(bf16[128,768]{1,0:T(8,128)(2,1)} %get-tuple-element.29.refs_9_.refs_10_) | copy-start | bytes 589828
  46.3 23.9 %copy-start.6 = (bf16[768,256]{1,0:T(8,128)(2,1)S(1)}, bf16[768,256]{1,0:T(8,128)(2,1)}, u32[]{:S(2)}) copy-start(bf16[768,256]{1,0:T(8,128)(2,1)} %get-tuple-element.28.refs_8_.refs_9_) | copy-start | bytes 1179652
  46.3 23.9 %copy-start.8 = (bf16[128,768]{1,0:T(8,128)(2,1)S(1)}, bf16[128,768]{1,0:T(8,128)(2,1)}, u32[]{:S(2)}) copy-start(bf16[128,768]{1,0:T(8,128)(2,1)} %get-tuple-element.29.refs_9_.refs_10_) | copy-start | bytes 589828
  46.3 23.9 %copy-start.10 = (bf16[192,256]{1,0:T(8,128)(2,1)S(1)}, bf16[192,256]{1,0:T(8,128)(2,1)}, u32[]{:S(2)}) copy-start(bf16[192,256]{1,0:T(8,128)(2,1)} %get-tuple-element.30.refs_10_.refs_11_) | copy-start | bytes 294916
  (4 other events, 2.9 us)

commit v4 on v3

--- a/solution.py
+++ b/solution.py
@@ -56,57 +56,41 @@
 def stack_rows(base, embed_ref, level_ref):
     filler = base - embed_ref.shape[0] - level_ref.shape[0]
     rows = [embed_ref[...].astype(F32), level_ref[...].astype(F32)]
-    return jnp.concatenate(rows + [jnp.zeros((filler, embed_ref.shape[1]), F32)], axis=0)
-
-
-def turned(base, embed_ref, level_ref, vel_ref):
-    left = stack_rows(base, embed_ref, level_ref)
-    return left.astype(BF16), left.T.astype(BF16), vel_ref[...].astype(F32).T.astype(BF16)
-
-
-def own_weights_kernel(rows, base, *refs):
-    qkv_hbm, out_hbm, acc_ref, wo_ref, gram_ref, gv_ref, buf, sems = refs[3:]
-    per = out_hbm.shape[0] // rows
-    copies = start_chunks(rows, range(4 * per), (0,), qkv_hbm, out_hbm, buf, sems)
-    left, right, vel = turned(base, *refs[:3])
-    gram_ref[...] = dot(left, right)
-    gv_ref[...] = dot(refs[2][...], right)
-    for chunk in range(4 * per):
-        copies[chunk].wait()
-        if chunk < 3 * per:
-            acc_ref[chunk * rows : (chunk + 1) * rows, :] = dot(buf[0, chunk], right)
-        else:
-            at = (chunk - 3 * per) * rows
-            wo_ref[at : at + rows, :] = dot(buf[0, chunk], vel)
-
-
-def other_weights_kernel(rows, base, count, second, *refs):
-    tables, refs = refs[: 3 * (count - 1)], refs[3 * (count - 1) :]
-    acc_ref, wo_acc, gram_acc, gv_acc, qkv_hbm, out_hbm, _ = refs[:7]
-    outs, buf, sems = refs[7:-2], refs[-2], refs[-1]
-    per = out_hbm.shape[0] // rows
+    rows = jnp.concatenate(rows + [jnp.zeros((filler, embed_ref.shape[1]), F32)], axis=0)
+    return rows.astype(BF16)
+
+
+def weights_kernel(rows, base, count, second, *refs):
+    shares = (0,) if count == 0 else tuple(range(1, count))
+    tables, refs = refs[: 3 * len(shares)], refs[3 * len(shares) :]
+    sums = ()
+    if count:
+        sums, refs = refs[: 3 if second else 1], refs[3 if second else 1 :]
+    qkv_hbm, out_hbm = refs[:2]
+    outs, buf, sems = refs[2:-2], refs[-2], refs[-1]
+    width = out_hbm.shape[0]
+    per = width // rows
     chunks = range(2 * per, 4 * per) if second else range(2 * per)
-    copies = start_chunks(rows, chunks, range(1, count), qkv_hbm, out_hbm, buf, sems)
-    rights = [turned(base, *tables[3 * at : 3 * at + 3]) for at in range(count - 1)]
+    copies = start_chunks(rows, chunks, shares, qkv_hbm, out_hbm, buf, sems)
+    lefts = [stack_rows(base, *tables[3 * at : 3 * at + 2]) for at in range(len(shares))]
+    vels = [tables[3 * at + 2][...] for at in range(len(shares))]
     if second:
-        gram, gv = gram_acc[...], gv_acc[...]
-        for at, (left, right, _) in enumerate(rights):
-            gram = gram + dot(left, right)
-            gv = gv + dot(tables[3 * at + 2][...], right)
-        outs[2][:base] = halves(gram, 1)
-        outs[2][base:] = halves(gv, 1)
+        gram = sum(dot_nt(jnp.concatenate([left, vel], axis=0), left) for left, vel in zip(lefts, vels))
+        outs[2][...] = halves(sums[2][...] + gram, 1) if count else gram
     for place, chunk in enumerate(chunks):
-        for at in range(count - 1):
-            copies[place * (count - 1) + at].wait()
-        kind = chunk // per
-        where = pl.ds((chunk % per) * rows, rows)
-        if kind < 3:
-            total = acc_ref[chunk * rows : (chunk + 1) * rows, :]
-        else:
-            total = wo_acc[where, :]
-        for at, (_, right, vel) in enumerate(rights):
-            total = total + dot(buf[at, place], right if kind < 3 else vel)
-        if kind % 2:
+        for at in range(len(shares)):
+            copies[place * len(shares) + at].wait()
+        last = chunk // per == 3
+        total = sum(dot_nt(buf[at, place], vels[at] if last else lefts[at]) for at in range(len(shares)))
+        spot = slice(place * rows, (place + 1) * rows)
+        if last:
+            spot = slice((place - per) * rows, (place - per + 1) * rows)
+        if count == 0:
+            outs[1 if last else 0][spot, :] = total
+            continue
+        total = total + sums[1 if last else 0][spot, :]
+        where = slice((chunk % per) * rows, (chunk % per + 1) * rows)
+        if chunk // per % 2:
             outs[1][:, where] = halves(total.T, 0)
         else:
             outs[0][where, :] = halves(total, 1)
@@ -210,50 +194,75 @@
     spread = jnp.sum(raw * raw, axis=1, keepdims=True) * (1.0 / HD)
     qbuf[...] = (raw * lax.rsqrt(spread + EPS * mean_q)[:, :, :]).reshape(width, query_lanes).astype(BF16)
 
-    def block(b, carry):
+    bound = HD * jnp.max(gain, axis=1, keepdims=True)
+    upper = lax.broadcasted_iota(jnp.int32, (2 * HD, LANES), 0) < HD
+    lane = lax.broadcasted_iota(jnp.int32, (1, 2 * LANES), 1)
+    within = lax.rem(lane, LANES) // tok
+
+    def place(b):
         lead = (b * LANES) // tok
         keys = pl.ds(pl.multiple_of(lead * tok, LANES), window)
-        lanes = pl.ds(pl.multiple_of(b * LANES, LANES), LANES)
-        lane = lax.broadcasted_iota(jnp.int32, (1, 2 * LANES), 1)
-        within = lax.rem(lane, LANES) // tok
-        bias_rows = []
-        reach = []
-        for j in range(query_block):
-            frame = first_key + HALO + lead + j
-            reach.append(reach_ref[jnp.clip(frame, 0, frames - 1)])
+        return lead, keys, pl.ds(pl.multiple_of(b * LANES, LANES), LANES)
+
+    def biases(lead, shift):
+        rows = []
         for k in range(2 * HALO + query_block):
             target = first_key + lead + k
             inside = (target >= 0) & (target < frames)
-            bias = jnp.zeros((1, 2 * LANES), F32)
+            row = jnp.zeros((1, 2 * LANES), F32)
             for j in range(query_block):
-                counted = inside & (abs(k - HALO - j) <= reach[j])
-                value = jnp.where(counted, 0.0, -1e30)
-                bias = jnp.where(within == j, value, bias) if query_block > 1 else bias + value
-            bias_rows.append(bias)
+                frame = first_key + HALO + lead + j
+                reach = reach_ref[jnp.clip(frame, 0, frames - 1)]
+                unused = (frame < 0) | (frame >= frames)
+                counted = (inside & (abs(k - HALO - j) <= reach)) | unused
+                row = jnp.where(within == j, jnp.where(counted, 0.0, -1e30), row)
+            rows.append(row - shift)
+        return rows
+
+    def scores(keys, lanes, cols, rows):
+        query = qbuf[cols, lanes]
+        zero = jnp.zeros_like(query)
+        query = jnp.concatenate([jnp.where(upper, query, zero), jnp.where(upper, zero, query)], axis=1)
+        score = dot(kbuf[keys, cols], query)
+        return jnp.concatenate([score[k * tok : (k + 1) * tok] + rows[k] for k in range(len(rows))], axis=0)
+
+    def mix(keys, lanes, cols, weight):
         ones = jnp.ones((16, window), BF16)
-        upper = lax.broadcasted_iota(jnp.int32, (2 * HD, LANES), 0) < HD
+        mixed = dot(jnp.concatenate([vbuf[cols, keys], ones], axis=0), weight.astype(BF16))
+        total = mixed[2 * HD : 2 * HD + 1, :]
+        scale = 1.0 / total
+        top = mixed[:HD, :LANES] * scale[:, :LANES]
+        bottom = mixed[HD : 2 * HD, LANES:] * scale[:, LANES:]
+        att[cols, lanes] = jnp.concatenate([top, bottom], axis=0).astype(BF16)
+        return total
+
+    def block(b, least):
+        lead, keys, lanes = place(b)
+        rows = biases(lead, bound)
+        held = None
         for pair in range(heads // 2):
             cols = slice(pair * 2 * HD, (pair + 1) * 2 * HD)
-            query = qbuf[cols, lanes]
-            zero = jnp.zeros_like(query)
-            query = jnp.concatenate([jnp.where(upper, query, zero), jnp.where(upper, zero, query)], axis=1)
-            score = dot(kbuf[keys, cols], query)
-            score = jnp.concatenate(
-                [score[k * tok : (k + 1) * tok] + bias_rows[k] for k in range(len(bias_rows))], axis=0
-            )
-            weight = jnp.exp2(score - jnp.max(score, axis=0, keepdims=True)).astype(BF16)
-            mixed = dot(jnp.concatenate([vbuf[cols, keys], ones], axis=0), weight)
-            total = 1.0 / mixed[2 * HD : 2 * HD + 1, :]
-            top = mixed[:HD, :LANES] * total[:, :LANES]
-            bottom = mixed[HD : 2 * HD, LANES:] * total[:, LANES:]
-            att[cols, lanes] = jnp.concatenate([top, bottom], axis=0).astype(BF16)
+            weight = jnp.exp2(scores(keys, lanes, cols, rows)).astype(BF16)
+            if held is not None:
+                least = jnp.minimum(least, mix(keys, lanes, *held))
+            held = (cols, weight)
+        return jnp.minimum(least, mix(keys, lanes, *held))
+
+    def exact_block(at, carry):
+        lead, keys, lanes = place(at // (heads // 2))
+        cols = pl.ds(pl.multiple_of(lax.rem(at, heads // 2) * 2 * HD, 2 * HD), 2 * HD)
+        score = scores(keys, lanes, cols, biases(lead, 0.0))
+        mix(keys, lanes, cols, jnp.exp2(score - jnp.max(score, axis=0, keepdims=True)))
         return carry
 
     blocks = query_lanes // LANES
-    if blocks == 1:
-        block(0, 0)
-    else:
-        lax.fori_loop(0, blocks, block, 0)
+    least = jnp.ones((1, 2 * LANES), F32)
+    least = block(0, least) if blocks == 1 else lax.fori_loop(0, blocks, block, least)
+
+    @pl.when(jnp.min(least) < 1e-25)
+    def _():
+        lax.fori_loop(0, blocks * (heads // 2), exact_block, 0)
+
     mixed = dot(wo_ref[...], att[...])
     partial = mixed[:channels] + mixed[channels:]
     if step < STEPS - 1:
@@ -321,73 +330,67 @@
     def from_ahead(value, distance):
         return lax.ppermute(value, "tok", [(source, (source - distance) % parts) for source in range(parts)])
 
-    state = jnp.where(position == frames - 1, fresh_noise[0], latent[0])[None]
-    rounds = []
-    reached = 1
-    while reached < frames:
-        group = min(4, frames // reached)
-        moved = [swapped(state, "queue", reached * d) for d in range(1, group)]
-        state = jnp.concatenate([state] + moved, axis=0)
-        rounds.append(state)
-        reached *= group
-    latents = [state] + [from_ahead(state, d) for d in range(1, parts)]
-
     share = depth // parts
     table = (embed_weight, level_embed, vel_weight.T)
     tables = [from_ahead(piece, d) for d in range(1, parts) for piece in table]
-
     rows = 384 if width % 384 == 0 else 256
-    chunks = 4 * width // rows
-    limit = pltpu.CompilerParams(vmem_limit_bytes=60 * 2**20)
-
-    def estimate(share_count):
-        return pl.CostEstimate(
-            flops=int(8 * base * width * share * share_count),
-            bytes_accessed=int(8 * width * share * share_count),
-            transcendentals=0,
-        )
-
-    sums = pl.pallas_call(
-        functools.partial(own_weights_kernel, rows, base),
-        out_shape=(
-            shape((3 * width, base), F32),
-            shape((width, channels), F32),
-            shape((base, base), F32),
-            shape((channels, base), F32),
-        ),
-        in_specs=[vmem] * 3 + [hbm] * 2,
-        out_specs=(vmem,) * 4,
-        scratch_shapes=[
-            pltpu.VMEM((1, chunks, rows, share), BF16),
-            pltpu.SemaphoreType.DMA((1, chunks)),
-        ],
-        compiler_params=limit,
-        cost_estimate=estimate(1),
-        name="own_weights",
-    )(*table, qkv_weight, out_weight)
-
-    def other_weights(second, after):
-        outs = [shape((width, 2 * base), BF16)]
-        if second:
-            outs += [shape((2 * channels, width), BF16), shape((base + channels, 2 * base), BF16)]
+    chunks = 2 * width // rows
+    qkv_weight = pltpu.with_memory_space_constraint(qkv_weight, pltpu.HBM)
+    out_weight = pltpu.with_memory_space_constraint(out_weight, pltpu.HBM)
+
+    def weights(count, second, *operands):
+        shares = max(1, count - 1)
+        if count == 0 and second:
+            outs = [shape((width, base), F32), shape((width, channels), F32), shape((base + channels, base), F32)]
+        elif count == 0:
+            outs = [shape((2 * width, base), F32)]
+        elif second:
+            outs = [
+                shape((width, 2 * base), BF16),
+                shape((2 * channels, width), BF16),
+                shape((base + channels, 2 * base), BF16),
+            ]
         else:
-            outs += [shape((2 * base, width), BF16)]
+            outs = [shape((width, 2 * base), BF16), shape((2 * base, width), BF16)]
         return pl.pallas_call(
-            functools.partial(other_weights_kernel, rows, base, parts, second),
+            functools.partial(weights_kernel, rows, base, count, second),
             out_shape=tuple(outs),
-            in_specs=[vmem] * (3 * (parts - 1) + 4) + [hbm] * 2 + [pl.BlockSpec(memory_space=pl.ANY)],
+            in_specs=[vmem] * len(operands) + [hbm] * 2,
             out_specs=(vmem,) * len(outs),
             scratch_shapes=[
-                pltpu.VMEM((parts - 1, chunks // 2, rows, share), BF16),
-                pltpu.SemaphoreType.DMA((parts - 1, chunks // 2)),
+                pltpu.VMEM((shares, chunks, rows, share), BF16),
+                pltpu.SemaphoreType.DMA((shares, chunks)),
             ],
-            compiler_params=limit,
-            cost_estimate=estimate(0.5 * (parts - 1)),
-            name="other_weights",
-        )(*tables, *sums, qkv_weight, out_weight, after)
-
-    mq, mk = other_weights(False, rounds[0])
-    mv, wo, gram = other_weights(True, rounds[-1])
+            compiler_params=pltpu.CompilerParams(vmem_limit_bytes=24 * 2**20),
+            cost_estimate=pl.CostEstimate(
+                flops=4 * base * width * share * shares,
+                bytes_accessed=4 * width * share * shares,
+                transcendentals=0,
+            ),
+            name="weights",
+        )(*operands, qkv_weight, out_weight)
+
+    state = jnp.where(position == frames - 1, fresh_noise[0], latent[0])[None]
+    work = [
+        lambda: weights(0, False, *table),
+        lambda: weights(0, True, *table),
+        lambda: weights(parts, False, *tables, *done[0]),
+        lambda: weights(parts, True, *tables, *done[1]),
+    ]
+    done = []
+    reached = 1
+    while reached < frames:
+        moved = swapped(state, "queue", reached)
+        if len(done) < len(work):
+            moved, result = lax.optimization_barrier((moved, work[len(done)]()))
+            done.append(result)
+        state = jnp.concatenate([state, moved], axis=0)
+        reached *= 2
+    while len(done) < len(work):
+        done.append(work[len(done)]())
+    latents = [state] + [from_ahead(state, d) for d in range(1, parts)]
+    mq, mk = done[2]
+    mv, wo, gram = done[3]
 
     query_block = max(1, LANES // tok)
     owned = []

time: 91.8 us -> 104 us (1.13)
  Pallas kernels: 59.5 us -> 79.4 us
  starting transfers between devices: 12.8 us -> 9.54 us
  waiting for transfers between devices: 6.78 us -> 4.47 us
  local copies, waits for them, and re-layouts: 4.56 us -> 2.78 us
    pallas_call x3, Pallas kernels: 38.2 us -> 60.9 us  [body(): pl.pallas_call(functools.partial(step_kernel, step, cfg), out_shape=tuple...]
    ppermute x6 -> x4, waiting for transfers between devices: 6.77 us -> 2.94 us  [swapped(): lax.ppermute(value, axis, [(source, source ^ distance) for source in rang...]
    ppermute x6 -> x4, starting transfers between devices: 12.2 us -> 8.44 us  [swapped(): lax.ppermute(value, axis, [(source, source ^ distance) for source in rang...]
    pallas_call x3 -> x4, Pallas kernels: 20.5 us -> 17.8 us  [weights(): pl.pallas_call(functools.partial(weights_kernel, rows, base, count, secon...]
    unnamed x41 -> x17, local copies, waits for them, and re-layouts: 4.55 us -> 2.77 us
    ppermute x4, waiting for transfers between devices: 0.01 us -> 1.53 us  [from_ahead(): lax.ppermute(value, 'tok', [(source, (source - distance) % parts) for sou...]
  transfers between devices with their start and end apart: 10 -> 8, of which waited for: 5 -> 3; matrix products, arithmetic and copies ran while one was open for 0% -> 1% of each run, Pallas kernels for 22% -> 17%
where the time goes in v4:
time: 104 us
  Pallas kernels  79.4 us (76%)
  starting transfers between devices  9.54 us (9%)
  blocking collectives  6.16 us (6%)
  waiting for transfers between devices  4.47 us (4%)
  local copies, waits for them, and re-layouts  2.78 us (3%)
    pallas_call x3, Pallas kernels, body(): pl.pallas_call(functools.partial(step_kernel, step, cfg), out_shape=tuple...  60.9 us
    pallas_call x4, Pallas kernels, weights(): pl.pallas_call(functools.partial(weights_kernel, rows, base, count, secon...  17.8 us
    ppermute x4, starting transfers between devices, swapped(): lax.ppermute(value, axis, [(source, source ^ distance) for source in rang...  8.44 us
    all_gather x3, blocking collectives, body(): gathered = lax.all_gather(part, 'tok', axis=0, tiled=False)  6.16 us
    ppermute x4, waiting for transfers between devices, swapped(): lax.ppermute(value, axis, [(source, source ^ distance) for source in rang...  2.94 us
    unnamed x17, local copies, waits for them, and re-layouts  2.77 us
  transfers between devices with their start and end apart: 8, of which 3 were waited for; matrix products, arithmetic and copies ran while one was open for 1% of the time, Pallas kernels for 17%

profile of v4, /device:TPU:0, one launch (start us, length us, event | category | flops | bytes accessed | tf_op | source)
XLA Modules:
  0.0 103.9 jit_solution(5645138246410290660)
XLA Ops:
  0.6 0.5 collective-permute-start.4
  1.2 0.4 collective-permute-start.3
  1.7 0.7 constant_dynamic-update-slice_fusion.4
  2.4 2.6 %collective-permute-start = (f32[1,32,64]{2,1,0:T(8,128)S(1)}, f32[1,32,64]{2,1,0:T(8,128)S(1)}, u32[]{:S(2)}, u32[]{:S(2)}) collective-permute-start(f32[1,32,64]{2,1,0:T(8,128)S(1)} %get-tuple-element.67), channel_id=1, source_target_pairs={{0,2},{2,0},{4,6},{6,4},{8,10},{10,8},{12,14},{14,12},{16,18},{18,... | collective-permute-start | bytes 24584 | tf_op jit(solution)/shard_map/ppermute | solution.py:328
  5.0 0.9 copy-done
  5.9 0.9 copy-done.1
  6.8 0.9 copy-done.2
  7.7 4.3 %weights.4.refs_3_ = f32[1536,128]{1,0:T(8,128)S(1)} custom-call(bf16[64,1536]{1,0:T(8,128)(2,1)S(1)} %copy-done.1, bf16[19,1536]{1,0:T(8,128)(2,1)S(1)} %copy-done.2, bf16[64,1536]{1,0:T(8,128)(2,1)S(1)} %bitcast.5, bf16[3,768,3072]{2,1,0:T(8,128)(2,1)} %refs_6_.2, bf16[768,3072]{1,0:T(8,128)(2,1)} %refs_7_.1), custom_call_target="tpu_custom_call" | custom-call | flops 603979776 | bytes 4718592 | tf_op jit(solution)/shard_map/weights/pallas_call | solution.py:355
  12.0 4.5 %weights.5 = (f32[768,128]{1,0:T(8,128)S(1)}, f32[768,64]{1,0:T(8,128)S(1)}, f32[192,128]{1,0:T(8,128)S(1)}) custom-call(bf16[64,1536]{1,0:T(8,128)(2,1)S(1)} %copy-done.1, bf16[19,1536]{1,0:T(8,128)(2,1)S(1)} %copy-done.2, bf16[64,1536]{1,0:T(8,128)(2,1)S(1)} %bitcast.6, bf16[3,768,3072]{2,1,0:T(8,128)(2,1)} %refs_6_.2, bf16[768,3072]{1,0:T(8,128)(2,1)} %refs_7_.1), custom_call_target="tpu_custom_call" | custom-call | flops 603979776 | bytes 4718592 | tf_op jit(solution)/shard_map/weights/pallas_call | solution.py:355
  16.5 1.6 %collective-permute-start.1 = (f32[2,32,64]{2,1,0:T(8,128)S(1)}, f32[2,32,64]{2,1,0:T(8,128)S(1)}, u32[]{:S(2)}, u32[]{:S(2)}) collective-permute-start(f32[2,32,64]{2,1,0:T(8,128)S(1)} %pad_maximum_fusion.2), channel_id=1, source_target_pairs={{0,4},{2,6},{4,0},{6,2},{8,12},{10,14},{12,8},{14,10},{16,20},{18,... | collective-permute-start | bytes 49160 | tf_op jit(solution)/shard_map/ppermute | solution.py:328
  18.1 2.4 %collective-permute-done.1 = f32[2,32,64]{2,1,0:T(8,128)S(1)} collective-permute-done((f32[2,32,64]{2,1,0:T(8,128)S(1)}, f32[2,32,64]{2,1,0:T(8,128)S(1)}, u32[]{:S(2)}, u32[]{:S(2)}) %collective-permute-start.1) | collective-permute-done | bytes 16416 | tf_op jit(solution)/shard_map/ppermute | solution.py:328
  20.5 1.6 %collective-permute-start.2 = (f32[4,32,64]{2,1,0:T(8,128)S(1)}, f32[4,32,64]{2,1,0:T(8,128)S(1)}, u32[]{:S(2)}, u32[]{:S(2)}) collective-permute-start(f32[4,32,64]{2,1,0:T(8,128)S(1)} %pad_maximum_fusion.1), channel_id=1, source_target_pairs={{0,8},{2,10},{4,12},{6,14},{8,0},{10,2},{12,4},{14,6},{16,24},{18,... | collective-permute-start | bytes 98312 | tf_op jit(solution)/shard_map/ppermute | solution.py:328
  22.1 4.5 %weights.6 = (bf16[768,256]{1,0:T(8,128)(2,1)S(1)}, bf16[256,768]{1,0:T(8,128)(2,1)S(1)}) custom-call(bf16[64,1536]{1,0:T(8,128)(2,1)S(1)} %collective-permute-done.3.refs_0_, bf16[19,1536]{1,0:T(8,128)(2,1)S(1)} %collective-permute-done.4.refs_1_, bf16[64,1536]{1,0:T(8,128)(2,1)S(1)} %collective-permute-done.5.refs_2_, f32[1536,128]{1,0:T(8,128)S(1)} %weights.4.refs_3_, ...), custom_call_target="tpu_custom_call" | custom-call | flops 603979776 | bytes 4718592 | tf_op jit(solution)/shard_map/weights/pallas_call | solution.py:355
  26.7 2.7 %collective-permute-start.6 = (f32[8,32,64]{2,1,0:T(8,128)S(1)}, f32[8,32,64]{2,1,0:T(8,128)S(1)}, u32[]{:S(2)}, u32[]{:S(2)}) collective-permute-start(f32[8,32,64]{2,1,0:T(8,128)S(1)} %pad_maximum_fusion), channel_id=1, source_target_pairs={{0,16},{2,18},{4,20},{6,22},{8,24},{10,26},{12,28},{14,30},{16,0},... | collective-permute-start | bytes 196616 | tf_op jit(solution)/shard_map/ppermute | solution.py:328
  29.4 4.6 %weights.7 = (bf16[768,256]{1,0:T(8,128)(2,1)S(1)}, bf16[128,768]{1,0:T(8,128)(2,1)S(1)}, bf16[192,256]{1,0:T(8,128)(2,1)S(1)}) custom-call(bf16[64,1536]{1,0:T(8,128)(2,1)S(1)} %collective-permute-done.3.refs_0_, bf16[19,1536]{1,0:T(8,128)(2,1)S(1)} %collective-permute-done.4.refs_1_, bf16[64,1536]{1,0:T(8,128)(2,1)S(1)} %collective-permute-done.5.refs_2_, ...), custom_call_target="tpu_custom_call" | custom-call | flops 603979776 | bytes 4718592 | tf_op jit(solution)/shard_map/weights/pallas_call | solution.py:355
  33.9 0.5 collective-permute-done.6
  34.6 1.5 %collective-permute-done.7.refs_3_ = f32[16,32,64]{2,1,0:T(8,128)S(1)} collective-permute-done((f32[16,32,64]{2,1,0:T(8,128)S(1)}, f32[16,32,64]{2,1,0:T(8,128)S(1)}, u32[]{:S(2)}, u32[]{:S(2)}) %collective-permute-start.7) | collective-permute-done | bytes 131104 | tf_op jit(solution)/shard_map/ppermute | solution.py:331
  36.1 34.4 %step0.1 = (f32[64,896]{1,0:T(8,128)S(1)}, f32[64,896]{1,0:T(8,128)S(1)}, f32[64,896]{1,0:T(8,128)S(1)}) custom-call(s32[16]{0:T(128)S(1)} %copy-done.5, s32[16]{0:T(128)S(1)} %copy-done.6, f32[16,32,64]{2,1,0:T(8,128)S(1)} %constant_dynamic-update-slice_fusion.refs_2_, f32[16,32,64]{2,1,0:T(8,128)S(1)} %collective-permute-done.7.refs_3_, ...), custom_call_target="tpu_custom_call" | custom-call | flops 2919235584 | bytes 786432 | tf_op jit(solution)/shard_map/step0/pallas_call | solution.py:417
  70.5 2.3 %all-gather = f32[128,896]{1,0:T(8,128)S(1)} all-gather(f32[64,896]{1,0:T(8,128)S(1)} %get-tuple-element.55), channel_id=2, replica_groups=mesh['queue'=16,'tok'=2] {'tok'}, dimensions={0}, use_global_device_ids=true | all-gather | bytes 688128 | tf_op jit(solution)/shard_map/all_gather | solution.py:440
  72.8 20.3 %step1.1 = (f32[64,512]{1,0:T(8,128)S(1)}, f32[64,512]{1,0:T(8,128)S(1)}, f32[64,512]{1,0:T(8,128)S(1)}, f32[32,64]{1,0:T(8,128)S(1)}) custom-call(s32[16]{0:T(128)S(1)} %copy-done.5, s32[16]{0:T(128)S(1)} %copy-done.6, f32[2,64,896]{2,1,0:T(8,128)S(1)} %bitcast.7, f32[64,896]{1,0:T(8,128)S(1)} %get-tuple-element.56.refs_3_, ...), custom_call_target="tpu_custom_call" | custom-call | flops 1862270976 | bytes 786432 | tf_op jit(solution)/shard_map/step1/pallas_call | solution.py:417
  93.1 2.0 %all-gather.1 = f32[128,512]{1,0:T(8,128)S(1)} all-gather(f32[64,512]{1,0:T(8,128)S(1)} %get-tuple-element.58), channel_id=3, replica_groups=mesh['queue'=16,'tok'=2] {'tok'}, dimensions={0}, use_global_device_ids=true | all-gather | bytes 393216 | tf_op jit(solution)/shard_map/all_gather | solution.py:440
  95.1 6.2 %step2.1 = (f32[64,128]{1,0:T(8,128)S(1)}, f32[64,128]{1,0:T(8,128)S(1)}, f32[64,128]{1,0:T(8,128)S(1)}, f32[32,64]{1,0:T(8,128)S(1)}) custom-call(s32[16]{0:T(128)S(1)} %copy-done.5, s32[16]{0:T(128)S(1)} %copy-done.6, f32[2,64,512]{2,1,0:T(8,128)S(1)} %bitcast.8, f32[64,512]{1,0:T(8,128)S(1)} %get-tuple-element.59.refs_3_, ...), custom_call_target="tpu_custom_call" | custom-call | flops 805306368 | bytes 786432 | tf_op jit(solution)/shard_map/step2/pallas_call | solution.py:417
  101.3 1.9 %all-gather.2 = f32[128,128]{1,0:T(8,128)S(1)} all-gather(f32[64,128]{1,0:T(8,128)S(1)} %get-tuple-element.61), channel_id=4, replica_groups=mesh['queue'=16,'tok'=2] {'tok'}, dimensions={0}, use_global_device_ids=true | all-gather | bytes 98304 | tf_op jit(solution)/shard_map/all_gather | solution.py:440
  103.2 0.7 last.1
  (25 shorter events, 0.2 us)
Async XLA Ops:
  0.6 21.5 %collective-permute-start.4 = (bf16[19,1536]{1,0:T(8,128)(2,1)}, bf16[19,1536]{1,0:T(8,128)(2,1)S(1)}, u32[]{:S(2)}, u32[]{:S(2)}) collective-permute-start(bf16[19,1536]{1,0:T(8,128)(2,1)} %refs_1_.6), channel_id=1, source_target_pairs={{0,1},{1,0},{2,3},{3,2},{4,5},{5,4},{6,7},{7,6},{8,9},{9,8},{10,11... | collective-permute-start | bytes 175112 | tf_op jit(solution)/shard_map/ppermute | solution.py:331
  1.1 21.0 %collective-permute-start.5 = (bf16[64,1536]{1,0:T(8,128)(2,1)}, bf16[64,1536]{1,0:T(8,128)(2,1)S(1)}, u32[]{:S(2)}, u32[]{:S(2)}) collective-permute-start(bf16[64,1536]{1,0:T(8,128)(2,1)} %bitcast.4), channel_id=1, source_target_pairs={{0,1},{1,0},{2,3},{3,2},{4,5},{5,4},{6,7},{7,6},{8,9},{9,8},{10,11... | collective-permute-start | bytes 589832 | tf_op jit(solution)/shard_map/ppermute | solution.py:331
  1.2 20.9 %collective-permute-start.3 = (bf16[64,1536]{1,0:T(8,128)(2,1)}, bf16[64,1536]{1,0:T(8,128)(2,1)S(1)}, u32[]{:S(2)}, u32[]{:S(2)}) collective-permute-start(bf16[64,1536]{1,0:T(8,128)(2,1)} %refs_0_.6), channel_id=1, source_target_pairs={{0,1},{1,0},{2,3},{3,2},{4,5},{5,4},{6,7},{7,6},{8,9},{9,8},{10,11... | collective-permute-start | bytes 589832 | tf_op jit(solution)/shard_map/ppermute | solution.py:331
  2.4 14.1 %collective-permute-start = (f32[1,32,64]{2,1,0:T(8,128)S(1)}, f32[1,32,64]{2,1,0:T(8,128)S(1)}, u32[]{:S(2)}, u32[]{:S(2)}) collective-permute-start(f32[1,32,64]{2,1,0:T(8,128)S(1)} %get-tuple-element.67), channel_id=1, source_target_pairs={{0,2},{2,0},{4,6},{6,4},{8,10},{10,8},{12,14},{14,12},{16,18},{18,... | collective-permute-start | bytes 24584 | tf_op jit(solution)/shard_map/ppermute | solution.py:328
  5.0 0.9 copy-start
  5.9 0.9 copy-start.1
  6.8 0.9 copy-start.2
  16.5 4.0 %collective-permute-start.1 = (f32[2,32,64]{2,1,0:T(8,128)S(1)}, f32[2,32,64]{2,1,0:T(8,128)S(1)}, u32[]{:S(2)}, u32[]{:S(2)}) collective-permute-start(f32[2,32,64]{2,1,0:T(8,128)S(1)} %pad_maximum_fusion.2), channel_id=1, source_target_pairs={{0,4},{2,6},{4,0},{6,2},{8,12},{10,14},{12,8},{14,10},{16,20},{18,... | collective-permute-start | bytes 49160 | tf_op jit(solution)/shard_map/ppermute | solution.py:328
  20.5 6.2 %collective-permute-start.2 = (f32[4,32,64]{2,1,0:T(8,128)S(1)}, f32[4,32,64]{2,1,0:T(8,128)S(1)}, u32[]{:S(2)}, u32[]{:S(2)}) collective-permute-start(f32[4,32,64]{2,1,0:T(8,128)S(1)} %pad_maximum_fusion.1), channel_id=1, source_target_pairs={{0,8},{2,10},{4,12},{6,14},{8,0},{10,2},{12,4},{14,6},{16,24},{18,... | collective-permute-start | bytes 98312 | tf_op jit(solution)/shard_map/ppermute | solution.py:328
  26.6 9.5 %copy-start.3 = (f32[3,32,64]{2,1,0:T(8,128)S(1)}, f32[3,32,64]{2,1,0:T(8,128)}, u32[]{:S(2)}) copy-start(f32[3,32,64]{2,1,0:T(8,128)} %refs_5_.6) | copy-start | bytes 73732
  26.6 9.5 %copy-start.4 = (f32[2,768]{1,0:T(2,128)S(1)}, f32[2,768]{1,0:T(2,128)}, u32[]{:S(2)}) copy-start(f32[2,768]{1,0:T(2,128)} %refs_5_.7) | copy-start | bytes 18436
  26.6 9.5 %copy-start.5 = (s32[16]{0:T(128)S(1)}, s32[16]{0:T(128)}, u32[]{:S(2)}) copy-start(s32[16]{0:T(128)} %refs_0_.9) | copy-start | bytes 196
  26.6 9.5 %copy-start.6 = (s32[16]{0:T(128)S(1)}, s32[16]{0:T(128)}, u32[]{:S(2)}) copy-start(s32[16]{0:T(128)} %refs_1_.9) | copy-start | bytes 196
  26.7 7.8 %collective-permute-start.6 = (f32[8,32,64]{2,1,0:T(8,128)S(1)}, f32[8,32,64]{2,1,0:T(8,128)S(1)}, u32[]{:S(2)}, u32[]{:S(2)}) collective-permute-start(f32[8,32,64]{2,1,0:T(8,128)S(1)} %pad_maximum_fusion), channel_id=1, source_target_pairs={{0,16},{2,18},{4,20},{6,22},{8,24},{10,26},{12,28},{14,30},{16,0},... | collective-permute-start | bytes 196616 | tf_op jit(solution)/shard_map/ppermute | solution.py:328
  34.5 1.6 %collective-permute-start.7 = (f32[16,32,64]{2,1,0:T(8,128)S(1)}, f32[16,32,64]{2,1,0:T(8,128)S(1)}, u32[]{:S(2)}, u32[]{:S(2)}) collective-permute-start(f32[16,32,64]{2,1,0:T(8,128)S(1)} %constant_dynamic-update-slice_fusion.refs_2_), channel_id=1, source_target_pairs={{0,1},{1,0},{2,3},{3,2},{4,5},{5,4},{6,7},{7,6},{8,9},{9,8},{10,11... | collective-permute-start | bytes 393224 | tf_op jit(solution)/shard_map/ppermute | solution.py:331

commit v5 on v4

--- a/solution.py
+++ b/solution.py
@@ -53,11 +53,15 @@
     return copies
 
 
-def stack_rows(base, embed_ref, level_ref):
-    filler = base - embed_ref.shape[0] - level_ref.shape[0]
-    rows = [embed_ref[...].astype(F32), level_ref[...].astype(F32)]
-    rows = jnp.concatenate(rows + [jnp.zeros((filler, embed_ref.shape[1]), F32)], axis=0)
-    return rows.astype(BF16)
+def stack_rows(base, embed, level):
+    rows = [embed.astype(F32), level.astype(F32)]
+    rows.append(jnp.zeros((base - embed.shape[0] - level.shape[0], embed.shape[1]), F32))
+    return jnp.concatenate(rows, axis=0).astype(BF16)
+
+
+def halved_dot(a, b):
+    half = round_up(a.shape[1] // 2, LANES)
+    return dot_nt(a[:, :half], b[:, :half]) + dot_nt(a[:, half:], b[:, half:])
 
 
 def weights_kernel(rows, base, count, second, *refs):
@@ -67,12 +71,22 @@
     if count:
         sums, refs = refs[: 3 if second else 1], refs[3 if second else 1 :]
     qkv_hbm, out_hbm = refs[:2]
-    outs, buf, sems = refs[2:-2], refs[-2], refs[-1]
+    scratch = 5 + 1 if count == 0 else 2
+    outs, buf, sems = refs[-scratch - (3 if second else 1 + (count > 0)) : -scratch], refs[-2], refs[-1]
     width = out_hbm.shape[0]
     per = width // rows
     chunks = range(2 * per, 4 * per) if second else range(2 * per)
+    if count == 0:
+        held, small = refs[-6:-3], refs[-3]
+        brought = [pltpu.make_async_copy(tables[at], held[at], small.at[at]) for at in range(3)]
+        for copy in brought:
+            copy.start()
     copies = start_chunks(rows, chunks, shares, qkv_hbm, out_hbm, buf, sems)
-    lefts = [stack_rows(base, *tables[3 * at : 3 * at + 2]) for at in range(len(shares))]
+    if count == 0:
+        for copy in brought:
+            copy.wait()
+        tables = held
+    lefts = [stack_rows(base, tables[3 * at][...], tables[3 * at + 1][...]) for at in range(len(shares))]
     vels = [tables[3 * at + 2][...] for at in range(len(shares))]
     if second:
         gram = sum(dot_nt(jnp.concatenate([left, vel], axis=0), left) for left, vel in zip(lefts, vels))
@@ -81,19 +95,19 @@
         for at in range(len(shares)):
             copies[place * len(shares) + at].wait()
         last = chunk // per == 3
-        total = sum(dot_nt(buf[at, place], vels[at] if last else lefts[at]) for at in range(len(shares)))
+        total = sum(halved_dot(vels[at] if last else lefts[at], buf[at, place]) for at in range(len(shares)))
         spot = slice(place * rows, (place + 1) * rows)
         if last:
             spot = slice((place - per) * rows, (place - per + 1) * rows)
         if count == 0:
-            outs[1 if last else 0][spot, :] = total
+            outs[1 if last else 0][:, spot] = total
             continue
-        total = total + sums[1 if last else 0][spot, :]
+        total = total + sums[1 if last else 0][:, spot]
         where = slice((chunk % per) * rows, (chunk % per + 1) * rows)
         if chunk // per % 2:
-            outs[1][:, where] = halves(total.T, 0)
+            outs[1][:, where] = halves(total, 0)
         else:
-            outs[0][where, :] = halves(total, 1)
+            outs[0][where, :] = halves(total.T, 1)
 
 
 def advance(level_count, tok, first, g_ref, hpart_ref, xq_ref):
@@ -127,8 +141,8 @@
     slot_ref, reach_ref = refs[0], refs[1]
     if step == 0:
         count = tok // part_rows
-        lat_refs = refs[2 : 2 + count]
-        refs = refs[2 + count :]
+        lat_refs, noise_refs = refs[2 : 2 + count], refs[2 + count : 1 + 2 * count]
+        refs = refs[1 + 2 * count :]
     else:
         g_ref, hprev_ref, xprev_ref = refs[2:5]
         refs = refs[5:]
@@ -145,11 +159,13 @@
     kbuf, vbuf, qbuf, att, tbuf, xbuf = refs
 
     if step == 0:
+        noise = [fresh_ref[0]] + [ref[...] for ref in noise_refs]
         for w in range(n_key):
             source = lax.rem(first_key - 1 + w + 2 * frames, frames)
             for t in range(count):
                 at = lax.rem(tok_index + t, count) * part_rows + w * tok
-                xbuf[pl.ds(pl.multiple_of(at, 8), part_rows), :] = lat_refs[t][position ^ source]
+                rows = jnp.where(source == frames - 1, noise[t], lat_refs[t][position ^ source])
+                xbuf[pl.ds(pl.multiple_of(at, 8), part_rows), :] = rows
         state = xbuf[...].T
     else:
         velocity, state = advance(level_count, tok, first_key - 1, g_ref, hprev_ref, xprev_ref)
@@ -165,21 +181,22 @@
     row = lax.broadcasted_iota(jnp.int32, (base - channels, key_lanes), 0)
     aug_t = jnp.concatenate([state, jnp.where(row == level_row, 1.0, 0.0)], axis=0)
     aug_t = aug_t.astype(BF16).astype(F32)
-    aug = aug_t.T
-    aug_b, aug_tb = aug.astype(BF16), aug_t.astype(BF16)
-    aug_q = aug_t[:, HALO * tok : HALO * tok + query_lanes]
-    aug_qb = aug_q.astype(BF16)
+    aug_tb = aug_t.astype(BF16)
+    both_t = jnp.concatenate([aug_tb, aug_tb], axis=0)
+    mean_t = jnp.sum(dot(gram_ref[:base, :], both_t) * aug_t, axis=0, keepdims=True) * (1.0 / depth)
+    mean_t = jnp.maximum(mean_t, 0.0) + EPS
+    queries = slice(HALO * tok, HALO * tok + query_lanes)
+    mean_q = mean_t[:, queries]
+    aug_qb = aug_t[:, queries].astype(BF16)
+    both_q = jnp.concatenate([aug_qb, aug_qb], axis=0)
+    last_row = lax.broadcasted_iota(jnp.int32, (base, key_lanes), 0) == base - 1
+    aug = jnp.where(last_row, EPS * mean_t, aug_t).T
+    eps_c = aug[:, base - 1 : base]
+    aug_b = aug.astype(BF16)
     both = jnp.concatenate([aug_b, aug_b], axis=1)
-    both_t = jnp.concatenate([aug_tb, aug_tb], axis=0)
-    both_q = jnp.concatenate([aug_qb, aug_qb], axis=0)
-    gram = gram_ref[:base, :]
-    mean_t = jnp.sum(dot(gram, both_t) * aug_t, axis=0, keepdims=True) * (1.0 / depth)
-    mean_q = jnp.sum(dot(gram, both_q) * aug_q, axis=0, keepdims=True) * (1.0 / depth)
-    mean_c = jnp.sum(dot_nt(both, gram) * aug, axis=1, keepdims=True) * (1.0 / depth)
-    mean_t, mean_q, mean_c = (jnp.maximum(m, 0.0) + EPS for m in (mean_t, mean_q, mean_c))
 
     hpart_ref[...] = dot(gram_ref[base:, :], both_q)
-    xq_ref[...] = state[:, HALO * tok : HALO * tok + query_lanes]
+    xq_ref[...] = state[:, queries]
 
     gain = gain_ref[0:1, :] * gain_ref[1:2, :] * (HD ** -0.5 * math.log2(math.e))
     span = 256 if width % 256 == 0 else 128
@@ -188,7 +205,7 @@
     for at in range(0, width, span):
         raw = dot(both, mk_ref[:, at : at + span])
         spread = dot((raw * raw).astype(BF16), average)
-        kbuf[:, at : at + span] = (raw * lax.rsqrt(spread + EPS * mean_c) * gain[:, at : at + span]).astype(BF16)
+        kbuf[:, at : at + span] = (raw * lax.rsqrt(spread + eps_c) * gain[:, at : at + span]).astype(BF16)
     vbuf[...] = (dot(mv_ref[...], both_t) * lax.rsqrt(mean_t)).astype(BF16)
     raw = dot(mq_ref[...], both_q).reshape(heads, HD, query_lanes)
     spread = jnp.sum(raw * raw, axis=1, keepdims=True) * (1.0 / HD)
@@ -314,12 +331,13 @@
         out_weight = jnp.pad(out_weight, ((0, spare), (0, 0)))
         width += spare
     heads = width // HD
-    base = round_up(channels + level_count, LANES)
+    base = round_up(channels + level_count + 1, LANES)
     cfg = (tok, frames, channels, base, depth, level_count, heads, part_rows)
-    vmem, smem, hbm = (
+    vmem, smem, hbm, anywhere = (
         pl.BlockSpec(memory_space=pltpu.VMEM),
         pl.BlockSpec(memory_space=pltpu.SMEM),
         pl.BlockSpec(memory_space=pltpu.HBM),
+        pl.BlockSpec(memory_space=pl.ANY),
     )
     shape = jax.ShapeDtypeStruct
 
@@ -333,17 +351,19 @@
     share = depth // parts
     table = (embed_weight, level_embed, vel_weight.T)
     tables = [from_ahead(piece, d) for d in range(1, parts) for piece in table]
+    noise = [from_ahead(fresh_noise[0], d) for d in range(1, parts)]
+    in_hbm = lambda array: pltpu.with_memory_space_constraint(array, pltpu.HBM)
+    table = tuple(in_hbm(piece) for piece in table)
+    qkv_weight, out_weight = in_hbm(qkv_weight), in_hbm(out_weight)
     rows = 384 if width % 384 == 0 else 256
     chunks = 2 * width // rows
-    qkv_weight = pltpu.with_memory_space_constraint(qkv_weight, pltpu.HBM)
-    out_weight = pltpu.with_memory_space_constraint(out_weight, pltpu.HBM)
-
-    def weights(count, second, *operands):
+
+    def weights(count, second, after, *operands):
         shares = max(1, count - 1)
         if count == 0 and second:
-            outs = [shape((width, base), F32), shape((width, channels), F32), shape((base + channels, base), F32)]
+            outs = [shape((base, width), F32), shape((channels, width), F32), shape((base + channels, base), F32)]
         elif count == 0:
-            outs = [shape((2 * width, base), F32)]
+            outs = [shape((base, 2 * width), F32)]
         elif second:
             outs = [
                 shape((width, 2 * base), BF16),
@@ -352,15 +372,16 @@
             ]
         else:
             outs = [shape((width, 2 * base), BF16), shape((2 * base, width), BF16)]
+        scratch = [pltpu.VMEM((shares, chunks, rows, share), BF16), pltpu.SemaphoreType.DMA((shares, chunks))]
+        if count == 0:
+            held = [pltpu.VMEM(piece.shape, BF16) for piece in table]
+            scratch = held + [pltpu.SemaphoreType.DMA((3,))] + scratch
         return pl.pallas_call(
             functools.partial(weights_kernel, rows, base, count, second),
             out_shape=tuple(outs),
-            in_specs=[vmem] * len(operands) + [hbm] * 2,
+            in_specs=[hbm if count == 0 else vmem] * len(operands) + [hbm] * 2 + [anywhere] * len(after),
             out_specs=(vmem,) * len(outs),
-            scratch_shapes=[
-                pltpu.VMEM((shares, chunks, rows, share), BF16),
-                pltpu.SemaphoreType.DMA((shares, chunks)),
-            ],
+            scratch_shapes=scratch,
             compiler_params=pltpu.CompilerParams(vmem_limit_bytes=24 * 2**20),
             cost_estimate=pl.CostEstimate(
                 flops=4 * base * width * share * shares,
@@ -368,27 +389,28 @@
                 transcendentals=0,
             ),
             name="weights",
-        )(*operands, qkv_weight, out_weight)
-
-    state = jnp.where(position == frames - 1, fresh_noise[0], latent[0])[None]
+        )(*operands, qkv_weight, out_weight, *after)
+
+    state = latent
     work = [
-        lambda: weights(0, False, *table),
-        lambda: weights(0, True, *table),
-        lambda: weights(parts, False, *tables, *done[0]),
-        lambda: weights(parts, True, *tables, *done[1]),
+        lambda *after: weights(0, False, after, *table),
+        lambda *after: weights(0, True, after, *table),
+        lambda *after: weights(parts, False, after, *tables, *done[0]),
+        lambda *after: weights(parts, True, after, *tables, *done[1]),
     ]
-    done = []
+    done, after = [], ()
     reached = 1
     while reached < frames:
         moved = swapped(state, "queue", reached)
         if len(done) < len(work):
-            moved, result = lax.optimization_barrier((moved, work[len(done)]()))
+            moved, noise, result = lax.optimization_barrier((moved, noise, work[len(done)](*after)))
             done.append(result)
+            after = (moved,)
         state = jnp.concatenate([state, moved], axis=0)
         reached *= 2
     while len(done) < len(work):
         done.append(work[len(done)]())
-    latents = [state] + [from_ahead(state, d) for d in range(1, parts)]
+    latents = [state] + [from_ahead(state, d) for d in range(1, parts)] + noise
     mq, mk = done[2]
     mv, wo, gram = done[3]
 
@@ -401,7 +423,7 @@
         specs = [smem, smem]
         if step == 0:
             args += latents
-            specs += [vmem] * parts
+            specs += [vmem] * len(latents)
         else:
             args += [gathered, hpart, xq]
             specs += [vmem] * 3

time: 104 us -> 99.8 us (0.960)
  Pallas kernels: 79.4 us -> 77.7 us
  local copies, waits for them, and re-layouts: 2.78 us -> 1.5 us
    unnamed x17 -> x14, local copies, waits for them, and re-layouts: 2.77 us -> 0.76 us
    pallas_call x4, Pallas kernels: 17.8 us -> 16.3 us  [weights(): pl.pallas_call(functools.partial(weights_kernel, rows, base, count, secon...]
  transfers between devices with their start and end apart: 8 -> 9, of which waited for: 3 -> 2; matrix products, arithmetic and copies ran while one was open for 1% -> 1% of each run, Pallas kernels for 17% -> 16%
where the time goes in v5:
time: 99.8 us; the launch traced here: 99.4 us
  Pallas kernels  77.7 us (78%)
  starting transfers between devices  9.64 us (10%)
  blocking collectives  6.16 us (6%)
  waiting for transfers between devices  3.56 us (4%)
  local copies, waits for them, and re-layouts  1.5 us (2%)
    pallas_call x3, Pallas kernels, body(): pl.pallas_call(functools.partial(step_kernel, step, cfg), out_shape=tuple...  60.7 us
    pallas_call x4, Pallas kernels, weights(): pl.pallas_call(functools.partial(weights_kernel, rows, base, count, secon...  16.3 us
    ppermute x4, starting transfers between devices, swapped(): lax.ppermute(value, axis, [(source, source ^ distance) for source in rang...  8.37 us
    all_gather x3, blocking collectives, body(): gathered = lax.all_gather(part, 'tok', axis=0, tiled=False)  6.16 us
    ppermute x4, waiting for transfers between devices, swapped(): lax.ppermute(value, axis, [(source, source ^ distance) for source in rang...  2.03 us
  transfers between devices with their start and end apart: 9, of which 2 were waited for; matrix products, arithmetic and copies ran while one was open for 1% of the time, Pallas kernels for 16%

profile of v5, /device:TPU:0, one launch (start us, length us, event | category | flops | bytes accessed | tf_op | source)
XLA Modules:
  0.0 99.4 jit_solution(13760146337017008466)
XLA Ops:
  0.6 0.7 slice_bitcast_fusion
  1.4 0.5 collective-permute-start.1
  1.8 2.5 %collective-permute-start = (f32[1,32,64]{2,1,0:T(8,128)}, f32[1,32,64]{2,1,0:T(8,128)S(1)}, u32[]{:S(2)}, u32[]{:S(2)}) collective-permute-start(f32[1,32,64]{2,1,0:T(8,128)} %param.10), channel_id=1, source_target_pairs={{0,2},{2,0},{4,6},{6,4},{8,10},{10,8},{12,14},{14,12},{16,18},{18,... | collective-permute-start | bytes 24584 | tf_op jit(solution)/shard_map/ppermute | solution.py:346
  4.3 0.2 collective-permute-start.6
  4.5 0.3 collective-permute-start.4
  4.8 0.2 collective-permute-start.5
  5.0 0.7 constant_dynamic-update-slice_fusion.4
  5.8 3.9 %weights.4.refs_3_ = f32[128,1536]{1,0:T(8,128)S(1)} custom-call(bf16[64,1536]{1,0:T(8,128)(2,1)} %refs_0_.6, bf16[19,1536]{1,0:T(8,128)(2,1)} %refs_1_.6, bf16[64,1536]{1,0:T(8,128)(2,1)} %bitcast.10, bf16[3,768,3072]{2,1,0:T(8,128)(2,1)} %refs_6_.3, bf16[768,3072]{1,0:T(8,128)(2,1)} %refs_7_.1), custom_call_target="tpu_custom_call" | custom-call | flops 603979776 | bytes 4718592 | tf_op jit(solution)/shard_map/weights/pallas_call | solution.py:379
  9.7 1.6 %collective-permute-start.2 = (f32[2,32,64]{2,1,0:T(8,128)S(1)}, f32[2,32,64]{2,1,0:T(8,128)S(1)}, u32[]{:S(2)}, u32[]{:S(2)}) collective-permute-start(f32[2,32,64]{2,1,0:T(8,128)S(1)} %pad_maximum_fusion.2), channel_id=1, source_target_pairs={{0,4},{2,6},{4,0},{6,2},{8,12},{10,14},{12,8},{14,10},{16,20},{18,... | collective-permute-start | bytes 49160 | tf_op jit(solution)/shard_map/ppermute | solution.py:346
  11.3 4.5 %weights.5 = (f32[128,768]{1,0:T(8,128)S(1)}, f32[64,768]{1,0:T(8,128)S(1)}, f32[192,128]{1,0:T(8,128)S(1)}) custom-call(bf16[64,1536]{1,0:T(8,128)(2,1)} %refs_0_.6, bf16[19,1536]{1,0:T(8,128)(2,1)} %refs_1_.6, bf16[64,1536]{1,0:T(8,128)(2,1)} %bitcast.11, bf16[3,768,3072]{2,1,0:T(8,128)(2,1)} %refs_6_.3, bf16[768,3072]{1,0:T(8,128)(2,1)} %refs_7_.1, ...), custom_call_target="tpu_custom_call" | custom-call | flops 603979776 | bytes 4718592 | tf_op jit(solution)/shard_map/weights/pallas_call | solution.py:379
  15.8 1.6 %collective-permute-start.3 = (f32[4,32,64]{2,1,0:T(8,128)S(1)}, f32[4,32,64]{2,1,0:T(8,128)S(1)}, u32[]{:S(2)}, u32[]{:S(2)}) collective-permute-start(f32[4,32,64]{2,1,0:T(8,128)S(1)} %pad_maximum_fusion.1), channel_id=1, source_target_pairs={{0,8},{2,10},{4,12},{6,14},{8,0},{10,2},{12,4},{14,6},{16,24},{18,... | collective-permute-start | bytes 98312 | tf_op jit(solution)/shard_map/ppermute | solution.py:346
  17.4 3.9 %weights.6 = (bf16[768,256]{1,0:T(8,128)(2,1)S(1)}, bf16[256,768]{1,0:T(8,128)(2,1)S(1)}) custom-call(bf16[64,1536]{1,0:T(8,128)(2,1)S(1)} %collective-permute-done.4.refs_0_, bf16[19,1536]{1,0:T(8,128)(2,1)S(1)} %collective-permute-done.5.refs_1_, bf16[64,1536]{1,0:T(8,128)(2,1)S(1)} %collective-permute-done.6.refs_2_, f32[128,1536]{1,0:T(8,128)S(1)} %weights.4.refs_3_, ...), custom_call_target="tpu_custom_call" | custom-call | flops 603979776 | bytes 4718592 | tf_op jit(solution)/shard_map/weights/pallas_call | solution.py:379
  21.4 2.7 %collective-permute-start.7 = (f32[8,32,64]{2,1,0:T(8,128)S(1)}, f32[8,32,64]{2,1,0:T(8,128)S(1)}, u32[]{:S(2)}, u32[]{:S(2)}) collective-permute-start(f32[8,32,64]{2,1,0:T(8,128)S(1)} %pad_maximum_fusion), channel_id=1, source_target_pairs={{0,16},{2,18},{4,20},{6,22},{8,24},{10,26},{12,28},{14,30},{16,0},... | collective-permute-start | bytes 196616 | tf_op jit(solution)/shard_map/ppermute | solution.py:346
  24.1 4.1 %weights.7 = (bf16[768,256]{1,0:T(8,128)(2,1)S(1)}, bf16[128,768]{1,0:T(8,128)(2,1)S(1)}, bf16[192,256]{1,0:T(8,128)(2,1)S(1)}) custom-call(bf16[64,1536]{1,0:T(8,128)(2,1)S(1)} %collective-permute-done.4.refs_0_, bf16[19,1536]{1,0:T(8,128)(2,1)S(1)} %collective-permute-done.5.refs_1_, bf16[64,1536]{1,0:T(8,128)(2,1)S(1)} %collective-permute-done.6.refs_2_, ...), custom_call_target="tpu_custom_call" | custom-call | flops 603979776 | bytes 4718592 | tf_op jit(solution)/shard_map/weights/pallas_call | solution.py:379
  28.2 2.0 %collective-permute-done.7 = f32[8,32,64]{2,1,0:T(8,128)S(1)} collective-permute-done((f32[8,32,64]{2,1,0:T(8,128)S(1)}, f32[8,32,64]{2,1,0:T(8,128)S(1)}, u32[]{:S(2)}, u32[]{:S(2)}) %collective-permute-start.7) | collective-permute-done | bytes 65568 | tf_op jit(solution)/shard_map/ppermute | solution.py:346
  30.2 0.1 collective-permute-start.8
  30.3 1.5 %collective-permute-done.8.refs_3_ = f32[16,32,64]{2,1,0:T(8,128)S(1)} collective-permute-done((f32[16,32,64]{2,1,0:T(8,128)S(1)}, f32[16,32,64]{2,1,0:T(8,128)S(1)}, u32[]{:S(2)}, u32[]{:S(2)}) %collective-permute-start.8) | collective-permute-done | bytes 131104 | tf_op jit(solution)/shard_map/ppermute | solution.py:349
  31.9 34.1 %step0.1 = (f32[64,896]{1,0:T(8,128)S(1)}, f32[64,896]{1,0:T(8,128)S(1)}, f32[64,896]{1,0:T(8,128)S(1)}) custom-call(s32[16]{0:T(128)S(1)} %copy-done.2, s32[16]{0:T(128)S(1)} %copy-done.3, f32[16,32,64]{2,1,0:T(8,128)S(1)} %constant_dynamic-update-slice_fusion.refs_2_, f32[16,32,64]{2,1,0:T(8,128)S(1)} %collective-permute-done.8.refs_3_, ...), custom_call_target="tpu_custom_call" | custom-call | flops 2919235584 | bytes 786432 | tf_op jit(solution)/shard_map/step0/pallas_call | solution.py:439
  65.9 2.3 %all-gather = f32[128,896]{1,0:T(8,128)S(1)} all-gather(f32[64,896]{1,0:T(8,128)S(1)} %get-tuple-element.63), channel_id=2, replica_groups=mesh['queue'=16,'tok'=2] {'tok'}, dimensions={0}, use_global_device_ids=true | all-gather | bytes 688128 | tf_op jit(solution)/shard_map/all_gather | solution.py:462
  68.2 20.1 %step1.1 = (f32[64,512]{1,0:T(8,128)S(1)}, f32[64,512]{1,0:T(8,128)S(1)}, f32[64,512]{1,0:T(8,128)S(1)}, f32[32,64]{1,0:T(8,128)S(1)}) custom-call(s32[16]{0:T(128)S(1)} %copy-done.2, s32[16]{0:T(128)S(1)} %copy-done.3, f32[2,64,896]{2,1,0:T(8,128)S(1)} %bitcast.6, f32[64,896]{1,0:T(8,128)S(1)} %get-tuple-element.64.refs_3_, ...), custom_call_target="tpu_custom_call" | custom-call | flops 1862270976 | bytes 786432 | tf_op jit(solution)/shard_map/step1/pallas_call | solution.py:439
  88.4 2.0 %all-gather.1 = f32[128,512]{1,0:T(8,128)S(1)} all-gather(f32[64,512]{1,0:T(8,128)S(1)} %get-tuple-element.66), channel_id=3, replica_groups=mesh['queue'=16,'tok'=2] {'tok'}, dimensions={0}, use_global_device_ids=true | all-gather | bytes 393216 | tf_op jit(solution)/shard_map/all_gather | solution.py:462
  90.4 6.5 %step2.1 = (f32[64,128]{1,0:T(8,128)S(1)}, f32[64,128]{1,0:T(8,128)S(1)}, f32[64,128]{1,0:T(8,128)S(1)}, f32[32,64]{1,0:T(8,128)S(1)}) custom-call(s32[16]{0:T(128)S(1)} %copy-done.2, s32[16]{0:T(128)S(1)} %copy-done.3, f32[2,64,512]{2,1,0:T(8,128)S(1)} %bitcast.7, f32[64,512]{1,0:T(8,128)S(1)} %get-tuple-element.67.refs_3_, ...), custom_call_target="tpu_custom_call" | custom-call | flops 805306368 | bytes 786432 | tf_op jit(solution)/shard_map/step2/pallas_call | solution.py:439
  96.9 1.9 %all-gather.2 = f32[128,128]{1,0:T(8,128)S(1)} all-gather(f32[64,128]{1,0:T(8,128)S(1)} %get-tuple-element.69), channel_id=4, replica_groups=mesh['queue'=16,'tok'=2] {'tok'}, dimensions={0}, use_global_device_ids=true | all-gather | bytes 98304 | tf_op jit(solution)/shard_map/all_gather | solution.py:462
  98.7 0.7 last.1
  (24 shorter events, 0.1 us)
Async XLA Ops:
  0.6 9.0 %copy-start.4 = (f32[1,32,64]{2,1,0:T(8,128)S(1)}, f32[1,32,64]{2,1,0:T(8,128)}, u32[]{:S(2)}) copy-start(f32[1,32,64]{2,1,0:T(8,128)} %param.10) | copy-start | bytes 24580
  1.4 8.3 %collective-permute-start.1 = (f32[32,64]{1,0:T(8,128)S(1)}, f32[32,64]{1,0:T(8,128)S(1)}, u32[]{:S(2)}, u32[]{:S(2)}) collective-permute-start(f32[32,64]{1,0:T(8,128)S(1)} %slice_bitcast_fusion), channel_id=1, source_target_pairs={{0,1},{1,0},{2,3},{3,2},{4,5},{5,4},{6,7},{7,6},{8,9},{9,8},{10,11... | collective-permute-start | bytes 24584 | tf_op jit(solution)/shard_map/ppermute | solution.py:349
  1.8 7.8 %collective-permute-start = (f32[1,32,64]{2,1,0:T(8,128)}, f32[1,32,64]{2,1,0:T(8,128)S(1)}, u32[]{:S(2)}, u32[]{:S(2)}) collective-permute-start(f32[1,32,64]{2,1,0:T(8,128)} %param.10), channel_id=1, source_target_pairs={{0,2},{2,0},{4,6},{6,4},{8,10},{10,8},{12,14},{14,12},{16,18},{18,... | collective-permute-start | bytes 24584 | tf_op jit(solution)/shard_map/ppermute | solution.py:346
  4.3 13.1 %collective-permute-start.6 = (bf16[64,1536]{1,0:T(8,128)(2,1)}, bf16[64,1536]{1,0:T(8,128)(2,1)S(1)}, u32[]{:S(2)}, u32[]{:S(2)}) collective-permute-start(bf16[64,1536]{1,0:T(8,128)(2,1)} %bitcast.9), channel_id=1, source_target_pairs={{0,1},{1,0},{2,3},{3,2},{4,5},{5,4},{6,7},{7,6},{8,9},{9,8},{10,11... | collective-permute-start | bytes 589832 | tf_op jit(solution)/shard_map/ppermute | solution.py:349
  4.5 12.9 %collective-permute-start.4 = (bf16[64,1536]{1,0:T(8,128)(2,1)}, bf16[64,1536]{1,0:T(8,128)(2,1)S(1)}, u32[]{:S(2)}, u32[]{:S(2)}) collective-permute-start(bf16[64,1536]{1,0:T(8,128)(2,1)} %refs_0_.6), channel_id=1, source_target_pairs={{0,1},{1,0},{2,3},{3,2},{4,5},{5,4},{6,7},{7,6},{8,9},{9,8},{10,11... | collective-permute-start | bytes 589832 | tf_op jit(solution)/shard_map/ppermute | solution.py:349
  4.8 12.6 %collective-permute-start.5 = (bf16[19,1536]{1,0:T(8,128)(2,1)}, bf16[19,1536]{1,0:T(8,128)(2,1)S(1)}, u32[]{:S(2)}, u32[]{:S(2)}) collective-permute-start(bf16[19,1536]{1,0:T(8,128)(2,1)} %refs_1_.6), channel_id=1, source_target_pairs={{0,1},{1,0},{2,3},{3,2},{4,5},{5,4},{6,7},{7,6},{8,9},{9,8},{10,11... | collective-permute-start | bytes 175112 | tf_op jit(solution)/shard_map/ppermute | solution.py:349
  9.7 6.1 %collective-permute-start.2 = (f32[2,32,64]{2,1,0:T(8,128)S(1)}, f32[2,32,64]{2,1,0:T(8,128)S(1)}, u32[]{:S(2)}, u32[]{:S(2)}) collective-permute-start(f32[2,32,64]{2,1,0:T(8,128)S(1)} %pad_maximum_fusion.2), channel_id=1, source_target_pairs={{0,4},{2,6},{4,0},{6,2},{8,12},{10,14},{12,8},{14,10},{16,20},{18,... | collective-permute-start | bytes 49160 | tf_op jit(solution)/shard_map/ppermute | solution.py:346
  15.8 5.6 %collective-permute-start.3 = (f32[4,32,64]{2,1,0:T(8,128)S(1)}, f32[4,32,64]{2,1,0:T(8,128)S(1)}, u32[]{:S(2)}, u32[]{:S(2)}) collective-permute-start(f32[4,32,64]{2,1,0:T(8,128)S(1)} %pad_maximum_fusion.1), channel_id=1, source_target_pairs={{0,8},{2,10},{4,12},{6,14},{8,0},{10,2},{12,4},{14,6},{16,24},{18,... | collective-permute-start | bytes 98312 | tf_op jit(solution)/shard_map/ppermute | solution.py:346
  21.4 10.5 %copy-start = (f32[3,32,64]{2,1,0:T(8,128)S(1)}, f32[3,32,64]{2,1,0:T(8,128)}, u32[]{:S(2)}) copy-start(f32[3,32,64]{2,1,0:T(8,128)} %refs_5_.6) | copy-start | bytes 73732
  21.4 10.5 %copy-start.1 = (f32[2,768]{1,0:T(2,128)S(1)}, f32[2,768]{1,0:T(2,128)}, u32[]{:S(2)}) copy-start(f32[2,768]{1,0:T(2,128)} %refs_5_.7) | copy-start | bytes 18436
  21.4 10.5 %copy-start.2 = (s32[16]{0:T(128)S(1)}, s32[16]{0:T(128)}, u32[]{:S(2)}) copy-start(s32[16]{0:T(128)} %refs_0_.9) | copy-start | bytes 196
  21.4 10.5 %copy-start.3 = (s32[16]{0:T(128)S(1)}, s32[16]{0:T(128)}, u32[]{:S(2)}) copy-start(s32[16]{0:T(128)} %refs_1_.9) | copy-start | bytes 196
  21.4 8.8 %collective-permute-start.7 = (f32[8,32,64]{2,1,0:T(8,128)S(1)}, f32[8,32,64]{2,1,0:T(8,128)S(1)}, u32[]{:S(2)}, u32[]{:S(2)}) collective-permute-start(f32[8,32,64]{2,1,0:T(8,128)S(1)} %pad_maximum_fusion), channel_id=1, source_target_pairs={{0,16},{2,18},{4,20},{6,22},{8,24},{10,26},{12,28},{14,30},{16,0},... | collective-permute-start | bytes 196616 | tf_op jit(solution)/shard_map/ppermute | solution.py:346
  30.2 1.6 %collective-permute-start.8 = (f32[16,32,64]{2,1,0:T(8,128)S(1)}, f32[16,32,64]{2,1,0:T(8,128)S(1)}, u32[]{:S(2)}, u32[]{:S(2)}) collective-permute-start(f32[16,32,64]{2,1,0:T(8,128)S(1)} %constant_dynamic-update-slice_fusion.refs_2_), channel_id=1, source_target_pairs={{0,1},{1,0},{2,3},{3,2},{4,5},{5,4},{6,7},{7,6},{8,9},{9,8},{10,11... | collective-permute-start | bytes 393224 | tf_op jit(solution)/shard_map/ppermute | solution.py:349

commit v6 on v5

--- a/solution.py
+++ b/solution.py
@@ -12,6 +12,7 @@
 STEPS = 3
 HALO = 3
 LANES = 128
+AHEAD = 3
 EPS = 1e-06
 F32, BF16 = jnp.float32, jnp.bfloat16
 
@@ -34,22 +35,20 @@
     return jnp.concatenate([high, low], axis=axis)
 
 
-def start_chunks(rows, chunks, parts, qkv_hbm, out_hbm, buf, sems):
+def chunk_copies(rows, chunks, parts, qkv_hbm, out_hbm, buf, sems):
     per = out_hbm.shape[0] // rows
     depth = buf.shape[-1]
     index, count = lax.axis_index("tok"), lax.axis_size("tok")
-    copies = []
+    copies = {}
     for place, chunk in enumerate(chunks):
         source = qkv_hbm.at[chunk // per] if chunk < 3 * per else out_hbm
         for at, part in enumerate(parts):
             columns = pl.ds(pl.multiple_of(lax.rem(index + part, count) * depth, LANES), depth)
-            copy = pltpu.make_async_copy(
+            copies[place, at] = pltpu.make_async_copy(
                 source.at[pl.ds((chunk % per) * rows, rows), columns],
                 buf.at[at, place],
                 sems.at[at, place],
             )
-            copy.start()
-            copies.append(copy)
     return copies
 
 
@@ -81,7 +80,10 @@
         brought = [pltpu.make_async_copy(tables[at], held[at], small.at[at]) for at in range(3)]
         for copy in brought:
             copy.start()
-    copies = start_chunks(rows, chunks, shares, qkv_hbm, out_hbm, buf, sems)
+    copies = chunk_copies(rows, chunks, shares, qkv_hbm, out_hbm, buf, sems)
+    for key in copies:
+        if key[0] < AHEAD:
+            copies[key].start()
     if count == 0:
         for copy in brought:
             copy.wait()
@@ -93,7 +95,9 @@
         outs[2][...] = halves(sums[2][...] + gram, 1) if count else gram
     for place, chunk in enumerate(chunks):
         for at in range(len(shares)):
-            copies[place * len(shares) + at].wait()
+            copies[place, at].wait()
+            if place + AHEAD < len(chunks):
+                copies[place + AHEAD, at].start()
         last = chunk // per == 3
         total = sum(halved_dot(vels[at] if last else lefts[at], buf[at, place]) for at in range(len(shares)))
         spot = slice(place * rows, (place + 1) * rows)
@@ -159,12 +163,17 @@
     kbuf, vbuf, qbuf, att, tbuf, xbuf = refs
 
     if step == 0:
-        noise = [fresh_ref[0]] + [ref[...] for ref in noise_refs]
+        noise = [fresh_ref[0]] + [ref[0] for ref in noise_refs]
         for w in range(n_key):
             source = lax.rem(first_key - 1 + w + 2 * frames, frames)
+            apart, bits = position ^ source, frames.bit_length() - 2
+            second = ((apart >> bits) & 1) == 1
+            entry = sum(((apart >> bit) & 1) << (bits - 1 - bit) for bit in range(bits))
             for t in range(count):
                 at = lax.rem(tok_index + t, count) * part_rows + w * tok
-                rows = jnp.where(source == frames - 1, noise[t], lat_refs[t][position ^ source])
+                beside = lat_refs[t][entry]
+                rows = jnp.where(second, beside[:, channels:], beside[:, :channels])
+                rows = jnp.where(source == frames - 1, noise[t], rows)
                 xbuf[pl.ds(pl.multiple_of(at, 8), part_rows), :] = rows
         state = xbuf[...].T
     else:
@@ -351,11 +360,11 @@
     share = depth // parts
     table = (embed_weight, level_embed, vel_weight.T)
     tables = [from_ahead(piece, d) for d in range(1, parts) for piece in table]
-    noise = [from_ahead(fresh_noise[0], d) for d in range(1, parts)]
+    noise = [from_ahead(fresh_noise, d) for d in range(1, parts)]
     in_hbm = lambda array: pltpu.with_memory_space_constraint(array, pltpu.HBM)
     table = tuple(in_hbm(piece) for piece in table)
     qkv_weight, out_weight = in_hbm(qkv_weight), in_hbm(out_weight)
-    rows = 384 if width % 384 == 0 else 256
+    rows = 256
     chunks = 2 * width // rows
 
     def weights(count, second, after, *operands):
@@ -399,15 +408,16 @@
         lambda *after: weights(parts, True, after, *tables, *done[1]),
     ]
     done, after = [], ()
-    reached = 1
-    while reached < frames:
-        moved = swapped(state, "queue", reached)
+    distance = frames // 2
+    while distance:
+        moved = swapped(state, "queue", distance)
         if len(done) < len(work):
             moved, noise, result = lax.optimization_barrier((moved, noise, work[len(done)](*after)))
             done.append(result)
             after = (moved,)
-        state = jnp.concatenate([state, moved], axis=0)
-        reached *= 2
+        axis = 2 if distance == frames // 2 else 0
+        state = lax.optimization_barrier(jnp.concatenate([state, moved], axis=axis))
+        distance //= 2
     while len(done) < len(work):
         done.append(work[len(done)]())
     latents = [state] + [from_ahead(state, d) for d in range(1, parts)] + noise

time: 99.8 us -> 99.7 us (level)
  Pallas kernels: 77.7 us -> 81.1 us
  waiting for transfers between devices: 3.56 us -> 1.36 us
  local copies, waits for them, and re-layouts: 1.5 us -> 0.03 us
    pallas_call x4, Pallas kernels: 16.3 us -> 19.4 us  [weights(): pl.pallas_call(functools.partial(weights_kernel, rows, base, count, secon...]
    ppermute x4, waiting for transfers between devices: 2.03 us -> 0.01 us  [swapped(): lax.ppermute(value, axis, [(source, source ^ distance) for source in rang...]
  transfers between devices with their start and end apart: 9 -> 9, of which waited for: 2 -> 1; matrix products, arithmetic and copies ran while one was open for 1% -> 0% of each run, Pallas kernels for 16% -> 19%
where the time goes in v6:
time: 99.7 us; the launch traced here: 99.5 us
  Pallas kernels  81.1 us (81%)
  starting transfers between devices  9.92 us (10%)
  blocking collectives  6.16 us (6%)
  waiting for transfers between devices  1.36 us (1%)
    pallas_call x3, Pallas kernels, body(): pl.pallas_call(functools.partial(step_kernel, step, cfg), out_shape=tuple...  61 us
    pallas_call x4, Pallas kernels, weights(): pl.pallas_call(functools.partial(weights_kernel, rows, base, count, secon...  19.4 us
    ppermute x4, starting transfers between devices, swapped(): lax.ppermute(value, axis, [(source, source ^ distance) for source in rang...  8.82 us
    all_gather x3, blocking collectives, body(): gathered = lax.all_gather(part, 'tok', axis=0, tiled=False)  6.16 us
  transfers between devices with their start and end apart: 9, of which 1 were waited for; matrix products, arithmetic and copies ran while one was open for 0% of the time, Pallas kernels for 19%

profile of v6, /device:TPU:0, one launch (start us, length us, event | category | flops | bytes accessed | tf_op | source)
XLA Modules:
  0.0 99.5 jit_solution(15262208297777211729)
XLA Ops:
  0.6 4.1 %collective-permute-start = (f32[1,32,64]{2,1,0:T(8,128)}, f32[1,32,64]{2,1,0:T(8,128)S(1)}, u32[]{:S(2)}, u32[]{:S(2)}) collective-permute-start(f32[1,32,64]{2,1,0:T(8,128)} %param.10), channel_id=1, source_target_pairs={{0,16},{2,18},{4,20},{6,22},{8,24},{10,26},{12,28},{14,30},{16,0},... | collective-permute-start | bytes 24584 | tf_op jit(solution)/shard_map/ppermute | solution.py:355
  4.7 0.5 collective-permute-start.5
  5.3 0.5 collective-permute-start.4
  5.8 4.8 %weights.4.refs_3_ = f32[128,1536]{1,0:T(8,128)S(1)} custom-call(bf16[64,1536]{1,0:T(8,128)(2,1)} %refs_0_.6, bf16[19,1536]{1,0:T(8,128)(2,1)} %refs_1_.6, bf16[64,1536]{1,0:T(8,128)(2,1)} %bitcast.8, bf16[3,768,3072]{2,1,0:T(8,128)(2,1)} %refs_6_.3, bf16[768,3072]{1,0:T(8,128)(2,1)} %refs_7_.1), custom_call_target="tpu_custom_call" | custom-call | flops 603979776 | bytes 4718592 | tf_op jit(solution)/shard_map/weights/pallas_call | solution.py:388
  10.6 0.1 pad_maximum_fusion.3
  10.7 1.6 %collective-permute-start.2 = (f32[1,32,128]{2,1,0:T(8,128)S(1)}, f32[1,32,128]{2,1,0:T(8,128)S(1)}, u32[]{:S(2)}, u32[]{:S(2)}) collective-permute-start(f32[1,32,128]{2,1,0:T(8,128)S(1)} %pad_maximum_fusion.3), channel_id=1, source_target_pairs={{0,8},{2,10},{4,12},{6,14},{8,0},{10,2},{12,4},{14,6},{16,24},{18,... | collective-permute-start | bytes 49160 | tf_op jit(solution)/shard_map/ppermute | solution.py:355
  12.3 4.8 %weights.5 = (f32[128,768]{1,0:T(8,128)S(1)}, f32[64,768]{1,0:T(8,128)S(1)}, f32[192,128]{1,0:T(8,128)S(1)}) custom-call(bf16[64,1536]{1,0:T(8,128)(2,1)} %refs_0_.6, bf16[19,1536]{1,0:T(8,128)(2,1)} %refs_1_.6, bf16[64,1536]{1,0:T(8,128)(2,1)} %bitcast.9, bf16[3,768,3072]{2,1,0:T(8,128)(2,1)} %refs_6_.3, bf16[768,3072]{1,0:T(8,128)(2,1)} %refs_7_.1, ...), custom_call_target="tpu_custom_call" | custom-call | flops 603979776 | bytes 4718592 | tf_op jit(solution)/shard_map/weights/pallas_call | solution.py:388
  17.1 1.6 %collective-permute-start.3 = (f32[2,32,128]{2,1,0:T(8,128)S(1)}, f32[2,32,128]{2,1,0:T(8,128)S(1)}, u32[]{:S(2)}, u32[]{:S(2)}) collective-permute-start(f32[2,32,128]{2,1,0:T(8,128)S(1)} %pad_maximum_fusion.2), channel_id=1, source_target_pairs={{0,4},{2,6},{4,0},{6,2},{8,12},{10,14},{12,8},{14,10},{16,20},{18,... | collective-permute-start | bytes 98312 | tf_op jit(solution)/shard_map/ppermute | solution.py:355
  18.7 4.8 %weights.6 = (bf16[768,256]{1,0:T(8,128)(2,1)S(1)}, bf16[256,768]{1,0:T(8,128)(2,1)S(1)}) custom-call(bf16[64,1536]{1,0:T(8,128)(2,1)S(1)} %collective-permute-done.4.refs_0_, bf16[19,1536]{1,0:T(8,128)(2,1)S(1)} %collective-permute-done.5.refs_1_, bf16[64,1536]{1,0:T(8,128)(2,1)S(1)} %collective-permute-done.6.refs_2_, f32[128,1536]{1,0:T(8,128)S(1)} %weights.4.refs_3_, ...), custom_call_target="tpu_custom_call" | custom-call | flops 603979776 | bytes 4718592 | tf_op jit(solution)/shard_map/weights/pallas_call | solution.py:388
  23.5 0.0 copy-start
  23.6 0.0 copy-start.1
  23.6 0.0 copy-start.2
  23.6 0.0 copy-start.3
  23.6 1.6 %collective-permute-start.7 = (f32[4,32,128]{2,1,0:T(8,128)S(1)}, f32[4,32,128]{2,1,0:T(8,128)S(1)}, u32[]{:S(2)}, u32[]{:S(2)}) collective-permute-start(f32[4,32,128]{2,1,0:T(8,128)S(1)} %pad_maximum_fusion.1), channel_id=1, source_target_pairs={{0,2},{2,0},{4,6},{6,4},{8,10},{10,8},{12,14},{14,12},{16,18},{18,... | collective-permute-start | bytes 196616 | tf_op jit(solution)/shard_map/ppermute | solution.py:355
  25.2 4.9 %weights.7 = (bf16[768,256]{1,0:T(8,128)(2,1)S(1)}, bf16[128,768]{1,0:T(8,128)(2,1)S(1)}, bf16[192,256]{1,0:T(8,128)(2,1)S(1)}) custom-call(bf16[64,1536]{1,0:T(8,128)(2,1)S(1)} %collective-permute-done.4.refs_0_, bf16[19,1536]{1,0:T(8,128)(2,1)S(1)} %collective-permute-done.5.refs_1_, bf16[64,1536]{1,0:T(8,128)(2,1)S(1)} %collective-permute-done.6.refs_2_, ...), custom_call_target="tpu_custom_call" | custom-call | flops 603979776 | bytes 4718592 | tf_op jit(solution)/shard_map/weights/pallas_call | solution.py:388
  30.1 0.1 collective-permute-start.8
  30.2 1.3 %collective-permute-done.8.refs_3_ = f32[8,32,128]{2,1,0:T(8,128)S(1)} collective-permute-done((f32[8,32,128]{2,1,0:T(8,128)S(1)}, f32[8,32,128]{2,1,0:T(8,128)S(1)}, u32[]{:S(2)}, u32[]{:S(2)}) %collective-permute-start.8) | collective-permute-done | bytes 131104 | tf_op jit(solution)/shard_map/ppermute | solution.py:358
  31.6 34.4 %step0.1 = (f32[64,896]{1,0:T(8,128)S(1)}, f32[64,896]{1,0:T(8,128)S(1)}, f32[64,896]{1,0:T(8,128)S(1)}) custom-call(s32[16]{0:T(128)S(1)} %copy-done.2, s32[16]{0:T(128)S(1)} %copy-done.3, f32[8,32,128]{2,1,0:T(8,128)S(1)} %pad_maximum_fusion.refs_2_, f32[8,32,128]{2,1,0:T(8,128)S(1)} %collective-permute-done.8.refs_3_, ...), custom_call_target="tpu_custom_call" | custom-call | flops 2919235584 | bytes 786432 | tf_op jit(solution)/shard_map/step0/pallas_call | solution.py:449
  66.0 2.3 %all-gather = f32[128,896]{1,0:T(8,128)S(1)} all-gather(f32[64,896]{1,0:T(8,128)S(1)} %get-tuple-element.63), channel_id=2, replica_groups=mesh['queue'=16,'tok'=2] {'tok'}, dimensions={0}, use_global_device_ids=true | all-gather | bytes 688128 | tf_op jit(solution)/shard_map/all_gather | solution.py:472
  68.3 20.1 %step1.1 = (f32[64,512]{1,0:T(8,128)S(1)}, f32[64,512]{1,0:T(8,128)S(1)}, f32[64,512]{1,0:T(8,128)S(1)}, f32[32,64]{1,0:T(8,128)S(1)}) custom-call(s32[16]{0:T(128)S(1)} %copy-done.2, s32[16]{0:T(128)S(1)} %copy-done.3, f32[2,64,896]{2,1,0:T(8,128)S(1)} %bitcast.4, f32[64,896]{1,0:T(8,128)S(1)} %get-tuple-element.64.refs_3_, ...), custom_call_target="tpu_custom_call" | custom-call | flops 1862270976 | bytes 786432 | tf_op jit(solution)/shard_map/step1/pallas_call | solution.py:449
  88.4 2.0 %all-gather.1 = f32[128,512]{1,0:T(8,128)S(1)} all-gather(f32[64,512]{1,0:T(8,128)S(1)} %get-tuple-element.66), channel_id=3, replica_groups=mesh['queue'=16,'tok'=2] {'tok'}, dimensions={0}, use_global_device_ids=true | all-gather | bytes 393216 | tf_op jit(solution)/shard_map/all_gather | solution.py:472
  90.4 6.5 %step2.1 = (f32[64,128]{1,0:T(8,128)S(1)}, f32[64,128]{1,0:T(8,128)S(1)}, f32[64,128]{1,0:T(8,128)S(1)}, f32[32,64]{1,0:T(8,128)S(1)}) custom-call(s32[16]{0:T(128)S(1)} %copy-done.2, s32[16]{0:T(128)S(1)} %copy-done.3, f32[2,64,512]{2,1,0:T(8,128)S(1)} %bitcast.5, f32[64,512]{1,0:T(8,128)S(1)} %get-tuple-element.67.refs_3_, ...), custom_call_target="tpu_custom_call" | custom-call | flops 805306368 | bytes 786432 | tf_op jit(solution)/shard_map/step2/pallas_call | solution.py:449
  96.9 1.9 %all-gather.2 = f32[128,128]{1,0:T(8,128)S(1)} all-gather(f32[64,128]{1,0:T(8,128)S(1)} %get-tuple-element.69), channel_id=4, replica_groups=mesh['queue'=16,'tok'=2] {'tok'}, dimensions={0}, use_global_device_ids=true | all-gather | bytes 98304 | tf_op jit(solution)/shard_map/all_gather | solution.py:472
  98.8 0.7 last.1
  (19 shorter events, 0.1 us)
Async XLA Ops:
  0.6 10.0 %copy-start.4 = (f32[1,32,64]{2,1,0:T(8,128)S(1)}, f32[1,32,64]{2,1,0:T(8,128)}, u32[]{:S(2)}) copy-start(f32[1,32,64]{2,1,0:T(8,128)} %param.10) | copy-start | bytes 24580
  0.6 10.0 %collective-permute-start = (f32[1,32,64]{2,1,0:T(8,128)}, f32[1,32,64]{2,1,0:T(8,128)S(1)}, u32[]{:S(2)}, u32[]{:S(2)}) collective-permute-start(f32[1,32,64]{2,1,0:T(8,128)} %param.10), channel_id=1, source_target_pairs={{0,16},{2,18},{4,20},{6,22},{8,24},{10,26},{12,28},{14,30},{16,0},... | collective-permute-start | bytes 24584 | tf_op jit(solution)/shard_map/ppermute | solution.py:355
  4.7 5.9 %collective-permute-start.1 = (f32[3,32,64]{2,1,0:T(8,128)}, f32[3,32,64]{2,1,0:T(8,128)S(1)}, u32[]{:S(2)}, u32[]{:S(2)}) collective-permute-start(f32[3,32,64]{2,1,0:T(8,128)} %refs_5_.6), channel_id=1, source_target_pairs={{0,1},{1,0},{2,3},{3,2},{4,5},{5,4},{6,7},{7,6},{8,9},{9,8},{10,11... | collective-permute-start | bytes 73736 | tf_op jit(solution)/shard_map/ppermute | solution.py:358
  4.7 14.0 %collective-permute-start.5 = (bf16[19,1536]{1,0:T(8,128)(2,1)}, bf16[19,1536]{1,0:T(8,128)(2,1)S(1)}, u32[]{:S(2)}, u32[]{:S(2)}) collective-permute-start(bf16[19,1536]{1,0:T(8,128)(2,1)} %refs_1_.6), channel_id=1, source_target_pairs={{0,1},{1,0},{2,3},{3,2},{4,5},{5,4},{6,7},{7,6},{8,9},{9,8},{10,11... | collective-permute-start | bytes 175112 | tf_op jit(solution)/shard_map/ppermute | solution.py:358
  5.3 13.4 %collective-permute-start.6 = (bf16[64,1536]{1,0:T(8,128)(2,1)}, bf16[64,1536]{1,0:T(8,128)(2,1)S(1)}, u32[]{:S(2)}, u32[]{:S(2)}) collective-permute-start(bf16[64,1536]{1,0:T(8,128)(2,1)} %bitcast.7), channel_id=1, source_target_pairs={{0,1},{1,0},{2,3},{3,2},{4,5},{5,4},{6,7},{7,6},{8,9},{9,8},{10,11... | collective-permute-start | bytes 589832 | tf_op jit(solution)/shard_map/ppermute | solution.py:358
  5.3 13.4 %collective-permute-start.4 = (bf16[64,1536]{1,0:T(8,128)(2,1)}, bf16[64,1536]{1,0:T(8,128)(2,1)S(1)}, u32[]{:S(2)}, u32[]{:S(2)}) collective-permute-start(bf16[64,1536]{1,0:T(8,128)(2,1)} %refs_0_.6), channel_id=1, source_target_pairs={{0,1},{1,0},{2,3},{3,2},{4,5},{5,4},{6,7},{7,6},{8,9},{9,8},{10,11... | collective-permute-start | bytes 589832 | tf_op jit(solution)/shard_map/ppermute | solution.py:358
  10.7 6.4 %collective-permute-start.2 = (f32[1,32,128]{2,1,0:T(8,128)S(1)}, f32[1,32,128]{2,1,0:T(8,128)S(1)}, u32[]{:S(2)}, u32[]{:S(2)}) collective-permute-start(f32[1,32,128]{2,1,0:T(8,128)S(1)} %pad_maximum_fusion.3), channel_id=1, source_target_pairs={{0,8},{2,10},{4,12},{6,14},{8,0},{10,2},{12,4},{14,6},{16,24},{18,... | collective-permute-start | bytes 49160 | tf_op jit(solution)/shard_map/ppermute | solution.py:355
  17.1 6.5 %collective-permute-start.3 = (f32[2,32,128]{2,1,0:T(8,128)S(1)}, f32[2,32,128]{2,1,0:T(8,128)S(1)}, u32[]{:S(2)}, u32[]{:S(2)}) collective-permute-start(f32[2,32,128]{2,1,0:T(8,128)S(1)} %pad_maximum_fusion.2), channel_id=1, source_target_pairs={{0,4},{2,6},{4,0},{6,2},{8,12},{10,14},{12,8},{14,10},{16,20},{18,... | collective-permute-start | bytes 98312 | tf_op jit(solution)/shard_map/ppermute | solution.py:355
  23.5 8.0 %copy-start = (f32[3,32,64]{2,1,0:T(8,128)S(1)}, f32[3,32,64]{2,1,0:T(8,128)}, u32[]{:S(2)}) copy-start(f32[3,32,64]{2,1,0:T(8,128)} %refs_5_.6) | copy-start | bytes 73732
  23.6 8.0 %copy-start.1 = (f32[2,768]{1,0:T(2,128)S(1)}, f32[2,768]{1,0:T(2,128)}, u32[]{:S(2)}) copy-start(f32[2,768]{1,0:T(2,128)} %refs_5_.7) | copy-start | bytes 18436
  23.6 8.0 %copy-start.2 = (s32[16]{0:T(128)S(1)}, s32[16]{0:T(128)}, u32[]{:S(2)}) copy-start(s32[16]{0:T(128)} %refs_0_.9) | copy-start | bytes 196
  23.6 8.0 %copy-start.3 = (s32[16]{0:T(128)S(1)}, s32[16]{0:T(128)}, u32[]{:S(2)}) copy-start(s32[16]{0:T(128)} %refs_1_.9) | copy-start | bytes 196
  23.6 6.5 %collective-permute-start.7 = (f32[4,32,128]{2,1,0:T(8,128)S(1)}, f32[4,32,128]{2,1,0:T(8,128)S(1)}, u32[]{:S(2)}, u32[]{:S(2)}) collective-permute-start(f32[4,32,128]{2,1,0:T(8,128)S(1)} %pad_maximum_fusion.1), channel_id=1, source_target_pairs={{0,2},{2,0},{4,6},{6,4},{8,10},{10,8},{12,14},{14,12},{16,18},{18,... | collective-permute-start | bytes 196616 | tf_op jit(solution)/shard_map/ppermute | solution.py:355
  30.1 1.4 %collective-permute-start.8 = (f32[8,32,128]{2,1,0:T(8,128)S(1)}, f32[8,32,128]{2,1,0:T(8,128)S(1)}, u32[]{:S(2)}, u32[]{:S(2)}) collective-permute-start(f32[8,32,128]{2,1,0:T(8,128)S(1)} %pad_maximum_fusion.refs_2_), channel_id=1, source_target_pairs={{0,1},{1,0},{2,3},{3,2},{4,5},{5,4},{6,7},{7,6},{8,9},{9,8},{10,11... | collective-permute-start | bytes 393224 | tf_op jit(solution)/shard_map/ppermute | solution.py:358

commit v7 on v6

--- a/solution.py
+++ b/solution.py
@@ -12,7 +12,6 @@
 STEPS = 3
 HALO = 3
 LANES = 128
-AHEAD = 3
 EPS = 1e-06
 F32, BF16 = jnp.float32, jnp.bfloat16
 
@@ -47,71 +46,101 @@
             copies[place, at] = pltpu.make_async_copy(
                 source.at[pl.ds((chunk % per) * rows, rows), columns],
                 buf.at[at, place],
-                sems.at[at, place],
+                sems.at[place, at],
             )
     return copies
 
 
-def stack_rows(base, embed, level):
-    rows = [embed.astype(F32), level.astype(F32)]
-    rows.append(jnp.zeros((base - embed.shape[0] - level.shape[0], embed.shape[1]), F32))
-    return jnp.concatenate(rows, axis=0).astype(BF16)
-
-
-def halved_dot(a, b):
-    half = round_up(a.shape[1] // 2, LANES)
-    return dot_nt(a[:, :half], b[:, :half]) + dot_nt(a[:, half:], b[:, half:])
-
-
-def weights_kernel(rows, base, count, second, *refs):
-    shares = (0,) if count == 0 else tuple(range(1, count))
-    tables, refs = refs[: 3 * len(shares)], refs[3 * len(shares) :]
-    sums = ()
-    if count:
-        sums, refs = refs[: 3 if second else 1], refs[3 if second else 1 :]
-    qkv_hbm, out_hbm = refs[:2]
-    scratch = 5 + 1 if count == 0 else 2
-    outs, buf, sems = refs[-scratch - (3 if second else 1 + (count > 0)) : -scratch], refs[-2], refs[-1]
-    width = out_hbm.shape[0]
-    per = width // rows
-    chunks = range(2 * per, 4 * per) if second else range(2 * per)
-    if count == 0:
-        held, small = refs[-6:-3], refs[-3]
-        brought = [pltpu.make_async_copy(tables[at], held[at], small.at[at]) for at in range(3)]
-        for copy in brought:
-            copy.start()
-    copies = chunk_copies(rows, chunks, shares, qkv_hbm, out_hbm, buf, sems)
-    for key in copies:
-        if key[0] < AHEAD:
-            copies[key].start()
-    if count == 0:
+def started(sources, targets, sems):
+    copies = [pltpu.make_async_copy(a, b, sems.at[i]) for i, (a, b) in enumerate(zip(sources, targets))]
+    for copy in copies:
+        copy.start()
+    return copies
+
+
+def turned(value):
+    return value.astype(F32).T.astype(BF16)
+
+
+def keys_kernel(rows, base, shares, *refs):
+    own, count = shares == (0,), len(shares)
+    tables, refs = refs[: 2 * count], refs[2 * count :]
+    if own:
+        qkv_hbm, out_hbm = refs[:2]
+        total_ref, gram_ref, right_ref, embed, level, small, buf, sems = refs[-8:]
+        brought = started(tables, (embed, level), small)
+    else:
+        sum_ref, gram_sum, qkv_hbm, out_hbm = refs[:4]
+        mq_ref, mk_ref, gram_ref, right_ref, buf, sems = refs[-6:]
+    per = out_hbm.shape[0] // rows
+    depth = buf.shape[-1]
+    copies = chunk_copies(rows, range(2 * per), shares, qkv_hbm, out_hbm, buf, sems)
+    for copy in copies.values():
+        copy.start()
+    if own:
         for copy in brought:
             copy.wait()
-        tables = held
-    lefts = [stack_rows(base, tables[3 * at][...], tables[3 * at + 1][...]) for at in range(len(shares))]
-    vels = [tables[3 * at + 2][...] for at in range(len(shares))]
-    if second:
-        gram = sum(dot_nt(jnp.concatenate([left, vel], axis=0), left) for left, vel in zip(lefts, vels))
-        outs[2][...] = halves(sums[2][...] + gram, 1) if count else gram
-    for place, chunk in enumerate(chunks):
-        for at in range(len(shares)):
+        tables = (embed, level)
+    gram = jnp.zeros((base, base), F32) if own else gram_sum[...]
+    for at in range(count):
+        left = [tables[2 * at][...].astype(F32), tables[2 * at + 1][...].astype(F32)]
+        left.append(jnp.zeros((base - left[0].shape[0] - left[1].shape[0], depth), F32))
+        left = jnp.concatenate(left, axis=0)
+        right_ref[at * depth : (at + 1) * depth, :] = left.T.astype(BF16)
+        gram = gram + dot(left.astype(BF16), right_ref[at * depth : (at + 1) * depth, :])
+    gram_ref[...] = gram if own else halves(gram, 1)
+    for chunk in range(2 * per):
+        spot = slice(chunk * rows, (chunk + 1) * rows)
+        total = None if own else sum_ref[spot, :]
+        for at in range(count):
+            copies[chunk, at].wait()
+            product = dot(buf[at, chunk], right_ref[at * depth : (at + 1) * depth, :])
+            total = product if total is None else total + product
+        where = slice((chunk % per) * rows, (chunk % per + 1) * rows)
+        if own:
+            total_ref[spot, :] = total
+        elif chunk < per:
+            mq_ref[where, :] = halves(total, 1)
+        else:
+            mk_ref[:, where] = halves(total.T, 0)
+
+
+def values_kernel(rows, shares, *refs):
+    own, count = shares == (0,), len(shares)
+    tables, right_ref, refs = refs[:count], refs[count], refs[count + 1 :]
+    if own:
+        qkv_hbm, out_hbm = refs[:2]
+        mv_ref, wo_ref, gv_ref, held, small, buf, sems = refs[-7:]
+        brought = started(tables, (held,), small)
+    else:
+        mv_sum, wo_sum, gv_sum, qkv_hbm, out_hbm = refs[:5]
+        mv_ref, wo_ref, gv_ref, buf, sems = refs[-5:]
+    per = out_hbm.shape[0] // rows
+    depth = buf.shape[-1]
+    copies = chunk_copies(rows, range(2 * per, 4 * per), shares, qkv_hbm, out_hbm, buf, sems)
+    for copy in copies.values():
+        copy.start()
+    if own:
+        brought[0].wait()
+        tables = (held,)
+    vels = [table[...] for table in tables]
+    gv = sum(dot(vel, right_ref[at * depth : (at + 1) * depth, :]) for at, vel in enumerate(vels))
+    gv_ref[...] = gv if own else halves(gv_sum[...] + gv, 1)
+    downs = [turned(vel) for vel in vels]
+    for place in range(2 * per):
+        where = slice((place % per) * rows, (place % per + 1) * rows)
+        total = None if own else (mv_sum if place < per else wo_sum)[where, :]
+        for at in range(count):
             copies[place, at].wait()
-            if place + AHEAD < len(chunks):
-                copies[place + AHEAD, at].start()
-        last = chunk // per == 3
-        total = sum(halved_dot(vels[at] if last else lefts[at], buf[at, place]) for at in range(len(shares)))
-        spot = slice(place * rows, (place + 1) * rows)
-        if last:
-            spot = slice((place - per) * rows, (place - per + 1) * rows)
-        if count == 0:
-            outs[1 if last else 0][:, spot] = total
-            continue
-        total = total + sums[1 if last else 0][:, spot]
-        where = slice((chunk % per) * rows, (chunk % per + 1) * rows)
-        if chunk // per % 2:
-            outs[1][:, where] = halves(total, 0)
+            right = right_ref[at * depth : (at + 1) * depth, :] if place < per else downs[at]
+            product = dot(buf[at, place], right)
+            total = product if total is None else total + product
+        if own:
+            (mv_ref if place < per else wo_ref)[where, :] = total
+        elif place < per:
+            mv_ref[where, :] = halves(total, 1)
         else:
-            outs[0][where, :] = halves(total.T, 1)
+            wo_ref[:, where] = halves(total.T, 0)
 
 
 def advance(level_count, tok, first, g_ref, hpart_ref, xq_ref):
@@ -153,8 +182,8 @@
     fresh_ref = None
     if step < STEPS - 1:
         fresh_ref = refs.pop(0)
-    gain_ref, mq_ref, mk_ref, mv_ref, wo_ref, gram_ref = refs[:6]
-    refs = refs[6:]
+    gain_ref, mq_ref, mk_ref, mv_ref, wo_ref, gram_ref, gv_ref = refs[:7]
+    refs = refs[7:]
     part_ref, hpart_ref, xq_ref = refs[:3]
     refs = refs[3:]
     own_ref = None
@@ -192,7 +221,7 @@
     aug_t = aug_t.astype(BF16).astype(F32)
     aug_tb = aug_t.astype(BF16)
     both_t = jnp.concatenate([aug_tb, aug_tb], axis=0)
-    mean_t = jnp.sum(dot(gram_ref[:base, :], both_t) * aug_t, axis=0, keepdims=True) * (1.0 / depth)
+    mean_t = jnp.sum(dot(gram_ref[...], both_t) * aug_t, axis=0, keepdims=True) * (1.0 / depth)
     mean_t = jnp.maximum(mean_t, 0.0) + EPS
     queries = slice(HALO * tok, HALO * tok + query_lanes)
     mean_q = mean_t[:, queries]
@@ -204,7 +233,7 @@
     aug_b = aug.astype(BF16)
     both = jnp.concatenate([aug_b, aug_b], axis=1)
 
-    hpart_ref[...] = dot(gram_ref[base:, :], both_q)
+    hpart_ref[...] = dot(gv_ref[...], both_q)
     xq_ref[...] = state[:, queries]
 
     gain = gain_ref[0:1, :] * gain_ref[1:2, :] * (HD ** -0.5 * math.log2(math.e))
@@ -359,54 +388,72 @@
 
     share = depth // parts
     table = (embed_weight, level_embed, vel_weight.T)
-    tables = [from_ahead(piece, d) for d in range(1, parts) for piece in table]
-    noise = [from_ahead(fresh_noise, d) for d in range(1, parts)]
+    around = range(1, parts)
+    tables = [from_ahead(piece, d) for d in around for piece in table[:2]]
+    vel_tables = [from_ahead(table[2], d) for d in around]
+    noise = [from_ahead(fresh_noise, d) for d in around]
     in_hbm = lambda array: pltpu.with_memory_space_constraint(array, pltpu.HBM)
     table = tuple(in_hbm(piece) for piece in table)
     qkv_weight, out_weight = in_hbm(qkv_weight), in_hbm(out_weight)
-    rows = 256
+    rows = 384 if width % 384 == 0 else 256
     chunks = 2 * width // rows
 
-    def weights(count, second, after, *operands):
-        shares = max(1, count - 1)
-        if count == 0 and second:
-            outs = [shape((base, width), F32), shape((channels, width), F32), shape((base + channels, base), F32)]
-        elif count == 0:
-            outs = [shape((base, 2 * width), F32)]
-        elif second:
-            outs = [
-                shape((width, 2 * base), BF16),
-                shape((2 * channels, width), BF16),
-                shape((base + channels, 2 * base), BF16),
-            ]
-        else:
-            outs = [shape((width, 2 * base), BF16), shape((2 * base, width), BF16)]
-        scratch = [pltpu.VMEM((shares, chunks, rows, share), BF16), pltpu.SemaphoreType.DMA((shares, chunks))]
-        if count == 0:
-            held = [pltpu.VMEM(piece.shape, BF16) for piece in table]
-            scratch = held + [pltpu.SemaphoreType.DMA((3,))] + scratch
+    def weights(kernel, shares, outs, held, after, *operands):
+        count = len(shares)
+        scratch = [pltpu.VMEM(piece.shape, BF16) for piece in held]
+        if held:
+            scratch.append(pltpu.SemaphoreType.DMA((len(held),)))
+        scratch += [pltpu.VMEM((count, chunks, rows, share), BF16), pltpu.SemaphoreType.DMA((chunks, count))]
         return pl.pallas_call(
-            functools.partial(weights_kernel, rows, base, count, second),
+            functools.partial(kernel, shares),
             out_shape=tuple(outs),
-            in_specs=[hbm if count == 0 else vmem] * len(operands) + [hbm] * 2 + [anywhere] * len(after),
+            in_specs=[hbm] * len(held)
+            + [vmem] * (len(operands) - len(held))
+            + [hbm] * 2
+            + [anywhere] * len(after),
             out_specs=(vmem,) * len(outs),
             scratch_shapes=scratch,
             compiler_params=pltpu.CompilerParams(vmem_limit_bytes=24 * 2**20),
             cost_estimate=pl.CostEstimate(
-                flops=4 * base * width * share * shares,
-                bytes_accessed=4 * width * share * shares,
+                flops=4 * base * width * share * count,
+                bytes_accessed=4 * width * share * count,
                 transcendentals=0,
             ),
             name="weights",
         )(*operands, qkv_weight, out_weight, *after)
 
+    keys_part = lambda shares, *refs: keys_kernel(rows, base, shares, *refs)
+    values_part = lambda shares, *refs: values_kernel(rows, shares, *refs)
+    right = lambda count: shape((count * share, base), BF16)
+    others = tuple(around)
+
+    def own_keys(*after):
+        outs = [shape((2 * width, base), F32), shape((base, base), F32), right(1)]
+        return weights(keys_part, (0,), outs, table[:2], after, *table[:2])
+
+    def own_values(*after):
+        outs = [shape((width, base), F32), shape((width, channels), F32), shape((channels, base), F32)]
+        return weights(values_part, (0,), outs, table[2:], after, table[2], done[0][2])
+
+    def other_keys(*after):
+        outs = [
+            shape((width, 2 * base), BF16),
+            shape((2 * base, width), BF16),
+            shape((base, 2 * base), BF16),
+            right(parts - 1),
+        ]
+        return weights(keys_part, others, outs, (), after, *tables, *done[0][:2])
+
+    def other_values(*after):
+        outs = [
+            shape((width, 2 * base), BF16),
+            shape((2 * channels, width), BF16),
+            shape((channels, 2 * base), BF16),
+        ]
+        return weights(values_part, others, outs, (), after, *vel_tables, done[2][3], *done[1])
+
     state = latent
-    work = [
-        lambda *after: weights(0, False, after, *table),
-        lambda *after: weights(0, True, after, *table),
-        lambda *after: weights(parts, False, after, *tables, *done[0]),
-        lambda *after: weights(parts, True, after, *tables, *done[1]),
-    ]
+    work = [own_keys, own_values, other_keys, other_values]
     done, after = [], ()
     distance = frames // 2
     while distance:
@@ -421,8 +468,8 @@
     while len(done) < len(work):
         done.append(work[len(done)]())
     latents = [state] + [from_ahead(state, d) for d in range(1, parts)] + noise
-    mq, mk = done[2]
-    mv, wo, gram = done[3]
+    mq, mk, gram = done[2][:3]
+    mv, wo, gv = done[3]
 
     query_block = max(1, LANES // tok)
     owned = []
@@ -440,8 +487,8 @@
         if step < STEPS - 1:
             args += [fresh_noise]
             specs += [vmem]
-        args += [qk_gain, mq, mk, mv, wo, gram]
-        specs += [vmem] * 6
+        args += [qk_gain, mq, mk, mv, wo, gram, gv]
+        specs += [vmem] * 7
         outs = [shape((channels, query_lanes), F32)] * 3
         if step > 0:
             outs += [shape((part_rows, channels), F32)]

time: 99.7 us -> 96 us (0.963)
  Pallas kernels: 81.1 us -> 77.9 us
    pallas_call x4, Pallas kernels: 19.4 us -> 16 us  [weights(): pl.pallas_call(functools.partial(kernel, shares), out_shape=tuple(outs),...]
  transfers between devices with their start and end apart: 9 -> 9, of which waited for: 1 -> 1; matrix products, arithmetic and copies ran while one was open for 0% -> 0% of each run, Pallas kernels for 19% -> 17%
where the time goes in v7:
time: 96 us; the launch traced here: 95.9 us
  Pallas kernels  77.9 us (81%)
  starting transfers between devices  9.65 us (10%)
  blocking collectives  5.98 us (6%)
  waiting for transfers between devices  1.36 us (1%)
    pallas_call x3, Pallas kernels, body(): pl.pallas_call(functools.partial(step_kernel, step, cfg), out_shape=tuple...  61.2 us
    pallas_call x4, Pallas kernels, weights(): pl.pallas_call(functools.partial(kernel, shares), out_shape=tuple(outs),...  16 us
    ppermute x4, starting transfers between devices, swapped(): lax.ppermute(value, axis, [(source, source ^ distance) for source in rang...  8.39 us
    all_gather x3, blocking collectives, body(): gathered = lax.all_gather(part, 'tok', axis=0, tiled=False)  5.98 us
  transfers between devices with their start and end apart: 9, of which 1 were waited for; matrix products, arithmetic and copies ran while one was open for 0% of the time, Pallas kernels for 17%

profile of v7, /device:TPU:0, one launch (start us, length us, event | category | flops | bytes accessed | tf_op | source)
XLA Modules:
  0.0 95.9 jit_solution(1289802314939827510)
XLA Ops:
  0.6 0.5 collective-permute-start.1
  1.2 3.7 %collective-permute-start = (f32[1,32,64]{2,1,0:T(8,128)}, f32[1,32,64]{2,1,0:T(8,128)S(1)}, u32[]{:S(2)}, u32[]{:S(2)}) collective-permute-start(f32[1,32,64]{2,1,0:T(8,128)} %param.10), channel_id=1, source_target_pairs={{0,16},{2,18},{4,20},{6,22},{8,24},{10,26},{12,28},{14,30},{16,0},... | collective-permute-start | bytes 24584 | tf_op jit(solution)/shard_map/ppermute | solution.py:384
  4.8 0.2 collective-permute-start.4
  5.0 0.3 collective-permute-start.5
  5.3 0.2 collective-permute-start.7
  5.5 4.5 %weights.4 = (f32[1536,128]{1,0:T(8,128)S(1)}, f32[128,128]{1,0:T(8,128)S(1)}, bf16[1536,128]{1,0:T(8,128)(2,1)S(1)}) custom-call(bf16[64,1536]{1,0:T(8,128)(2,1)} %refs_0_.4, bf16[19,1536]{1,0:T(8,128)(2,1)} %refs_1_.4, bf16[3,768,3072]{2,1,0:T(8,128)(2,1)} %refs_5_.6, bf16[768,3072]{1,0:T(8,128)(2,1)} %refs_6_.3), custom_call_target="tpu_custom_call" | custom-call | flops 603979776 | bytes 4718592 | tf_op jit(solution)/shard_map/weights/pallas_call | solution.py:407
  10.0 0.1 pad_maximum_fusion.3
  10.1 1.6 %collective-permute-start.2 = (f32[1,32,128]{2,1,0:T(8,128)S(1)}, f32[1,32,128]{2,1,0:T(8,128)S(1)}, u32[]{:S(2)}, u32[]{:S(2)}) collective-permute-start(f32[1,32,128]{2,1,0:T(8,128)S(1)} %pad_maximum_fusion.3), channel_id=1, source_target_pairs={{0,8},{2,10},{4,12},{6,14},{8,0},{10,2},{12,4},{14,6},{16,24},{18,... | collective-permute-start | bytes 49160 | tf_op jit(solution)/shard_map/ppermute | solution.py:384
  11.7 4.4 %weights.5 = (f32[768,128]{1,0:T(8,128)S(1)}, f32[768,64]{1,0:T(8,128)S(1)}, f32[64,128]{1,0:T(8,128)S(1)}) custom-call(bf16[64,1536]{1,0:T(8,128)(2,1)} %bitcast.8, bf16[1536,128]{1,0:T(8,128)(2,1)S(1)} %get-tuple-element.52.refs_1_, bf16[3,768,3072]{2,1,0:T(8,128)(2,1)} %refs_5_.6, bf16[768,3072]{1,0:T(8,128)(2,1)} %refs_6_.3, ...), custom_call_target="tpu_custom_call" | custom-call | flops 603979776 | bytes 4718592 | tf_op jit(solution)/shard_map/weights/pallas_call | solution.py:407
  16.2 1.6 %collective-permute-start.3 = (f32[2,32,128]{2,1,0:T(8,128)S(1)}, f32[2,32,128]{2,1,0:T(8,128)S(1)}, u32[]{:S(2)}, u32[]{:S(2)}) collective-permute-start(f32[2,32,128]{2,1,0:T(8,128)S(1)} %pad_maximum_fusion.2), channel_id=1, source_target_pairs={{0,4},{2,6},{4,0},{6,2},{8,12},{10,14},{12,8},{14,10},{16,20},{18,... | collective-permute-start | bytes 98312 | tf_op jit(solution)/shard_map/ppermute | solution.py:384
  17.8 3.7 %weights.6 = (bf16[768,256]{1,0:T(8,128)(2,1)S(1)}, bf16[256,768]{1,0:T(8,128)(2,1)S(1)}, bf16[128,256]{1,0:T(8,128)(2,1)S(1)}, bf16[1536,128]{1,0:T(8,128)(2,1)S(1)}) custom-call(bf16[64,1536]{1,0:T(8,128)(2,1)S(1)} %collective-permute-done.4.refs_0_, bf16[19,1536]{1,0:T(8,128)(2,1)S(1)} %collective-permute-done.5.refs_1_, ...), custom_call_target="tpu_custom_call" | custom-call | flops 603979776 | bytes 4718592 | tf_op jit(solution)/shard_map/weights/pallas_call | solution.py:407
  21.5 0.0 copy-start.2
  21.5 0.0 copy-start.3
  21.5 1.6 %collective-permute-start.6 = (f32[4,32,128]{2,1,0:T(8,128)S(1)}, f32[4,32,128]{2,1,0:T(8,128)S(1)}, u32[]{:S(2)}, u32[]{:S(2)}) collective-permute-start(f32[4,32,128]{2,1,0:T(8,128)S(1)} %pad_maximum_fusion.1), channel_id=1, source_target_pairs={{0,2},{2,0},{4,6},{6,4},{8,10},{10,8},{12,14},{14,12},{16,18},{18,... | collective-permute-start | bytes 196616 | tf_op jit(solution)/shard_map/ppermute | solution.py:384
  23.1 3.4 %weights.7 = (bf16[768,256]{1,0:T(8,128)(2,1)S(1)}, bf16[128,768]{1,0:T(8,128)(2,1)S(1)}, bf16[64,256]{1,0:T(8,128)(2,1)S(1)}) custom-call(bf16[64,1536]{1,0:T(8,128)(2,1)S(1)} %collective-permute-done.7.refs_0_, bf16[1536,128]{1,0:T(8,128)(2,1)S(1)} %get-tuple-element.66.refs_1_, f32[768,128]{1,0:T(8,128)S(1)} %get-tuple-element.67.refs_2_, ...), custom_call_target="tpu_custom_call" | custom-call | flops 603979776 | bytes 4718592 | tf_op jit(solution)/shard_map/weights/pallas_call | solution.py:407
  26.5 0.1 collective-permute-start.8
  26.6 1.3 %collective-permute-done.8.refs_3_ = f32[8,32,128]{2,1,0:T(8,128)S(1)} collective-permute-done((f32[8,32,128]{2,1,0:T(8,128)S(1)}, f32[8,32,128]{2,1,0:T(8,128)S(1)}, u32[]{:S(2)}, u32[]{:S(2)}) %collective-permute-start.8) | collective-permute-done | bytes 131104 | tf_op jit(solution)/shard_map/ppermute | solution.py:387
  28.0 34.6 %step0.1 = (f32[64,896]{1,0:T(8,128)S(1)}, f32[64,896]{1,0:T(8,128)S(1)}, f32[64,896]{1,0:T(8,128)S(1)}) custom-call(s32[16]{0:T(128)S(1)} %copy-done.2, s32[16]{0:T(128)S(1)} %copy-done.3, f32[8,32,128]{2,1,0:T(8,128)S(1)} %pad_maximum_fusion.refs_2_, f32[8,32,128]{2,1,0:T(8,128)S(1)} %collective-permute-done.8.refs_3_, ...), custom_call_target="tpu_custom_call" | custom-call | flops 2919235584 | bytes 786432 | tf_op jit(solution)/shard_map/step0/pallas_call | solution.py:496
  62.5 2.1 %all-gather = f32[128,896]{1,0:T(8,128)S(1)} all-gather(f32[64,896]{1,0:T(8,128)S(1)} %get-tuple-element.81), channel_id=2, replica_groups=mesh['queue'=16,'tok'=2] {'tok'}, dimensions={0}, use_global_device_ids=true | all-gather | bytes 688128 | tf_op jit(solution)/shard_map/all_gather | solution.py:519
  64.7 20.1 %step1.1 = (f32[64,512]{1,0:T(8,128)S(1)}, f32[64,512]{1,0:T(8,128)S(1)}, f32[64,512]{1,0:T(8,128)S(1)}, f32[32,64]{1,0:T(8,128)S(1)}) custom-call(s32[16]{0:T(128)S(1)} %copy-done.2, s32[16]{0:T(128)S(1)} %copy-done.3, f32[2,64,896]{2,1,0:T(8,128)S(1)} %bitcast.4, f32[64,896]{1,0:T(8,128)S(1)} %get-tuple-element.82.refs_3_, ...), custom_call_target="tpu_custom_call" | custom-call | flops 1862270976 | bytes 786432 | tf_op jit(solution)/shard_map/step1/pallas_call | solution.py:496
  84.8 2.0 %all-gather.1 = f32[128,512]{1,0:T(8,128)S(1)} all-gather(f32[64,512]{1,0:T(8,128)S(1)} %get-tuple-element.84), channel_id=3, replica_groups=mesh['queue'=16,'tok'=2] {'tok'}, dimensions={0}, use_global_device_ids=true | all-gather | bytes 393216 | tf_op jit(solution)/shard_map/all_gather | solution.py:519
  86.8 6.5 %step2.1 = (f32[64,128]{1,0:T(8,128)S(1)}, f32[64,128]{1,0:T(8,128)S(1)}, f32[64,128]{1,0:T(8,128)S(1)}, f32[32,64]{1,0:T(8,128)S(1)}) custom-call(s32[16]{0:T(128)S(1)} %copy-done.2, s32[16]{0:T(128)S(1)} %copy-done.3, f32[2,64,512]{2,1,0:T(8,128)S(1)} %bitcast.5, f32[64,512]{1,0:T(8,128)S(1)} %get-tuple-element.85.refs_3_, ...), custom_call_target="tpu_custom_call" | custom-call | flops 805306368 | bytes 786432 | tf_op jit(solution)/shard_map/step2/pallas_call | solution.py:496
  93.3 1.9 %all-gather.2 = f32[128,128]{1,0:T(8,128)S(1)} all-gather(f32[64,128]{1,0:T(8,128)S(1)} %get-tuple-element.87), channel_id=4, replica_groups=mesh['queue'=16,'tok'=2] {'tok'}, dimensions={0}, use_global_device_ids=true | all-gather | bytes 98304 | tf_op jit(solution)/shard_map/all_gather | solution.py:519
  95.1 0.7 last.1
  (19 shorter events, 0.1 us)
Async XLA Ops:
  0.6 9.4 %copy-start.4 = (f32[1,32,64]{2,1,0:T(8,128)S(1)}, f32[1,32,64]{2,1,0:T(8,128)}, u32[]{:S(2)}) copy-start(f32[1,32,64]{2,1,0:T(8,128)} %param.10) | copy-start | bytes 24580
  0.6 9.4 %collective-permute-start.1 = (f32[3,32,64]{2,1,0:T(8,128)}, f32[3,32,64]{2,1,0:T(8,128)S(1)}, u32[]{:S(2)}, u32[]{:S(2)}) collective-permute-start(f32[3,32,64]{2,1,0:T(8,128)} %refs_5_.8), channel_id=1, source_target_pairs={{0,1},{1,0},{2,3},{3,2},{4,5},{5,4},{6,7},{7,6},{8,9},{9,8},{10,11... | collective-permute-start | bytes 73736 | tf_op jit(solution)/shard_map/ppermute | solution.py:387
  1.2 8.8 %collective-permute-start = (f32[1,32,64]{2,1,0:T(8,128)}, f32[1,32,64]{2,1,0:T(8,128)S(1)}, u32[]{:S(2)}, u32[]{:S(2)}) collective-permute-start(f32[1,32,64]{2,1,0:T(8,128)} %param.10), channel_id=1, source_target_pairs={{0,16},{2,18},{4,20},{6,22},{8,24},{10,26},{12,28},{14,30},{16,0},... | collective-permute-start | bytes 24584 | tf_op jit(solution)/shard_map/ppermute | solution.py:384
  4.8 12.9 %collective-permute-start.4 = (bf16[64,1536]{1,0:T(8,128)(2,1)}, bf16[64,1536]{1,0:T(8,128)(2,1)S(1)}, u32[]{:S(2)}, u32[]{:S(2)}) collective-permute-start(bf16[64,1536]{1,0:T(8,128)(2,1)} %refs_0_.4), channel_id=1, source_target_pairs={{0,1},{1,0},{2,3},{3,2},{4,5},{5,4},{6,7},{7,6},{8,9},{9,8},{10,11... | collective-permute-start | bytes 589832 | tf_op jit(solution)/shard_map/ppermute | solution.py:387
  5.0 12.8 %collective-permute-start.5 = (bf16[19,1536]{1,0:T(8,128)(2,1)}, bf16[19,1536]{1,0:T(8,128)(2,1)S(1)}, u32[]{:S(2)}, u32[]{:S(2)}) collective-permute-start(bf16[19,1536]{1,0:T(8,128)(2,1)} %refs_1_.4), channel_id=1, source_target_pairs={{0,1},{1,0},{2,3},{3,2},{4,5},{5,4},{6,7},{7,6},{8,9},{9,8},{10,11... | collective-permute-start | bytes 175112 | tf_op jit(solution)/shard_map/ppermute | solution.py:387
  5.3 17.7 %collective-permute-start.7 = (bf16[64,1536]{1,0:T(8,128)(2,1)}, bf16[64,1536]{1,0:T(8,128)(2,1)S(1)}, u32[]{:S(2)}, u32[]{:S(2)}) collective-permute-start(bf16[64,1536]{1,0:T(8,128)(2,1)} %bitcast.7), channel_id=1, source_target_pairs={{0,1},{1,0},{2,3},{3,2},{4,5},{5,4},{6,7},{7,6},{8,9},{9,8},{10,11... | collective-permute-start | bytes 589832 | tf_op jit(solution)/shard_map/ppermute | solution.py:387
  10.1 6.0 %collective-permute-start.2 = (f32[1,32,128]{2,1,0:T(8,128)S(1)}, f32[1,32,128]{2,1,0:T(8,128)S(1)}, u32[]{:S(2)}, u32[]{:S(2)}) collective-permute-start(f32[1,32,128]{2,1,0:T(8,128)S(1)} %pad_maximum_fusion.3), channel_id=1, source_target_pairs={{0,8},{2,10},{4,12},{6,14},{8,0},{10,2},{12,4},{14,6},{16,24},{18,... | collective-permute-start | bytes 49160 | tf_op jit(solution)/shard_map/ppermute | solution.py:384
  16.2 5.3 %collective-permute-start.3 = (f32[2,32,128]{2,1,0:T(8,128)S(1)}, f32[2,32,128]{2,1,0:T(8,128)S(1)}, u32[]{:S(2)}, u32[]{:S(2)}) collective-permute-start(f32[2,32,128]{2,1,0:T(8,128)S(1)} %pad_maximum_fusion.2), channel_id=1, source_target_pairs={{0,4},{2,6},{4,0},{6,2},{8,12},{10,14},{12,8},{14,10},{16,20},{18,... | collective-permute-start | bytes 98312 | tf_op jit(solution)/shard_map/ppermute | solution.py:384
  21.4 6.5 %copy-start = (f32[3,32,64]{2,1,0:T(8,128)S(1)}, f32[3,32,64]{2,1,0:T(8,128)}, u32[]{:S(2)}) copy-start(f32[3,32,64]{2,1,0:T(8,128)} %refs_5_.8) | copy-start | bytes 73732
  21.4 6.5 %copy-start.1 = (f32[2,768]{1,0:T(2,128)S(1)}, f32[2,768]{1,0:T(2,128)}, u32[]{:S(2)}) copy-start(f32[2,768]{1,0:T(2,128)} %refs_5_.9) | copy-start | bytes 18436
  21.5 6.5 %copy-start.2 = (s32[16]{0:T(128)S(1)}, s32[16]{0:T(128)}, u32[]{:S(2)}) copy-start(s32[16]{0:T(128)} %refs_0_.7) | copy-start | bytes 196
  21.5 6.5 %copy-start.3 = (s32[16]{0:T(128)S(1)}, s32[16]{0:T(128)}, u32[]{:S(2)}) copy-start(s32[16]{0:T(128)} %refs_1_.7) | copy-start | bytes 196
  21.5 5.0 %collective-permute-start.6 = (f32[4,32,128]{2,1,0:T(8,128)S(1)}, f32[4,32,128]{2,1,0:T(8,128)S(1)}, u32[]{:S(2)}, u32[]{:S(2)}) collective-permute-start(f32[4,32,128]{2,1,0:T(8,128)S(1)} %pad_maximum_fusion.1), channel_id=1, source_target_pairs={{0,2},{2,0},{4,6},{6,4},{8,10},{10,8},{12,14},{14,12},{16,18},{18,... | collective-permute-start | bytes 196616 | tf_op jit(solution)/shard_map/ppermute | solution.py:384
  26.5 1.4 %collective-permute-start.8 = (f32[8,32,128]{2,1,0:T(8,128)S(1)}, f32[8,32,128]{2,1,0:T(8,128)S(1)}, u32[]{:S(2)}, u32[]{:S(2)}) collective-permute-start(f32[8,32,128]{2,1,0:T(8,128)S(1)} %pad_maximum_fusion.refs_2_), channel_id=1, source_target_pairs={{0,1},{1,0},{2,3},{3,2},{4,5},{5,4},{6,7},{7,6},{8,9},{9,8},{10,11... | collective-permute-start | bytes 393224 | tf_op jit(solution)/shard_map/ppermute | solution.py:387

commit v8 on v6

--- a/solution.py
+++ b/solution.py
@@ -12,7 +12,6 @@
 STEPS = 3
 HALO = 3
 LANES = 128
-AHEAD = 3
 EPS = 1e-06
 F32, BF16 = jnp.float32, jnp.bfloat16
 
@@ -35,83 +34,73 @@
     return jnp.concatenate([high, low], axis=axis)
 
 
-def chunk_copies(rows, chunks, parts, qkv_hbm, out_hbm, buf, sems):
-    per = out_hbm.shape[0] // rows
-    depth = buf.shape[-1]
-    index, count = lax.axis_index("tok"), lax.axis_size("tok")
-    copies = {}
-    for place, chunk in enumerate(chunks):
-        source = qkv_hbm.at[chunk // per] if chunk < 3 * per else out_hbm
-        for at, part in enumerate(parts):
-            columns = pl.ds(pl.multiple_of(lax.rem(index + part, count) * depth, LANES), depth)
-            copies[place, at] = pltpu.make_async_copy(
-                source.at[pl.ds((chunk % per) * rows, rows), columns],
-                buf.at[at, place],
-                sems.at[at, place],
-            )
+def started(sources, targets, sems):
+    copies = [pltpu.make_async_copy(a, b, sems.at[i]) for i, (a, b) in enumerate(zip(sources, targets))]
+    for copy in copies:
+        copy.start()
     return copies
 
 
-def stack_rows(base, embed, level):
-    rows = [embed.astype(F32), level.astype(F32)]
-    rows.append(jnp.zeros((base - embed.shape[0] - level.shape[0], embed.shape[1]), F32))
-    return jnp.concatenate(rows, axis=0).astype(BF16)
-
-
-def halved_dot(a, b):
-    half = round_up(a.shape[1] // 2, LANES)
-    return dot_nt(a[:, :half], b[:, :half]) + dot_nt(a[:, half:], b[:, half:])
-
-
-def weights_kernel(rows, base, count, second, *refs):
-    shares = (0,) if count == 0 else tuple(range(1, count))
-    tables, refs = refs[: 3 * len(shares)], refs[3 * len(shares) :]
-    sums = ()
-    if count:
-        sums, refs = refs[: 3 if second else 1], refs[3 if second else 1 :]
-    qkv_hbm, out_hbm = refs[:2]
-    scratch = 5 + 1 if count == 0 else 2
-    outs, buf, sems = refs[-scratch - (3 if second else 1 + (count > 0)) : -scratch], refs[-2], refs[-1]
-    width = out_hbm.shape[0]
-    per = width // rows
-    chunks = range(2 * per, 4 * per) if second else range(2 * per)
-    if count == 0:
-        held, small = refs[-6:-3], refs[-3]
-        brought = [pltpu.make_async_copy(tables[at], held[at], small.at[at]) for at in range(3)]
-        for copy in brought:
-            copy.start()
-    copies = chunk_copies(rows, chunks, shares, qkv_hbm, out_hbm, buf, sems)
-    for key in copies:
-        if key[0] < AHEAD:
-            copies[key].start()
-    if count == 0:
-        for copy in brought:
-            copy.wait()
-        tables = held
-    lefts = [stack_rows(base, tables[3 * at][...], tables[3 * at + 1][...]) for at in range(len(shares))]
-    vels = [tables[3 * at + 2][...] for at in range(len(shares))]
-    if second:
-        gram = sum(dot_nt(jnp.concatenate([left, vel], axis=0), left) for left, vel in zip(lefts, vels))
-        outs[2][...] = halves(sums[2][...] + gram, 1) if count else gram
-    for place, chunk in enumerate(chunks):
-        for at in range(len(shares)):
-            copies[place, at].wait()
-            if place + AHEAD < len(chunks):
-                copies[place + AHEAD, at].start()
-        last = chunk // per == 3
-        total = sum(halved_dot(vels[at] if last else lefts[at], buf[at, place]) for at in range(len(shares)))
-        spot = slice(place * rows, (place + 1) * rows)
-        if last:
-            spot = slice((place - per) * rows, (place - per + 1) * rows)
-        if count == 0:
-            outs[1 if last else 0][:, spot] = total
-            continue
-        total = total + sums[1 if last else 0][:, spot]
-        where = slice((chunk % per) * rows, (chunk % per + 1) * rows)
-        if chunk // per % 2:
-            outs[1][:, where] = halves(total, 0)
+def fetched(rows, weight, buf, sems):
+    half = buf.shape[-1]
+    return {
+        (at, side): pltpu.make_async_copy(
+            weight.at[pl.ds(at * rows, rows), pl.ds(side * half, half)], buf.at[at, side], sems.at[at, side]
+        )
+        for at in range(buf.shape[0])
+        for side in range(2)
+    }
+
+
+def weigh(rows, across, copies, buf, table_ref, out_ref):
+    half = buf.shape[-1]
+    for at in range(buf.shape[0]):
+        total = 0.0
+        for side in range(2):
+            copies[at, side].wait()
+            total = total + dot(buf[at, side], table_ref[side * half : (side + 1) * half, :])
+        if across:
+            out_ref[:, at * rows : (at + 1) * rows] = halves(total.T, 0)
         else:
-            outs[0][where, :] = halves(total.T, 1)
+            out_ref[at * rows : (at + 1) * rows, :] = halves(total, 1)
+
+
+def first_weights_kernel(rows, base, parts, *refs):
+    tables, weight = refs[: 3 * parts], refs[3 * parts].at[0]
+    out_ref, right_ref, down_ref, gram_ref, gv_ref = refs[3 * parts + 1 : 3 * parts + 6]
+    held, small, buf, sems = refs[-6:-3], refs[-3], refs[-2], refs[-1]
+    brought = started(tables[:3], held, small)
+    copies = fetched(rows, weight, buf, sems)
+    for copy in copies.values():
+        copy.start()
+    for copy in brought:
+        copy.wait()
+    tables = tuple(held) + tables[3:]
+    share = tables[0].shape[1]
+    index = lax.axis_index("tok")
+    gram = gv = 0.0
+    for at in range(parts):
+        spot = pl.ds(pl.multiple_of(lax.rem(index + at, parts) * share, LANES), share)
+        left = [tables[3 * at][...].astype(F32), tables[3 * at + 1][...].astype(F32)]
+        left.append(jnp.zeros((base - left[0].shape[0] - left[1].shape[0], share), F32))
+        left = jnp.concatenate(left, axis=0)
+        right = left.T.astype(BF16)
+        vel = tables[3 * at + 2][...]
+        right_ref[spot, :] = right
+        down_ref[spot, :] = vel.astype(F32).T.astype(BF16)
+        gram = gram + dot(left.astype(BF16), right)
+        gv = gv + dot(vel, right)
+    gram_ref[...] = halves(gram, 1)
+    gv_ref[...] = halves(gv, 1)
+    weigh(rows, False, copies, buf, right_ref, out_ref)
+
+
+def weights_kernel(rows, across, kind, weight, table_ref, *refs):
+    out_ref, buf, sems = refs[-3:]
+    copies = fetched(rows, weight if kind is None else weight.at[kind], buf, sems)
+    for copy in copies.values():
+        copy.start()
+    weigh(rows, across, copies, buf, table_ref, out_ref)
 
 
 def advance(level_count, tok, first, g_ref, hpart_ref, xq_ref):
@@ -153,8 +142,8 @@
     fresh_ref = None
     if step < STEPS - 1:
         fresh_ref = refs.pop(0)
-    gain_ref, mq_ref, mk_ref, mv_ref, wo_ref, gram_ref = refs[:6]
-    refs = refs[6:]
+    gain_ref, mq_ref, mk_ref, mv_ref, wo_ref, gram_ref, gv_ref = refs[:7]
+    refs = refs[7:]
     part_ref, hpart_ref, xq_ref = refs[:3]
     refs = refs[3:]
     own_ref = None
@@ -192,7 +181,7 @@
     aug_t = aug_t.astype(BF16).astype(F32)
     aug_tb = aug_t.astype(BF16)
     both_t = jnp.concatenate([aug_tb, aug_tb], axis=0)
-    mean_t = jnp.sum(dot(gram_ref[:base, :], both_t) * aug_t, axis=0, keepdims=True) * (1.0 / depth)
+    mean_t = jnp.sum(dot(gram_ref[...], both_t) * aug_t, axis=0, keepdims=True) * (1.0 / depth)
     mean_t = jnp.maximum(mean_t, 0.0) + EPS
     queries = slice(HALO * tok, HALO * tok + query_lanes)
     mean_q = mean_t[:, queries]
@@ -204,7 +193,7 @@
     aug_b = aug.astype(BF16)
     both = jnp.concatenate([aug_b, aug_b], axis=1)
 
-    hpart_ref[...] = dot(gram_ref[base:, :], both_q)
+    hpart_ref[...] = dot(gv_ref[...], both_q)
     xq_ref[...] = state[:, queries]
 
     gain = gain_ref[0:1, :] * gain_ref[1:2, :] * (HD ** -0.5 * math.log2(math.e))
@@ -359,53 +348,59 @@
 
     share = depth // parts
     table = (embed_weight, level_embed, vel_weight.T)
-    tables = [from_ahead(piece, d) for d in range(1, parts) for piece in table]
-    noise = [from_ahead(fresh_noise, d) for d in range(1, parts)]
+    around = range(1, parts)
+    tables = [from_ahead(piece, d) for d in around for piece in table]
+    noise = [from_ahead(fresh_noise, d) for d in around]
+    rows = 384 if width % 384 == 0 else 256
+
     in_hbm = lambda array: pltpu.with_memory_space_constraint(array, pltpu.HBM)
-    table = tuple(in_hbm(piece) for piece in table)
     qkv_weight, out_weight = in_hbm(qkv_weight), in_hbm(out_weight)
-    rows = 256
-    chunks = 2 * width // rows
-
-    def weights(count, second, after, *operands):
-        shares = max(1, count - 1)
-        if count == 0 and second:
-            outs = [shape((base, width), F32), shape((channels, width), F32), shape((base + channels, base), F32)]
-        elif count == 0:
-            outs = [shape((base, 2 * width), F32)]
-        elif second:
-            outs = [
+    fetching = [
+        pltpu.VMEM((width // rows, 2, rows, depth // 2), BF16),
+        pltpu.SemaphoreType.DMA((width // rows, 2)),
+    ]
+    price = pl.CostEstimate(flops=4 * base * width * depth, bytes_accessed=2 * width * depth, transcendentals=0)
+
+    def first_weights():
+        return pl.pallas_call(
+            functools.partial(first_weights_kernel, rows, base, parts),
+            out_shape=(
                 shape((width, 2 * base), BF16),
-                shape((2 * channels, width), BF16),
-                shape((base + channels, 2 * base), BF16),
-            ]
-        else:
-            outs = [shape((width, 2 * base), BF16), shape((2 * base, width), BF16)]
-        scratch = [pltpu.VMEM((shares, chunks, rows, share), BF16), pltpu.SemaphoreType.DMA((shares, chunks))]
-        if count == 0:
-            held = [pltpu.VMEM(piece.shape, BF16) for piece in table]
-            scratch = held + [pltpu.SemaphoreType.DMA((3,))] + scratch
+                shape((depth, base), BF16),
+                shape((depth, channels), BF16),
+                shape((base, 2 * base), BF16),
+                shape((channels, 2 * base), BF16),
+            ),
+            in_specs=[hbm] * 3 + [vmem] * len(tables) + [hbm],
+            out_specs=(vmem,) * 5,
+            scratch_shapes=[pltpu.VMEM(piece.shape, BF16) for piece in table]
+            + [pltpu.SemaphoreType.DMA((3,))]
+            + fetching,
+            compiler_params=pltpu.CompilerParams(vmem_limit_bytes=24 * 2**20),
+            cost_estimate=price,
+            name="first_weights",
+        )(*map(in_hbm, table), *tables, qkv_weight)
+
+    def weights(weight, kind, at, across, *after):
+        factor = done[0][at]
+        wide = 2 * factor.shape[1]
         return pl.pallas_call(
-            functools.partial(weights_kernel, rows, base, count, second),
-            out_shape=tuple(outs),
-            in_specs=[hbm if count == 0 else vmem] * len(operands) + [hbm] * 2 + [anywhere] * len(after),
-            out_specs=(vmem,) * len(outs),
-            scratch_shapes=scratch,
+            functools.partial(weights_kernel, rows, across, kind),
+            out_shape=shape((wide, width) if across else (width, wide), BF16),
+            in_specs=[hbm, vmem] + [anywhere] * len(after),
+            out_specs=vmem,
+            scratch_shapes=fetching,
             compiler_params=pltpu.CompilerParams(vmem_limit_bytes=24 * 2**20),
-            cost_estimate=pl.CostEstimate(
-                flops=4 * base * width * share * shares,
-                bytes_accessed=4 * width * share * shares,
-                transcendentals=0,
-            ),
+            cost_estimate=price,
             name="weights",
-        )(*operands, qkv_weight, out_weight, *after)
+        )(weight, factor, *after)
 
     state = latent
     work = [
-        lambda *after: weights(0, False, after, *table),
-        lambda *after: weights(0, True, after, *table),
-        lambda *after: weights(parts, False, after, *tables, *done[0]),
-        lambda *after: weights(parts, True, after, *tables, *done[1]),
+        first_weights,
+        functools.partial(weights, qkv_weight, 1, 1, True),
+        functools.partial(weights, qkv_weight, 2, 1, False),
+        functools.partial(weights, out_weight, None, 2, True),
     ]
     done, after = [], ()
     distance = frames // 2
@@ -421,8 +416,7 @@
     while len(done) < len(work):
         done.append(work[len(done)]())
     latents = [state] + [from_ahead(state, d) for d in range(1, parts)] + noise
-    mq, mk = done[2]
-    mv, wo, gram = done[3]
+    (mq, _, _, gram, gv), mk, mv, wo = done
 
     query_block = max(1, LANES // tok)
     owned = []
@@ -440,8 +434,8 @@
         if step < STEPS - 1:
             args += [fresh_noise]
             specs += [vmem]
-        args += [qk_gain, mq, mk, mv, wo, gram]
-        specs += [vmem] * 6
+        args += [qk_gain, mq, mk, mv, wo, gram, gv]
+        specs += [vmem] * 7
         outs = [shape((channels, query_lanes), F32)] * 3
         if step > 0:
             outs += [shape((part_rows, channels), F32)]

time: 99.7 us -> 99.7 us (level)
  transfers between devices with their start and end apart: 9 -> 9, of which waited for: 1 -> 1; matrix products, arithmetic and copies ran while one was open for 0% -> 0% of each run, Pallas kernels for 19% -> 20%
where the time goes in v8:
time: 99.7 us; the launch traced here: 99.5 us
  Pallas kernels  81.6 us (82%)
  starting transfers between devices  9.65 us (10%)
  blocking collectives  5.98 us (6%)
  waiting for transfers between devices  1.36 us (1%)
    pallas_call x3, Pallas kernels, body(): pl.pallas_call(functools.partial(step_kernel, step, cfg), out_shape=tuple...  61.2 us
    pallas_call x3, Pallas kernels, weights(): pl.pallas_call(functools.partial(weights_kernel, rows, across, kind), out...  13.8 us
    ppermute x4, starting transfers between devices, swapped(): lax.ppermute(value, axis, [(source, source ^ distance) for source in rang...  8.39 us
    all_gather x3, blocking collectives, body(): gathered = lax.all_gather(part, 'tok', axis=0, tiled=False)  5.98 us
    pallas_call x1, Pallas kernels, first_weights(): pl.pallas_call(functools.partial(first_weights_kernel, rows, base, parts)...  5.91 us
  transfers between devices with their start and end apart: 9, of which 1 were waited for; matrix products, arithmetic and copies ran while one was open for 0% of the time, Pallas kernels for 20%

profile of v8, /device:TPU:0, one launch (start us, length us, event | category | flops | bytes accessed | tf_op | source)
XLA Modules:
  0.0 99.5 jit_solution(11785435490032939168)
XLA Ops:
  0.6 0.5 collective-permute-start.4
  1.2 0.1 collective-permute-start.2
  1.2 0.4 collective-permute-start.3
  1.7 3.7 %collective-permute-start = (f32[1,32,64]{2,1,0:T(8,128)}, f32[1,32,64]{2,1,0:T(8,128)S(1)}, u32[]{:S(2)}, u32[]{:S(2)}) collective-permute-start(f32[1,32,64]{2,1,0:T(8,128)} %param.10), channel_id=1, source_target_pairs={{0,16},{2,18},{4,20},{6,22},{8,24},{10,26},{12,28},{14,30},{16,0},... | collective-permute-start | bytes 24584 | tf_op jit(solution)/shard_map/ppermute | solution.py:344
  5.3 0.2 collective-permute-start.1
  5.5 5.9 %first_weights.1 = (bf16[768,256]{1,0:T(8,128)(2,1)S(1)}, bf16[3072,128]{1,0:T(8,128)(2,1)S(1)}, bf16[3072,64]{1,0:T(8,128)(2,1)S(1)}, bf16[128,256]{1,0:T(8,128)(2,1)S(1)}, bf16[64,256]{1,0:T(8,128)(2,1)S(1)}) custom-call(bf16[64,1536]{1,0:T(8,128)(2,1)} %refs_0_.4, bf16[19,1536]{1,0:T(8,128)(2,1)} %refs_1_.4, bf16[64,1536]{1,0:T(8,128)(2,1)} %bitcast.8, ...), custom_call_target="tpu_custom_call" | custom-call | flops 1207959552 | bytes 4718592 | tf_op jit(solution)/shard_map/first_weights/pallas_call | solution.py:365
  11.5 0.1 pad_maximum_fusion.3
  11.5 1.6 %collective-permute-start.5 = (f32[1,32,128]{2,1,0:T(8,128)S(1)}, f32[1,32,128]{2,1,0:T(8,128)S(1)}, u32[]{:S(2)}, u32[]{:S(2)}) collective-permute-start(f32[1,32,128]{2,1,0:T(8,128)S(1)} %pad_maximum_fusion.3), channel_id=1, source_target_pairs={{0,8},{2,10},{4,12},{6,14},{8,0},{10,2},{12,4},{14,6},{16,24},{18,... | collective-permute-start | bytes 49160 | tf_op jit(solution)/shard_map/ppermute | solution.py:344
  13.1 4.7 %weights.3.refs_8_.refs_7_ = bf16[256,768]{1,0:T(8,128)(2,1)S(1)} custom-call(bf16[3,768,3072]{2,1,0:T(8,128)(2,1)} %weight.4, bf16[3072,128]{1,0:T(8,128)(2,1)S(1)} %get-tuple-element.41.table_ref, f32[1,32,64]{2,1,0:T(8,128)S(1)} %collective-permute-done.refs_0_), custom_call_target="tpu_custom_call" | custom-call | flops 1207959552 | bytes 4718592 | tf_op jit(solution)/shard_map/weights/pallas_call | solution.py:387
  17.8 0.0 copy-start
  17.8 0.0 copy-start.1
  17.8 1.6 %collective-permute-start.6 = (f32[2,32,128]{2,1,0:T(8,128)S(1)}, f32[2,32,128]{2,1,0:T(8,128)S(1)}, u32[]{:S(2)}, u32[]{:S(2)}) collective-permute-start(f32[2,32,128]{2,1,0:T(8,128)S(1)} %pad_maximum_fusion.2), channel_id=1, source_target_pairs={{0,4},{2,6},{4,0},{6,2},{8,12},{10,14},{12,8},{14,10},{16,20},{18,... | collective-permute-start | bytes 98312 | tf_op jit(solution)/shard_map/ppermute | solution.py:344
  19.4 4.5 %weights.4.refs_9_.refs_8_ = bf16[768,256]{1,0:T(8,128)(2,1)S(1)} custom-call(bf16[3,768,3072]{2,1,0:T(8,128)(2,1)} %weight.4, bf16[3072,128]{1,0:T(8,128)(2,1)S(1)} %get-tuple-element.41.table_ref, f32[1,32,128]{2,1,0:T(8,128)S(1)} %collective-permute-done.5.refs_0_), custom_call_target="tpu_custom_call" | custom-call | flops 1207959552 | bytes 4718592 | tf_op jit(solution)/shard_map/weights/pallas_call | solution.py:387
  24.0 1.6 %collective-permute-start.7 = (f32[4,32,128]{2,1,0:T(8,128)S(1)}, f32[4,32,128]{2,1,0:T(8,128)S(1)}, u32[]{:S(2)}, u32[]{:S(2)}) collective-permute-start(f32[4,32,128]{2,1,0:T(8,128)S(1)} %pad_maximum_fusion.1), channel_id=1, source_target_pairs={{0,2},{2,0},{4,6},{6,4},{8,10},{10,8},{12,14},{14,12},{16,18},{18,... | collective-permute-start | bytes 196616 | tf_op jit(solution)/shard_map/ppermute | solution.py:344
  25.5 4.6 %weights.5.refs_10_.refs_9_ = bf16[128,768]{1,0:T(8,128)(2,1)S(1)} custom-call(bf16[768,3072]{1,0:T(8,128)(2,1)} %weight.5, bf16[3072,64]{1,0:T(8,128)(2,1)S(1)} %get-tuple-element.46.table_ref, f32[2,32,128]{2,1,0:T(8,128)S(1)} %collective-permute-done.6.refs_0_), custom_call_target="tpu_custom_call" | custom-call | flops 1207959552 | bytes 4718592 | tf_op jit(solution)/shard_map/weights/pallas_call | solution.py:387
  30.2 0.1 collective-permute-start.8
  30.3 1.3 %collective-permute-done.8.refs_3_ = f32[8,32,128]{2,1,0:T(8,128)S(1)} collective-permute-done((f32[8,32,128]{2,1,0:T(8,128)S(1)}, f32[8,32,128]{2,1,0:T(8,128)S(1)}, u32[]{:S(2)}, u32[]{:S(2)}) %collective-permute-start.8) | collective-permute-done | bytes 131104 | tf_op jit(solution)/shard_map/ppermute | solution.py:347
  31.6 34.6 %step0.1 = (f32[64,896]{1,0:T(8,128)S(1)}, f32[64,896]{1,0:T(8,128)S(1)}, f32[64,896]{1,0:T(8,128)S(1)}) custom-call(s32[16]{0:T(128)S(1)} %copy-done.2, s32[16]{0:T(128)S(1)} %copy-done.3, f32[8,32,128]{2,1,0:T(8,128)S(1)} %pad_maximum_fusion.refs_2_, f32[8,32,128]{2,1,0:T(8,128)S(1)} %collective-permute-done.8.refs_3_, ...), custom_call_target="tpu_custom_call" | custom-call | flops 2919235584 | bytes 786432 | tf_op jit(solution)/shard_map/step0/pallas_call | solution.py:443
  66.2 2.1 %all-gather = f32[128,896]{1,0:T(8,128)S(1)} all-gather(f32[64,896]{1,0:T(8,128)S(1)} %get-tuple-element.55), channel_id=2, replica_groups=mesh['queue'=16,'tok'=2] {'tok'}, dimensions={0}, use_global_device_ids=true | all-gather | bytes 688128 | tf_op jit(solution)/shard_map/all_gather | solution.py:466
  68.3 20.1 %step1.1 = (f32[64,512]{1,0:T(8,128)S(1)}, f32[64,512]{1,0:T(8,128)S(1)}, f32[64,512]{1,0:T(8,128)S(1)}, f32[32,64]{1,0:T(8,128)S(1)}) custom-call(s32[16]{0:T(128)S(1)} %copy-done.2, s32[16]{0:T(128)S(1)} %copy-done.3, f32[2,64,896]{2,1,0:T(8,128)S(1)} %bitcast.4, f32[64,896]{1,0:T(8,128)S(1)} %get-tuple-element.56.refs_3_, ...), custom_call_target="tpu_custom_call" | custom-call | flops 1862270976 | bytes 786432 | tf_op jit(solution)/shard_map/step1/pallas_call | solution.py:443
  88.5 2.0 %all-gather.1 = f32[128,512]{1,0:T(8,128)S(1)} all-gather(f32[64,512]{1,0:T(8,128)S(1)} %get-tuple-element.58), channel_id=3, replica_groups=mesh['queue'=16,'tok'=2] {'tok'}, dimensions={0}, use_global_device_ids=true | all-gather | bytes 393216 | tf_op jit(solution)/shard_map/all_gather | solution.py:466
  90.5 6.5 %step2.1 = (f32[64,128]{1,0:T(8,128)S(1)}, f32[64,128]{1,0:T(8,128)S(1)}, f32[64,128]{1,0:T(8,128)S(1)}, f32[32,64]{1,0:T(8,128)S(1)}) custom-call(s32[16]{0:T(128)S(1)} %copy-done.2, s32[16]{0:T(128)S(1)} %copy-done.3, f32[2,64,512]{2,1,0:T(8,128)S(1)} %bitcast.5, f32[64,512]{1,0:T(8,128)S(1)} %get-tuple-element.59.refs_3_, ...), custom_call_target="tpu_custom_call" | custom-call | flops 805306368 | bytes 786432 | tf_op jit(solution)/shard_map/step2/pallas_call | solution.py:443
  96.9 1.9 %all-gather.2 = f32[128,128]{1,0:T(8,128)S(1)} all-gather(f32[64,128]{1,0:T(8,128)S(1)} %get-tuple-element.61), channel_id=4, replica_groups=mesh['queue'=16,'tok'=2] {'tok'}, dimensions={0}, use_global_device_ids=true | all-gather | bytes 98304 | tf_op jit(solution)/shard_map/all_gather | solution.py:466
  98.8 0.7 last.1
  (19 shorter events, 0.1 us)
Async XLA Ops:
  0.6 10.8 %copy-start.4 = (f32[1,32,64]{2,1,0:T(8,128)S(1)}, f32[1,32,64]{2,1,0:T(8,128)}, u32[]{:S(2)}) copy-start(f32[1,32,64]{2,1,0:T(8,128)} %param.10) | copy-start | bytes 24580
  0.6 4.9 %collective-permute-start.4 = (bf16[64,1536]{1,0:T(8,128)(2,1)}, bf16[64,1536]{1,0:T(8,128)(2,1)S(1)}, u32[]{:S(2)}, u32[]{:S(2)}) collective-permute-start(bf16[64,1536]{1,0:T(8,128)(2,1)} %bitcast.7), channel_id=1, source_target_pairs={{0,1},{1,0},{2,3},{3,2},{4,5},{5,4},{6,7},{7,6},{8,9},{9,8},{10,11... | collective-permute-start | bytes 589832 | tf_op jit(solution)/shard_map/ppermute | solution.py:347
  1.2 4.3 %collective-permute-start.2 = (bf16[64,1536]{1,0:T(8,128)(2,1)}, bf16[64,1536]{1,0:T(8,128)(2,1)S(1)}, u32[]{:S(2)}, u32[]{:S(2)}) collective-permute-start(bf16[64,1536]{1,0:T(8,128)(2,1)} %refs_0_.4), channel_id=1, source_target_pairs={{0,1},{1,0},{2,3},{3,2},{4,5},{5,4},{6,7},{7,6},{8,9},{9,8},{10,11... | collective-permute-start | bytes 589832 | tf_op jit(solution)/shard_map/ppermute | solution.py:347
  1.2 4.3 %collective-permute-start.3 = (bf16[19,1536]{1,0:T(8,128)(2,1)}, bf16[19,1536]{1,0:T(8,128)(2,1)S(1)}, u32[]{:S(2)}, u32[]{:S(2)}) collective-permute-start(bf16[19,1536]{1,0:T(8,128)(2,1)} %refs_1_.4), channel_id=1, source_target_pairs={{0,1},{1,0},{2,3},{3,2},{4,5},{5,4},{6,7},{7,6},{8,9},{9,8},{10,11... | collective-permute-start | bytes 175112 | tf_op jit(solution)/shard_map/ppermute | solution.py:347
  1.7 9.8 %collective-permute-start = (f32[1,32,64]{2,1,0:T(8,128)}, f32[1,32,64]{2,1,0:T(8,128)S(1)}, u32[]{:S(2)}, u32[]{:S(2)}) collective-permute-start(f32[1,32,64]{2,1,0:T(8,128)} %param.10), channel_id=1, source_target_pairs={{0,16},{2,18},{4,20},{6,22},{8,24},{10,26},{12,28},{14,30},{16,0},... | collective-permute-start | bytes 24584 | tf_op jit(solution)/shard_map/ppermute | solution.py:344
  5.3 6.1 %collective-permute-start.1 = (f32[3,32,64]{2,1,0:T(8,128)}, f32[3,32,64]{2,1,0:T(8,128)S(1)}, u32[]{:S(2)}, u32[]{:S(2)}) collective-permute-start(f32[3,32,64]{2,1,0:T(8,128)} %refs_5_.4), channel_id=1, source_target_pairs={{0,1},{1,0},{2,3},{3,2},{4,5},{5,4},{6,7},{7,6},{8,9},{9,8},{10,11... | collective-permute-start | bytes 73736 | tf_op jit(solution)/shard_map/ppermute | solution.py:347
  11.5 6.3 %collective-permute-start.5 = (f32[1,32,128]{2,1,0:T(8,128)S(1)}, f32[1,32,128]{2,1,0:T(8,128)S(1)}, u32[]{:S(2)}, u32[]{:S(2)}) collective-permute-start(f32[1,32,128]{2,1,0:T(8,128)S(1)} %pad_maximum_fusion.3), channel_id=1, source_target_pairs={{0,8},{2,10},{4,12},{6,14},{8,0},{10,2},{12,4},{14,6},{16,24},{18,... | collective-permute-start | bytes 49160 | tf_op jit(solution)/shard_map/ppermute | solution.py:344
  17.8 13.8 %copy-start = (f32[3,32,64]{2,1,0:T(8,128)S(1)}, f32[3,32,64]{2,1,0:T(8,128)}, u32[]{:S(2)}) copy-start(f32[3,32,64]{2,1,0:T(8,128)} %refs_5_.4) | copy-start | bytes 73732
  17.8 13.8 %copy-start.1 = (f32[2,768]{1,0:T(2,128)S(1)}, f32[2,768]{1,0:T(2,128)}, u32[]{:S(2)}) copy-start(f32[2,768]{1,0:T(2,128)} %refs_5_.5) | copy-start | bytes 18436
  17.8 13.8 %copy-start.2 = (s32[16]{0:T(128)S(1)}, s32[16]{0:T(128)}, u32[]{:S(2)}) copy-start(s32[16]{0:T(128)} %refs_0_.7) | copy-start | bytes 196
  17.8 13.8 %copy-start.3 = (s32[16]{0:T(128)S(1)}, s32[16]{0:T(128)}, u32[]{:S(2)}) copy-start(s32[16]{0:T(128)} %refs_1_.7) | copy-start | bytes 196
  17.8 6.1 %collective-permute-start.6 = (f32[2,32,128]{2,1,0:T(8,128)S(1)}, f32[2,32,128]{2,1,0:T(8,128)S(1)}, u32[]{:S(2)}, u32[]{:S(2)}) collective-permute-start(f32[2,32,128]{2,1,0:T(8,128)S(1)} %pad_maximum_fusion.2), channel_id=1, source_target_pairs={{0,4},{2,6},{4,0},{6,2},{8,12},{10,14},{12,8},{14,10},{16,20},{18,... | collective-permute-start | bytes 98312 | tf_op jit(solution)/shard_map/ppermute | solution.py:344
  24.0 6.2 %collective-permute-start.7 = (f32[4,32,128]{2,1,0:T(8,128)S(1)}, f32[4,32,128]{2,1,0:T(8,128)S(1)}, u32[]{:S(2)}, u32[]{:S(2)}) collective-permute-start(f32[4,32,128]{2,1,0:T(8,128)S(1)} %pad_maximum_fusion.1), channel_id=1, source_target_pairs={{0,2},{2,0},{4,6},{6,4},{8,10},{10,8},{12,14},{14,12},{16,18},{18,... | collective-permute-start | bytes 196616 | tf_op jit(solution)/shard_map/ppermute | solution.py:344
  30.2 1.4 %collective-permute-start.8 = (f32[8,32,128]{2,1,0:T(8,128)S(1)}, f32[8,32,128]{2,1,0:T(8,128)S(1)}, u32[]{:S(2)}, u32[]{:S(2)}) collective-permute-start(f32[8,32,128]{2,1,0:T(8,128)S(1)} %pad_maximum_fusion.refs_2_), channel_id=1, source_target_pairs={{0,1},{1,0},{2,3},{3,2},{4,5},{5,4},{6,7},{7,6},{8,9},{9,8},{10,11... | collective-permute-start | bytes 393224 | tf_op jit(solution)/shard_map/ppermute | solution.py:347

commit v9 on v7

--- a/solution.py
+++ b/solution.py
@@ -167,7 +167,6 @@
     n_key = n_query + 2 * HALO
     key_lanes, query_lanes = n_key * tok, n_query * tok
     width = heads * HD
-    window = (2 * HALO + query_block) * tok
     position, tok_index = lax.axis_index("queue"), lax.axis_index("tok")
     first_key = position - HALO - (HALO + 1) * (STEPS - 1 - step)
     refs = list(refs)
@@ -254,25 +253,34 @@
     lane = lax.broadcasted_iota(jnp.int32, (1, 2 * LANES), 1)
     within = lax.rem(lane, LANES) // tok
 
-    def place(b):
-        lead = (b * LANES) // tok
-        keys = pl.ds(pl.multiple_of(lead * tok, LANES), window)
-        return lead, keys, pl.ds(pl.multiple_of(b * LANES, LANES), LANES)
+    full = 2 * HALO + query_block
+    if query_block == 1:
+        cuts = [(HALO - r, 2 * r + 1) for r in range(HALO + 1)]
+    else:
+        cuts = [(2, full - 4), (2, full - 2), (0, full - 2), (0, full)]
+
+    def reaches(lead):
+        widths = []
+        for j in range(query_block):
+            frame = first_key + HALO + lead + j
+            needed = (frame >= 0) & (frame < frames) & (lead + j <= n_query - query_block)
+            widths.append(jnp.where(needed, reach_ref[jnp.clip(frame, 0, frames - 1)], -1))
+        return widths
 
     def biases(lead, shift):
-        rows = []
-        for k in range(2 * HALO + query_block):
+        rows, widths = [], reaches(lead)
+        for k in range(full):
             target = first_key + lead + k
             inside = (target >= 0) & (target < frames)
             row = jnp.zeros((1, 2 * LANES), F32)
             for j in range(query_block):
-                frame = first_key + HALO + lead + j
-                reach = reach_ref[jnp.clip(frame, 0, frames - 1)]
-                unused = (frame < 0) | (frame >= frames)
-                counted = (inside & (abs(k - HALO - j) <= reach)) | unused
+                counted = (inside & (abs(k - HALO - j) <= widths[j])) | (widths[j] < 0)
                 row = jnp.where(within == j, jnp.where(counted, 0.0, -1e30), row)
             rows.append(row - shift)
         return rows
+
+    def span_of(first, count):
+        return pl.ds(pl.multiple_of(first * tok, LANES), count * tok)
 
     def scores(keys, lanes, cols, rows):
         query = qbuf[cols, lanes]
@@ -282,7 +290,7 @@
         return jnp.concatenate([score[k * tok : (k + 1) * tok] + rows[k] for k in range(len(rows))], axis=0)
 
     def mix(keys, lanes, cols, weight):
-        ones = jnp.ones((16, window), BF16)
+        ones = jnp.ones((16, weight.shape[0]), BF16)
         mixed = dot(jnp.concatenate([vbuf[cols, keys], ones], axis=0), weight.astype(BF16))
         total = mixed[2 * HD : 2 * HD + 1, :]
         scale = 1.0 / total
@@ -292,19 +300,35 @@
         return total
 
     def block(b, least):
-        lead, keys, lanes = place(b)
-        rows = biases(lead, bound)
-        held = None
-        for pair in range(heads // 2):
-            cols = slice(pair * 2 * HD, (pair + 1) * 2 * HD)
-            weight = jnp.exp2(scores(keys, lanes, cols, rows)).astype(BF16)
-            if held is not None:
-                least = jnp.minimum(least, mix(keys, lanes, *held))
-            held = (cols, weight)
-        return jnp.minimum(least, mix(keys, lanes, *held))
+        lead = (b * LANES) // tok
+        lanes = pl.ds(pl.multiple_of(b * LANES, LANES), LANES)
+        rows, widths = biases(lead, bound), reaches(lead)
+
+        def run(first, count, least):
+            keys = span_of(lead + first, count)
+            held = None
+            for pair in range(heads // 2):
+                cols = slice(pair * 2 * HD, (pair + 1) * 2 * HD)
+                weight = jnp.exp2(scores(keys, lanes, cols, rows[first : first + count])).astype(BF16)
+                if held is not None:
+                    least = jnp.minimum(least, mix(keys, lanes, *held))
+                held = (cols, weight)
+            return jnp.minimum(least, mix(keys, lanes, *held))
+
+        if query_block == 1:
+            chosen = jnp.maximum(widths[0], 0)
+        else:
+            left, right = widths[0], widths[0] - query_block + 1
+            for j in range(1, query_block):
+                left = jnp.maximum(left, widths[j] - j)
+                right = jnp.maximum(right, widths[j] + j - query_block + 1)
+            chosen = jnp.where(left > 1, 2, 0) + jnp.where(right > 1, 1, 0)
+        return lax.switch(chosen, [functools.partial(run, *cut) for cut in cuts], least)
 
     def exact_block(at, carry):
-        lead, keys, lanes = place(at // (heads // 2))
+        lead = (at // (heads // 2) * LANES) // tok
+        keys = span_of(lead, full)
+        lanes = pl.ds(pl.multiple_of(at // (heads // 2) * LANES, LANES), LANES)
         cols = pl.ds(pl.multiple_of(lax.rem(at, heads // 2) * 2 * HD, 2 * HD), 2 * HD)
         score = scores(keys, lanes, cols, biases(lead, 0.0))
         mix(keys, lanes, cols, jnp.exp2(score - jnp.max(score, axis=0, keepdims=True)))

time: 96 us -> 93.6 us (0.975)
  Pallas kernels: 77.9 us -> 75.1 us
    pallas_call x3, Pallas kernels: 61.2 us -> 58.4 us  [body(): pl.pallas_call(functools.partial(step_kernel, step, cfg), out_shape=tuple...]
where the time goes in v9:
time: 93.6 us; the launch traced here: 93.1 us
  Pallas kernels  75.1 us (80%)
  starting transfers between devices  9.65 us (10%)
  blocking collectives  5.98 us (6%)
  waiting for transfers between devices  1.36 us (1%)
    pallas_call x3, Pallas kernels, body(): pl.pallas_call(functools.partial(step_kernel, step, cfg), out_shape=tuple...  58.4 us
    pallas_call x4, Pallas kernels, weights(): pl.pallas_call(functools.partial(kernel, shares), out_shape=tuple(outs),...  16 us
    ppermute x4, starting transfers between devices, swapped(): lax.ppermute(value, axis, [(source, source ^ distance) for source in rang...  8.39 us
    all_gather x3, blocking collectives, body(): gathered = lax.all_gather(part, 'tok', axis=0, tiled=False)  5.98 us
  transfers between devices with their start and end apart: 9, of which 1 were waited for; matrix products, arithmetic and copies ran while one was open for 0% of the time, Pallas kernels for 17%

profile of v9, /device:TPU:0, one launch (start us, length us, event | category | flops | bytes accessed | tf_op | source)
XLA Modules:
  0.0 93.1 jit_solution(3714247234349265544)
XLA Ops:
  0.6 0.5 collective-permute-start.1
  1.2 3.7 %collective-permute-start = (f32[1,32,64]{2,1,0:T(8,128)}, f32[1,32,64]{2,1,0:T(8,128)S(1)}, u32[]{:S(2)}, u32[]{:S(2)}) collective-permute-start(f32[1,32,64]{2,1,0:T(8,128)} %param.10), channel_id=1, source_target_pairs={{0,16},{2,18},{4,20},{6,22},{8,24},{10,26},{12,28},{14,30},{16,0},... | collective-permute-start | bytes 24584 | tf_op jit(solution)/shard_map/ppermute | solution.py:408
  4.8 0.2 collective-permute-start.4
  5.0 0.3 collective-permute-start.5
  5.3 0.2 collective-permute-start.7
  5.5 4.5 %weights.4 = (f32[1536,128]{1,0:T(8,128)S(1)}, f32[128,128]{1,0:T(8,128)S(1)}, bf16[1536,128]{1,0:T(8,128)(2,1)S(1)}) custom-call(bf16[64,1536]{1,0:T(8,128)(2,1)} %refs_0_.4, bf16[19,1536]{1,0:T(8,128)(2,1)} %refs_1_.4, bf16[3,768,3072]{2,1,0:T(8,128)(2,1)} %refs_5_.6, bf16[768,3072]{1,0:T(8,128)(2,1)} %refs_6_.3), custom_call_target="tpu_custom_call" | custom-call | flops 603979776 | bytes 4718592 | tf_op jit(solution)/shard_map/weights/pallas_call | solution.py:431
  10.0 0.1 pad_maximum_fusion.3
  10.1 1.6 %collective-permute-start.2 = (f32[1,32,128]{2,1,0:T(8,128)S(1)}, f32[1,32,128]{2,1,0:T(8,128)S(1)}, u32[]{:S(2)}, u32[]{:S(2)}) collective-permute-start(f32[1,32,128]{2,1,0:T(8,128)S(1)} %pad_maximum_fusion.3), channel_id=1, source_target_pairs={{0,8},{2,10},{4,12},{6,14},{8,0},{10,2},{12,4},{14,6},{16,24},{18,... | collective-permute-start | bytes 49160 | tf_op jit(solution)/shard_map/ppermute | solution.py:408
  11.7 4.4 %weights.5 = (f32[768,128]{1,0:T(8,128)S(1)}, f32[768,64]{1,0:T(8,128)S(1)}, f32[64,128]{1,0:T(8,128)S(1)}) custom-call(bf16[64,1536]{1,0:T(8,128)(2,1)} %bitcast.8, bf16[1536,128]{1,0:T(8,128)(2,1)S(1)} %get-tuple-element.52.refs_1_, bf16[3,768,3072]{2,1,0:T(8,128)(2,1)} %refs_5_.6, bf16[768,3072]{1,0:T(8,128)(2,1)} %refs_6_.3, ...), custom_call_target="tpu_custom_call" | custom-call | flops 603979776 | bytes 4718592 | tf_op jit(solution)/shard_map/weights/pallas_call | solution.py:431
  16.2 1.6 %collective-permute-start.3 = (f32[2,32,128]{2,1,0:T(8,128)S(1)}, f32[2,32,128]{2,1,0:T(8,128)S(1)}, u32[]{:S(2)}, u32[]{:S(2)}) collective-permute-start(f32[2,32,128]{2,1,0:T(8,128)S(1)} %pad_maximum_fusion.2), channel_id=1, source_target_pairs={{0,4},{2,6},{4,0},{6,2},{8,12},{10,14},{12,8},{14,10},{16,20},{18,... | collective-permute-start | bytes 98312 | tf_op jit(solution)/shard_map/ppermute | solution.py:408
  17.8 3.7 %weights.6 = (bf16[768,256]{1,0:T(8,128)(2,1)S(1)}, bf16[256,768]{1,0:T(8,128)(2,1)S(1)}, bf16[128,256]{1,0:T(8,128)(2,1)S(1)}, bf16[1536,128]{1,0:T(8,128)(2,1)S(1)}) custom-call(bf16[64,1536]{1,0:T(8,128)(2,1)S(1)} %collective-permute-done.4.refs_0_, bf16[19,1536]{1,0:T(8,128)(2,1)S(1)} %collective-permute-done.5.refs_1_, ...), custom_call_target="tpu_custom_call" | custom-call | flops 603979776 | bytes 4718592 | tf_op jit(solution)/shard_map/weights/pallas_call | solution.py:431
  21.4 0.0 copy-start
  21.4 0.0 copy-start.1
  21.5 1.6 %collective-permute-start.6 = (f32[4,32,128]{2,1,0:T(8,128)S(1)}, f32[4,32,128]{2,1,0:T(8,128)S(1)}, u32[]{:S(2)}, u32[]{:S(2)}) collective-permute-start(f32[4,32,128]{2,1,0:T(8,128)S(1)} %pad_maximum_fusion.1), channel_id=1, source_target_pairs={{0,2},{2,0},{4,6},{6,4},{8,10},{10,8},{12,14},{14,12},{16,18},{18,... | collective-permute-start | bytes 196616 | tf_op jit(solution)/shard_map/ppermute | solution.py:408
  23.1 3.4 %weights.7 = (bf16[768,256]{1,0:T(8,128)(2,1)S(1)}, bf16[128,768]{1,0:T(8,128)(2,1)S(1)}, bf16[64,256]{1,0:T(8,128)(2,1)S(1)}) custom-call(bf16[64,1536]{1,0:T(8,128)(2,1)S(1)} %collective-permute-done.7.refs_0_, bf16[1536,128]{1,0:T(8,128)(2,1)S(1)} %get-tuple-element.66.refs_1_, f32[768,128]{1,0:T(8,128)S(1)} %get-tuple-element.67.refs_2_, ...), custom_call_target="tpu_custom_call" | custom-call | flops 603979776 | bytes 4718592 | tf_op jit(solution)/shard_map/weights/pallas_call | solution.py:431
  26.5 0.1 collective-permute-start.8
  26.6 1.3 %collective-permute-done.8.refs_3_ = f32[8,32,128]{2,1,0:T(8,128)S(1)} collective-permute-done((f32[8,32,128]{2,1,0:T(8,128)S(1)}, f32[8,32,128]{2,1,0:T(8,128)S(1)}, u32[]{:S(2)}, u32[]{:S(2)}) %collective-permute-start.8) | collective-permute-done | bytes 131104 | tf_op jit(solution)/shard_map/ppermute | solution.py:411
  28.0 33.2 %step0.1 = (f32[64,896]{1,0:T(8,128)S(1)}, f32[64,896]{1,0:T(8,128)S(1)}, f32[64,896]{1,0:T(8,128)S(1)}) custom-call(s32[16]{0:T(128)S(1)} %copy-done.2, s32[16]{0:T(128)S(1)} %copy-done.3, f32[8,32,128]{2,1,0:T(8,128)S(1)} %pad_maximum_fusion.refs_2_, f32[8,32,128]{2,1,0:T(8,128)S(1)} %collective-permute-done.8.refs_3_, ...), custom_call_target="tpu_custom_call" | custom-call | flops 2919235584 | bytes 786432 | tf_op jit(solution)/shard_map/step0/pallas_call | solution.py:520
  61.1 2.1 %all-gather = f32[128,896]{1,0:T(8,128)S(1)} all-gather(f32[64,896]{1,0:T(8,128)S(1)} %get-tuple-element.81), channel_id=2, replica_groups=mesh['queue'=16,'tok'=2] {'tok'}, dimensions={0}, use_global_device_ids=true | all-gather | bytes 688128 | tf_op jit(solution)/shard_map/all_gather | solution.py:543
  63.3 19.2 %step1.1 = (f32[64,512]{1,0:T(8,128)S(1)}, f32[64,512]{1,0:T(8,128)S(1)}, f32[64,512]{1,0:T(8,128)S(1)}, f32[32,64]{1,0:T(8,128)S(1)}) custom-call(s32[16]{0:T(128)S(1)} %copy-done.2, s32[16]{0:T(128)S(1)} %copy-done.3, f32[2,64,896]{2,1,0:T(8,128)S(1)} %bitcast.4, f32[64,896]{1,0:T(8,128)S(1)} %get-tuple-element.82.refs_3_, ...), custom_call_target="tpu_custom_call" | custom-call | flops 1862270976 | bytes 786432 | tf_op jit(solution)/shard_map/step1/pallas_call | solution.py:520
  82.4 2.0 %all-gather.1 = f32[128,512]{1,0:T(8,128)S(1)} all-gather(f32[64,512]{1,0:T(8,128)S(1)} %get-tuple-element.84), channel_id=3, replica_groups=mesh['queue'=16,'tok'=2] {'tok'}, dimensions={0}, use_global_device_ids=true | all-gather | bytes 393216 | tf_op jit(solution)/shard_map/all_gather | solution.py:543
  84.4 6.0 %step2.1 = (f32[64,128]{1,0:T(8,128)S(1)}, f32[64,128]{1,0:T(8,128)S(1)}, f32[64,128]{1,0:T(8,128)S(1)}, f32[32,64]{1,0:T(8,128)S(1)}) custom-call(s32[16]{0:T(128)S(1)} %copy-done.2, s32[16]{0:T(128)S(1)} %copy-done.3, f32[2,64,512]{2,1,0:T(8,128)S(1)} %bitcast.5, f32[64,512]{1,0:T(8,128)S(1)} %get-tuple-element.85.refs_3_, ...), custom_call_target="tpu_custom_call" | custom-call | flops 805306368 | bytes 786432 | tf_op jit(solution)/shard_map/step2/pallas_call | solution.py:520
  90.5 1.9 %all-gather.2 = f32[128,128]{1,0:T(8,128)S(1)} all-gather(f32[64,128]{1,0:T(8,128)S(1)} %get-tuple-element.87), channel_id=4, replica_groups=mesh['queue'=16,'tok'=2] {'tok'}, dimensions={0}, use_global_device_ids=true | all-gather | bytes 98304 | tf_op jit(solution)/shard_map/all_gather | solution.py:543
  92.3 0.7 last.1
  (19 shorter events, 0.1 us)
Async XLA Ops:
  0.6 9.4 %copy-start.4 = (f32[1,32,64]{2,1,0:T(8,128)S(1)}, f32[1,32,64]{2,1,0:T(8,128)}, u32[]{:S(2)}) copy-start(f32[1,32,64]{2,1,0:T(8,128)} %param.10) | copy-start | bytes 24580
  0.6 9.4 %collective-permute-start.1 = (f32[3,32,64]{2,1,0:T(8,128)}, f32[3,32,64]{2,1,0:T(8,128)S(1)}, u32[]{:S(2)}, u32[]{:S(2)}) collective-permute-start(f32[3,32,64]{2,1,0:T(8,128)} %refs_5_.8), channel_id=1, source_target_pairs={{0,1},{1,0},{2,3},{3,2},{4,5},{5,4},{6,7},{7,6},{8,9},{9,8},{10,11... | collective-permute-start | bytes 73736 | tf_op jit(solution)/shard_map/ppermute | solution.py:411
  1.2 8.8 %collective-permute-start = (f32[1,32,64]{2,1,0:T(8,128)}, f32[1,32,64]{2,1,0:T(8,128)S(1)}, u32[]{:S(2)}, u32[]{:S(2)}) collective-permute-start(f32[1,32,64]{2,1,0:T(8,128)} %param.10), channel_id=1, source_target_pairs={{0,16},{2,18},{4,20},{6,22},{8,24},{10,26},{12,28},{14,30},{16,0},... | collective-permute-start | bytes 24584 | tf_op jit(solution)/shard_map/ppermute | solution.py:408
  4.8 12.9 %collective-permute-start.4 = (bf16[64,1536]{1,0:T(8,128)(2,1)}, bf16[64,1536]{1,0:T(8,128)(2,1)S(1)}, u32[]{:S(2)}, u32[]{:S(2)}) collective-permute-start(bf16[64,1536]{1,0:T(8,128)(2,1)} %refs_0_.4), channel_id=1, source_target_pairs={{0,1},{1,0},{2,3},{3,2},{4,5},{5,4},{6,7},{7,6},{8,9},{9,8},{10,11... | collective-permute-start | bytes 589832 | tf_op jit(solution)/shard_map/ppermute | solution.py:411
  5.0 12.8 %collective-permute-start.5 = (bf16[19,1536]{1,0:T(8,128)(2,1)}, bf16[19,1536]{1,0:T(8,128)(2,1)S(1)}, u32[]{:S(2)}, u32[]{:S(2)}) collective-permute-start(bf16[19,1536]{1,0:T(8,128)(2,1)} %refs_1_.4), channel_id=1, source_target_pairs={{0,1},{1,0},{2,3},{3,2},{4,5},{5,4},{6,7},{7,6},{8,9},{9,8},{10,11... | collective-permute-start | bytes 175112 | tf_op jit(solution)/shard_map/ppermute | solution.py:411
  5.3 17.7 %collective-permute-start.7 = (bf16[64,1536]{1,0:T(8,128)(2,1)}, bf16[64,1536]{1,0:T(8,128)(2,1)S(1)}, u32[]{:S(2)}, u32[]{:S(2)}) collective-permute-start(bf16[64,1536]{1,0:T(8,128)(2,1)} %bitcast.7), channel_id=1, source_target_pairs={{0,1},{1,0},{2,3},{3,2},{4,5},{5,4},{6,7},{7,6},{8,9},{9,8},{10,11... | collective-permute-start | bytes 589832 | tf_op jit(solution)/shard_map/ppermute | solution.py:411
  10.1 6.0 %collective-permute-start.2 = (f32[1,32,128]{2,1,0:T(8,128)S(1)}, f32[1,32,128]{2,1,0:T(8,128)S(1)}, u32[]{:S(2)}, u32[]{:S(2)}) collective-permute-start(f32[1,32,128]{2,1,0:T(8,128)S(1)} %pad_maximum_fusion.3), channel_id=1, source_target_pairs={{0,8},{2,10},{4,12},{6,14},{8,0},{10,2},{12,4},{14,6},{16,24},{18,... | collective-permute-start | bytes 49160 | tf_op jit(solution)/shard_map/ppermute | solution.py:408
  16.2 5.3 %collective-permute-start.3 = (f32[2,32,128]{2,1,0:T(8,128)S(1)}, f32[2,32,128]{2,1,0:T(8,128)S(1)}, u32[]{:S(2)}, u32[]{:S(2)}) collective-permute-start(f32[2,32,128]{2,1,0:T(8,128)S(1)} %pad_maximum_fusion.2), channel_id=1, source_target_pairs={{0,4},{2,6},{4,0},{6,2},{8,12},{10,14},{12,8},{14,10},{16,20},{18,... | collective-permute-start | bytes 98312 | tf_op jit(solution)/shard_map/ppermute | solution.py:408
  21.4 6.5 %copy-start = (f32[3,32,64]{2,1,0:T(8,128)S(1)}, f32[3,32,64]{2,1,0:T(8,128)}, u32[]{:S(2)}) copy-start(f32[3,32,64]{2,1,0:T(8,128)} %refs_5_.8) | copy-start | bytes 73732
  21.4 6.5 %copy-start.1 = (f32[2,768]{1,0:T(2,128)S(1)}, f32[2,768]{1,0:T(2,128)}, u32[]{:S(2)}) copy-start(f32[2,768]{1,0:T(2,128)} %refs_5_.9) | copy-start | bytes 18436
  21.5 6.5 %copy-start.2 = (s32[16]{0:T(128)S(1)}, s32[16]{0:T(128)}, u32[]{:S(2)}) copy-start(s32[16]{0:T(128)} %refs_0_.7) | copy-start | bytes 196
  21.5 6.5 %copy-start.3 = (s32[16]{0:T(128)S(1)}, s32[16]{0:T(128)}, u32[]{:S(2)}) copy-start(s32[16]{0:T(128)} %refs_1_.7) | copy-start | bytes 196
  21.5 5.0 %collective-permute-start.6 = (f32[4,32,128]{2,1,0:T(8,128)S(1)}, f32[4,32,128]{2,1,0:T(8,128)S(1)}, u32[]{:S(2)}, u32[]{:S(2)}) collective-permute-start(f32[4,32,128]{2,1,0:T(8,128)S(1)} %pad_maximum_fusion.1), channel_id=1, source_target_pairs={{0,2},{2,0},{4,6},{6,4},{8,10},{10,8},{12,14},{14,12},{16,18},{18,... | collective-permute-start | bytes 196616 | tf_op jit(solution)/shard_map/ppermute | solution.py:408
  26.5 1.4 %collective-permute-start.8 = (f32[8,32,128]{2,1,0:T(8,128)S(1)}, f32[8,32,128]{2,1,0:T(8,128)S(1)}, u32[]{:S(2)}, u32[]{:S(2)}) collective-permute-start(f32[8,32,128]{2,1,0:T(8,128)S(1)} %pad_maximum_fusion.refs_2_), channel_id=1, source_target_pairs={{0,1},{1,0},{2,3},{3,2},{4,5},{5,4},{6,7},{7,6},{8,9},{9,8},{10,11... | collective-permute-start | bytes 393224 | tf_op jit(solution)/shard_map/ppermute | solution.py:411

commit v10 on v9

--- a/solution.py
+++ b/solution.py
@@ -64,14 +64,14 @@
 
 def keys_kernel(rows, base, shares, *refs):
     own, count = shares == (0,), len(shares)
-    tables, refs = refs[: 2 * count], refs[2 * count :]
+    tables, refs = refs[: 3 * count], refs[3 * count :]
     if own:
         qkv_hbm, out_hbm = refs[:2]
-        total_ref, gram_ref, right_ref, embed, level, small, buf, sems = refs[-8:]
-        brought = started(tables, (embed, level), small)
+        total_ref, gram_ref, gv_ref, right_ref, down_ref, *held, small, buf, sems = refs[-11:]
+        brought = started(tables, held, small)
     else:
-        sum_ref, gram_sum, qkv_hbm, out_hbm = refs[:4]
-        mq_ref, mk_ref, gram_ref, right_ref, buf, sems = refs[-6:]
+        sum_ref, gram_sum, gv_sum, qkv_hbm, out_hbm = refs[:5]
+        mq_ref, mk_ref, gram_ref, gv_ref, right_ref, down_ref, buf, sems = refs[-8:]
     per = out_hbm.shape[0] // rows
     depth = buf.shape[-1]
     copies = chunk_copies(rows, range(2 * per), shares, qkv_hbm, out_hbm, buf, sems)
@@ -80,15 +80,20 @@
     if own:
         for copy in brought:
             copy.wait()
-        tables = (embed, level)
-    gram = jnp.zeros((base, base), F32) if own else gram_sum[...]
+        tables = held
+    gram, gv = (0.0, 0.0) if own else (gram_sum[...], gv_sum[...])
     for at in range(count):
-        left = [tables[2 * at][...].astype(F32), tables[2 * at + 1][...].astype(F32)]
+        spot = slice(at * depth, (at + 1) * depth)
+        left = [tables[3 * at][...].astype(F32), tables[3 * at + 1][...].astype(F32)]
         left.append(jnp.zeros((base - left[0].shape[0] - left[1].shape[0], depth), F32))
         left = jnp.concatenate(left, axis=0)
-        right_ref[at * depth : (at + 1) * depth, :] = left.T.astype(BF16)
-        gram = gram + dot(left.astype(BF16), right_ref[at * depth : (at + 1) * depth, :])
+        vel = tables[3 * at + 2][...]
+        right_ref[spot, :] = left.T.astype(BF16)
+        down_ref[spot, :] = turned(vel)
+        gram = gram + dot(left.astype(BF16), right_ref[spot, :])
+        gv = gv + dot(vel, right_ref[spot, :])
     gram_ref[...] = gram if own else halves(gram, 1)
+    gv_ref[...] = gv if own else halves(gv, 1)
     for chunk in range(2 * per):
         spot = slice(chunk * rows, (chunk + 1) * rows)
         total = None if own else sum_ref[spot, :]
@@ -105,35 +110,23 @@
             mk_ref[:, where] = halves(total.T, 0)
 
 
-def values_kernel(rows, shares, *refs):
+def values_kernel(rows, shares, right_ref, down_ref, *refs):
     own, count = shares == (0,), len(shares)
-    tables, right_ref, refs = refs[:count], refs[count], refs[count + 1 :]
-    if own:
-        qkv_hbm, out_hbm = refs[:2]
-        mv_ref, wo_ref, gv_ref, held, small, buf, sems = refs[-7:]
-        brought = started(tables, (held,), small)
-    else:
-        mv_sum, wo_sum, gv_sum, qkv_hbm, out_hbm = refs[:5]
-        mv_ref, wo_ref, gv_ref, buf, sems = refs[-5:]
+    sums, refs = ((), refs) if own else (refs[:2], refs[2:])
+    qkv_hbm, out_hbm = refs[:2]
+    mv_ref, wo_ref, buf, sems = refs[-4:]
     per = out_hbm.shape[0] // rows
     depth = buf.shape[-1]
     copies = chunk_copies(rows, range(2 * per, 4 * per), shares, qkv_hbm, out_hbm, buf, sems)
     for copy in copies.values():
         copy.start()
-    if own:
-        brought[0].wait()
-        tables = (held,)
-    vels = [table[...] for table in tables]
-    gv = sum(dot(vel, right_ref[at * depth : (at + 1) * depth, :]) for at, vel in enumerate(vels))
-    gv_ref[...] = gv if own else halves(gv_sum[...] + gv, 1)
-    downs = [turned(vel) for vel in vels]
     for place in range(2 * per):
         where = slice((place % per) * rows, (place % per + 1) * rows)
-        total = None if own else (mv_sum if place < per else wo_sum)[where, :]
+        total = None if own else sums[place // per][where, :]
+        factor = right_ref if place < per else down_ref
         for at in range(count):
             copies[place, at].wait()
-            right = right_ref[at * depth : (at + 1) * depth, :] if place < per else downs[at]
-            product = dot(buf[at, place], right)
+            product = dot(buf[at, place], factor[at * depth : (at + 1) * depth, :])
             total = product if total is None else total + product
         if own:
             (mv_ref if place < per else wo_ref)[where, :] = total
@@ -413,8 +406,7 @@
     share = depth // parts
     table = (embed_weight, level_embed, vel_weight.T)
     around = range(1, parts)
-    tables = [from_ahead(piece, d) for d in around for piece in table[:2]]
-    vel_tables = [from_ahead(table[2], d) for d in around]
+    tables = [from_ahead(piece, d) for d in around for piece in table]
     noise = [from_ahead(fresh_noise, d) for d in around]
     in_hbm = lambda array: pltpu.with_memory_space_constraint(array, pltpu.HBM)
     table = tuple(in_hbm(piece) for piece in table)
@@ -448,33 +440,29 @@
 
     keys_part = lambda shares, *refs: keys_kernel(rows, base, shares, *refs)
     values_part = lambda shares, *refs: values_kernel(rows, shares, *refs)
-    right = lambda count: shape((count * share, base), BF16)
+    turned_tables = lambda count: [shape((count * share, base), BF16), shape((count * share, channels), BF16)]
     others = tuple(around)
 
     def own_keys(*after):
-        outs = [shape((2 * width, base), F32), shape((base, base), F32), right(1)]
-        return weights(keys_part, (0,), outs, table[:2], after, *table[:2])
+        outs = [shape((2 * width, base), F32), shape((base, base), F32), shape((channels, base), F32)]
+        return weights(keys_part, (0,), outs + turned_tables(1), table, after, *table)
 
     def own_values(*after):
-        outs = [shape((width, base), F32), shape((width, channels), F32), shape((channels, base), F32)]
-        return weights(values_part, (0,), outs, table[2:], after, table[2], done[0][2])
+        outs = [shape((width, base), F32), shape((width, channels), F32)]
+        return weights(values_part, (0,), outs, (), after, *done[0][3:])
 
     def other_keys(*after):
         outs = [
             shape((width, 2 * base), BF16),
             shape((2 * base, width), BF16),
             shape((base, 2 * base), BF16),
-            right(parts - 1),
-        ]
-        return weights(keys_part, others, outs, (), after, *tables, *done[0][:2])
-
-    def other_values(*after):
-        outs = [
-            shape((width, 2 * base), BF16),
-            shape((2 * channels, width), BF16),
             shape((channels, 2 * base), BF16),
         ]
-        return weights(values_part, others, outs, (), after, *vel_tables, done[2][3], *done[1])
+        return weights(keys_part, others, outs + turned_tables(parts - 1), (), after, *tables, *done[0][:3])
+
+    def other_values(*after):
+        outs = [shape((width, 2 * base), BF16), shape((2 * channels, width), BF16)]
+        return weights(values_part, others, outs, (), after, *done[2][4:], *done[1])
 
     state = latent
     work = [own_keys, own_values, other_keys, other_values]
@@ -492,8 +480,8 @@
     while len(done) < len(work):
         done.append(work[len(done)]())
     latents = [state] + [from_ahead(state, d) for d in range(1, parts)] + noise
-    mq, mk, gram = done[2][:3]
-    mv, wo, gv = done[3]
+    mq, mk, gram, gv = done[2][:4]
+    mv, wo = done[3]
 
     query_block = max(1, LANES // tok)
     owned = []

time: 93.6 us -> 93.5 us (level)
  no operation moved by 1% of the time
where the time goes in v10:
time: 93.5 us
  Pallas kernels  75.5 us (81%)
  starting transfers between devices  9.65 us (10%)
  blocking collectives  5.98 us (6%)
  waiting for transfers between devices  1.36 us (1%)
    pallas_call x3, Pallas kernels, body(): pl.pallas_call(functools.partial(step_kernel, step, cfg), out_shape=tuple...  58.8 us
    pallas_call x4, Pallas kernels, weights(): pl.pallas_call(functools.partial(kernel, shares), out_shape=tuple(outs),...  16 us
    ppermute x4, starting transfers between devices, swapped(): lax.ppermute(value, axis, [(source, source ^ distance) for source in rang...  8.39 us
    all_gather x3, blocking collectives, body(): gathered = lax.all_gather(part, 'tok', axis=0, tiled=False)  5.98 us
  transfers between devices with their start and end apart: 9, of which 1 were waited for; matrix products, arithmetic and copies ran while one was open for 0% of the time, Pallas kernels for 17%

profile of v10, /device:TPU:0, one launch (start us, length us, event | category | flops | bytes accessed | tf_op | source)
XLA Modules:
  0.0 93.5 jit_solution(6523061505892877087)
XLA Ops:
  0.6 0.5 collective-permute-start.1
  1.2 3.7 %collective-permute-start = (f32[1,32,64]{2,1,0:T(8,128)}, f32[1,32,64]{2,1,0:T(8,128)S(1)}, u32[]{:S(2)}, u32[]{:S(2)}) collective-permute-start(f32[1,32,64]{2,1,0:T(8,128)} %param.10), channel_id=1, source_target_pairs={{0,16},{2,18},{4,20},{6,22},{8,24},{10,26},{12,28},{14,30},{16,0},... | collective-permute-start | bytes 24584 | tf_op jit(solution)/shard_map/ppermute | solution.py:401
  4.8 0.2 collective-permute-start.6
  5.0 0.3 collective-permute-start.4
  5.3 0.2 collective-permute-start.5
  5.5 4.6 %weights.4 = (f32[1536,128]{1,0:T(8,128)S(1)}, f32[128,128]{1,0:T(8,128)S(1)}, f32[64,128]{1,0:T(8,128)S(1)}, bf16[1536,128]{1,0:T(8,128)(2,1)S(1)}, bf16[1536,64]{1,0:T(8,128)(2,1)S(1)}) custom-call(bf16[64,1536]{1,0:T(8,128)(2,1)} %refs_0_.4, bf16[19,1536]{1,0:T(8,128)(2,1)} %refs_1_.4, bf16[64,1536]{1,0:T(8,128)(2,1)} %bitcast.8, ...), custom_call_target="tpu_custom_call" | custom-call | flops 603979776 | bytes 4718592 | tf_op jit(solution)/shard_map/weights/pallas_call | solution.py:423
  10.1 0.1 pad_maximum_fusion.3
  10.2 1.6 %collective-permute-start.2 = (f32[1,32,128]{2,1,0:T(8,128)S(1)}, f32[1,32,128]{2,1,0:T(8,128)S(1)}, u32[]{:S(2)}, u32[]{:S(2)}) collective-permute-start(f32[1,32,128]{2,1,0:T(8,128)S(1)} %pad_maximum_fusion.3), channel_id=1, source_target_pairs={{0,8},{2,10},{4,12},{6,14},{8,0},{10,2},{12,4},{14,6},{16,24},{18,... | collective-permute-start | bytes 49160 | tf_op jit(solution)/shard_map/ppermute | solution.py:401
  11.8 4.3 %weights.5 = (f32[768,128]{1,0:T(8,128)S(1)}, f32[768,64]{1,0:T(8,128)S(1)}) custom-call(bf16[1536,128]{1,0:T(8,128)(2,1)S(1)} %get-tuple-element.58.refs_0_, bf16[1536,64]{1,0:T(8,128)(2,1)S(1)} %get-tuple-element.59.refs_1_, bf16[3,768,3072]{2,1,0:T(8,128)(2,1)} %refs_4_.3, bf16[768,3072]{1,0:T(8,128)(2,1)} %refs_5_.4, ...), custom_call_target="tpu_custom_call" | custom-call | flops 603979776 | bytes 4718592 | tf_op jit(solution)/shard_map/weights/pallas_call | solution.py:423
  16.1 1.6 %collective-permute-start.3 = (f32[2,32,128]{2,1,0:T(8,128)S(1)}, f32[2,32,128]{2,1,0:T(8,128)S(1)}, u32[]{:S(2)}, u32[]{:S(2)}) collective-permute-start(f32[2,32,128]{2,1,0:T(8,128)S(1)} %pad_maximum_fusion.2), channel_id=1, source_target_pairs={{0,4},{2,6},{4,0},{6,2},{8,12},{10,14},{12,8},{14,10},{16,20},{18,... | collective-permute-start | bytes 98312 | tf_op jit(solution)/shard_map/ppermute | solution.py:401
  17.7 3.7 %weights.6 = (bf16[768,256]{1,0:T(8,128)(2,1)S(1)}, bf16[256,768]{1,0:T(8,128)(2,1)S(1)}, bf16[128,256]{1,0:T(8,128)(2,1)S(1)}, bf16[64,256]{1,0:T(8,128)(2,1)S(...) custom-call(bf16[64,1536]{1,0:T(8,128)(2,1)S(1)} %collective-permute-done.4.refs_0_, ...), custom_call_target="tpu_custom_call" | custom-call | flops 603979776 | bytes 4718592 | tf_op jit(solution)/shard_map/weights/pallas_call | solution.py:423
  21.5 0.0 copy-start.2
  21.5 0.0 copy-start.3
  21.5 1.6 %collective-permute-start.7 = (f32[4,32,128]{2,1,0:T(8,128)S(1)}, f32[4,32,128]{2,1,0:T(8,128)S(1)}, u32[]{:S(2)}, u32[]{:S(2)}) collective-permute-start(f32[4,32,128]{2,1,0:T(8,128)S(1)} %pad_maximum_fusion.1), channel_id=1, source_target_pairs={{0,2},{2,0},{4,6},{6,4},{8,10},{10,8},{12,14},{14,12},{16,18},{18,... | collective-permute-start | bytes 196616 | tf_op jit(solution)/shard_map/ppermute | solution.py:401
  23.1 3.4 %weights.7 = (bf16[768,256]{1,0:T(8,128)(2,1)S(1)}, bf16[128,768]{1,0:T(8,128)(2,1)S(1)}) custom-call(bf16[1536,128]{1,0:T(8,128)(2,1)S(1)} %get-tuple-element.75.refs_0_, bf16[1536,64]{1,0:T(8,128)(2,1)S(1)} %get-tuple-element.76.refs_1_, f32[768,128]{1,0:T(8,128)S(1)} %get-tuple-element.77.refs_2_, f32[768,64]{1,0:T(8,128)S(1)} %get-tuple-element.78.refs_3_, ...), custom_call_target="tpu_custom_call" | custom-call | flops 603979776 | bytes 4718592 | tf_op jit(solution)/shard_map/weights/pallas_call | solution.py:423
  26.5 0.1 collective-permute-start.8
  26.6 1.3 %collective-permute-done.8.refs_3_ = f32[8,32,128]{2,1,0:T(8,128)S(1)} collective-permute-done((f32[8,32,128]{2,1,0:T(8,128)S(1)}, f32[8,32,128]{2,1,0:T(8,128)S(1)}, u32[]{:S(2)}, u32[]{:S(2)}) %collective-permute-start.8) | collective-permute-done | bytes 131104 | tf_op jit(solution)/shard_map/ppermute | solution.py:404
  27.9 33.3 %step0.1 = (f32[64,896]{1,0:T(8,128)S(1)}, f32[64,896]{1,0:T(8,128)S(1)}, f32[64,896]{1,0:T(8,128)S(1)}) custom-call(s32[16]{0:T(128)S(1)} %copy-done.2, s32[16]{0:T(128)S(1)} %copy-done.3, f32[8,32,128]{2,1,0:T(8,128)S(1)} %pad_maximum_fusion.refs_2_, f32[8,32,128]{2,1,0:T(8,128)S(1)} %collective-permute-done.8.refs_3_, ...), custom_call_target="tpu_custom_call" | custom-call | flops 2919235584 | bytes 786432 | tf_op jit(solution)/shard_map/step0/pallas_call | solution.py:508
  61.3 2.1 %all-gather = f32[128,896]{1,0:T(8,128)S(1)} all-gather(f32[64,896]{1,0:T(8,128)S(1)} %get-tuple-element.89), channel_id=2, replica_groups=mesh['queue'=16,'tok'=2] {'tok'}, dimensions={0}, use_global_device_ids=true | all-gather | bytes 688128 | tf_op jit(solution)/shard_map/all_gather | solution.py:531
  63.4 19.5 %step1.1 = (f32[64,512]{1,0:T(8,128)S(1)}, f32[64,512]{1,0:T(8,128)S(1)}, f32[64,512]{1,0:T(8,128)S(1)}, f32[32,64]{1,0:T(8,128)S(1)}) custom-call(s32[16]{0:T(128)S(1)} %copy-done.2, s32[16]{0:T(128)S(1)} %copy-done.3, f32[2,64,896]{2,1,0:T(8,128)S(1)} %bitcast.4, f32[64,896]{1,0:T(8,128)S(1)} %get-tuple-element.90.refs_3_, ...), custom_call_target="tpu_custom_call" | custom-call | flops 1862270976 | bytes 786432 | tf_op jit(solution)/shard_map/step1/pallas_call | solution.py:508
  82.9 2.0 %all-gather.1 = f32[128,512]{1,0:T(8,128)S(1)} all-gather(f32[64,512]{1,0:T(8,128)S(1)} %get-tuple-element.92), channel_id=3, replica_groups=mesh['queue'=16,'tok'=2] {'tok'}, dimensions={0}, use_global_device_ids=true | all-gather | bytes 393216 | tf_op jit(solution)/shard_map/all_gather | solution.py:531
  84.9 6.0 %step2.1 = (f32[64,128]{1,0:T(8,128)S(1)}, f32[64,128]{1,0:T(8,128)S(1)}, f32[64,128]{1,0:T(8,128)S(1)}, f32[32,64]{1,0:T(8,128)S(1)}) custom-call(s32[16]{0:T(128)S(1)} %copy-done.2, s32[16]{0:T(128)S(1)} %copy-done.3, f32[2,64,512]{2,1,0:T(8,128)S(1)} %bitcast.5, f32[64,512]{1,0:T(8,128)S(1)} %get-tuple-element.93.refs_3_, ...), custom_call_target="tpu_custom_call" | custom-call | flops 805306368 | bytes 786432 | tf_op jit(solution)/shard_map/step2/pallas_call | solution.py:508
  90.9 1.9 %all-gather.2 = f32[128,128]{1,0:T(8,128)S(1)} all-gather(f32[64,128]{1,0:T(8,128)S(1)} %get-tuple-element.95), channel_id=4, replica_groups=mesh['queue'=16,'tok'=2] {'tok'}, dimensions={0}, use_global_device_ids=true | all-gather | bytes 98304 | tf_op jit(solution)/shard_map/all_gather | solution.py:531
  92.8 0.7 last.1
  (19 shorter events, 0.1 us)
Async XLA Ops:
  0.6 9.5 %copy-start.4 = (f32[1,32,64]{2,1,0:T(8,128)S(1)}, f32[1,32,64]{2,1,0:T(8,128)}, u32[]{:S(2)}) copy-start(f32[1,32,64]{2,1,0:T(8,128)} %param.10) | copy-start | bytes 24580
  0.6 9.5 %collective-permute-start.1 = (f32[3,32,64]{2,1,0:T(8,128)}, f32[3,32,64]{2,1,0:T(8,128)S(1)}, u32[]{:S(2)}, u32[]{:S(2)}) collective-permute-start(f32[3,32,64]{2,1,0:T(8,128)} %refs_5_.6), channel_id=1, source_target_pairs={{0,1},{1,0},{2,3},{3,2},{4,5},{5,4},{6,7},{7,6},{8,9},{9,8},{10,11... | collective-permute-start | bytes 73736 | tf_op jit(solution)/shard_map/ppermute | solution.py:404
  1.2 8.9 %collective-permute-start = (f32[1,32,64]{2,1,0:T(8,128)}, f32[1,32,64]{2,1,0:T(8,128)S(1)}, u32[]{:S(2)}, u32[]{:S(2)}) collective-permute-start(f32[1,32,64]{2,1,0:T(8,128)} %param.10), channel_id=1, source_target_pairs={{0,16},{2,18},{4,20},{6,22},{8,24},{10,26},{12,28},{14,30},{16,0},... | collective-permute-start | bytes 24584 | tf_op jit(solution)/shard_map/ppermute | solution.py:401
  4.8 12.9 %collective-permute-start.6 = (bf16[64,1536]{1,0:T(8,128)(2,1)}, bf16[64,1536]{1,0:T(8,128)(2,1)S(1)}, u32[]{:S(2)}, u32[]{:S(2)}) collective-permute-start(bf16[64,1536]{1,0:T(8,128)(2,1)} %bitcast.7), channel_id=1, source_target_pairs={{0,1},{1,0},{2,3},{3,2},{4,5},{5,4},{6,7},{7,6},{8,9},{9,8},{10,11... | collective-permute-start | bytes 589832 | tf_op jit(solution)/shard_map/ppermute | solution.py:404
  5.0 12.8 %collective-permute-start.4 = (bf16[64,1536]{1,0:T(8,128)(2,1)}, bf16[64,1536]{1,0:T(8,128)(2,1)S(1)}, u32[]{:S(2)}, u32[]{:S(2)}) collective-permute-start(bf16[64,1536]{1,0:T(8,128)(2,1)} %refs_0_.4), channel_id=1, source_target_pairs={{0,1},{1,0},{2,3},{3,2},{4,5},{5,4},{6,7},{7,6},{8,9},{9,8},{10,11... | collective-permute-start | bytes 589832 | tf_op jit(solution)/shard_map/ppermute | solution.py:404
  5.3 12.4 %collective-permute-start.5 = (bf16[19,1536]{1,0:T(8,128)(2,1)}, bf16[19,1536]{1,0:T(8,128)(2,1)S(1)}, u32[]{:S(2)}, u32[]{:S(2)}) collective-permute-start(bf16[19,1536]{1,0:T(8,128)(2,1)} %refs_1_.4), channel_id=1, source_target_pairs={{0,1},{1,0},{2,3},{3,2},{4,5},{5,4},{6,7},{7,6},{8,9},{9,8},{10,11... | collective-permute-start | bytes 175112 | tf_op jit(solution)/shard_map/ppermute | solution.py:404
  10.2 5.9 %collective-permute-start.2 = (f32[1,32,128]{2,1,0:T(8,128)S(1)}, f32[1,32,128]{2,1,0:T(8,128)S(1)}, u32[]{:S(2)}, u32[]{:S(2)}) collective-permute-start(f32[1,32,128]{2,1,0:T(8,128)S(1)} %pad_maximum_fusion.3), channel_id=1, source_target_pairs={{0,8},{2,10},{4,12},{6,14},{8,0},{10,2},{12,4},{14,6},{16,24},{18,... | collective-permute-start | bytes 49160 | tf_op jit(solution)/shard_map/ppermute | solution.py:401
  16.1 5.3 %collective-permute-start.3 = (f32[2,32,128]{2,1,0:T(8,128)S(1)}, f32[2,32,128]{2,1,0:T(8,128)S(1)}, u32[]{:S(2)}, u32[]{:S(2)}) collective-permute-start(f32[2,32,128]{2,1,0:T(8,128)S(1)} %pad_maximum_fusion.2), channel_id=1, source_target_pairs={{0,4},{2,6},{4,0},{6,2},{8,12},{10,14},{12,8},{14,10},{16,20},{18,... | collective-permute-start | bytes 98312 | tf_op jit(solution)/shard_map/ppermute | solution.py:401
  21.4 6.5 %copy-start = (f32[3,32,64]{2,1,0:T(8,128)S(1)}, f32[3,32,64]{2,1,0:T(8,128)}, u32[]{:S(2)}) copy-start(f32[3,32,64]{2,1,0:T(8,128)} %refs_5_.6) | copy-start | bytes 73732
  21.5 6.5 %copy-start.1 = (f32[2,768]{1,0:T(2,128)S(1)}, f32[2,768]{1,0:T(2,128)}, u32[]{:S(2)}) copy-start(f32[2,768]{1,0:T(2,128)} %refs_5_.7) | copy-start | bytes 18436
  21.5 6.4 %copy-start.2 = (s32[16]{0:T(128)S(1)}, s32[16]{0:T(128)}, u32[]{:S(2)}) copy-start(s32[16]{0:T(128)} %refs_0_.7) | copy-start | bytes 196
  21.5 6.4 %copy-start.3 = (s32[16]{0:T(128)S(1)}, s32[16]{0:T(128)}, u32[]{:S(2)}) copy-start(s32[16]{0:T(128)} %refs_1_.7) | copy-start | bytes 196
  21.5 5.0 %collective-permute-start.7 = (f32[4,32,128]{2,1,0:T(8,128)S(1)}, f32[4,32,128]{2,1,0:T(8,128)S(1)}, u32[]{:S(2)}, u32[]{:S(2)}) collective-permute-start(f32[4,32,128]{2,1,0:T(8,128)S(1)} %pad_maximum_fusion.1), channel_id=1, source_target_pairs={{0,2},{2,0},{4,6},{6,4},{8,10},{10,8},{12,14},{14,12},{16,18},{18,... | collective-permute-start | bytes 196616 | tf_op jit(solution)/shard_map/ppermute | solution.py:401
  26.5 1.4 %collective-permute-start.8 = (f32[8,32,128]{2,1,0:T(8,128)S(1)}, f32[8,32,128]{2,1,0:T(8,128)S(1)}, u32[]{:S(2)}, u32[]{:S(2)}) collective-permute-start(f32[8,32,128]{2,1,0:T(8,128)S(1)} %pad_maximum_fusion.refs_2_), channel_id=1, source_target_pairs={{0,1},{1,0},{2,3},{3,2},{4,5},{5,4},{6,7},{7,6},{8,9},{9,8},{10,11... | collective-permute-start | bytes 393224 | tf_op jit(solution)/shard_map/ppermute | solution.py:404

commit v11 on v9

--- a/solution.py
+++ b/solution.py
@@ -100,9 +100,9 @@
         if own:
             total_ref[spot, :] = total
         elif chunk < per:
-            mq_ref[where, :] = halves(total, 1)
+            mq_ref[where, :] = total.astype(BF16)
         else:
-            mk_ref[:, where] = halves(total.T, 0)
+            mk_ref[:, where] = total.T.astype(BF16)
 
 
 def values_kernel(rows, shares, *refs):
@@ -138,7 +138,7 @@
         if own:
             (mv_ref if place < per else wo_ref)[where, :] = total
         elif place < per:
-            mv_ref[where, :] = halves(total, 1)
+            mv_ref[where, :] = total.astype(BF16)
         else:
             wo_ref[:, where] = halves(total.T, 0)
 
@@ -230,7 +230,6 @@
     aug = jnp.where(last_row, EPS * mean_t, aug_t).T
     eps_c = aug[:, base - 1 : base]
     aug_b = aug.astype(BF16)
-    both = jnp.concatenate([aug_b, aug_b], axis=1)
 
     hpart_ref[...] = dot(gv_ref[...], both_q)
     xq_ref[...] = state[:, queries]
@@ -240,11 +239,11 @@
     head_of = lambda axis: lax.broadcasted_iota(jnp.int32, (span, span), axis) // HD
     average = jnp.where(head_of(0) == head_of(1), 1.0 / HD, 0.0).astype(BF16)
     for at in range(0, width, span):
-        raw = dot(both, mk_ref[:, at : at + span])
+        raw = dot(aug_b, mk_ref[:, at : at + span])
         spread = dot((raw * raw).astype(BF16), average)
         kbuf[:, at : at + span] = (raw * lax.rsqrt(spread + eps_c) * gain[:, at : at + span]).astype(BF16)
-    vbuf[...] = (dot(mv_ref[...], both_t) * lax.rsqrt(mean_t)).astype(BF16)
-    raw = dot(mq_ref[...], both_q).reshape(heads, HD, query_lanes)
+    vbuf[...] = (dot(mv_ref[...], aug_tb) * lax.rsqrt(mean_t)).astype(BF16)
+    raw = dot(mq_ref[...], aug_qb).reshape(heads, HD, query_lanes)
     spread = jnp.sum(raw * raw, axis=1, keepdims=True) * (1.0 / HD)
     qbuf[...] = (raw * lax.rsqrt(spread + EPS * mean_q)[:, :, :]).reshape(width, query_lanes).astype(BF16)
 
@@ -461,8 +460,8 @@
 
     def other_keys(*after):
         outs = [
-            shape((width, 2 * base), BF16),
-            shape((2 * base, width), BF16),
+            shape((width, base), BF16),
+            shape((base, width), BF16),
             shape((base, 2 * base), BF16),
             right(parts - 1),
         ]
@@ -470,7 +469,7 @@
 
     def other_values(*after):
         outs = [
-            shape((width, 2 * base), BF16),
+            shape((width, base), BF16),
             shape((2 * channels, width), BF16),
             shape((channels, 2 * base), BF16),
         ]

time: 93.6 us -> 94.1 us (level)
  no operation moved by 1% of the time
where the time goes in v11:
time: 94.1 us; the launch traced here: 94 us
  Pallas kernels  76 us (81%)
  starting transfers between devices  9.65 us (10%)
  blocking collectives  5.98 us (6%)
  waiting for transfers between devices  1.36 us (1%)
    pallas_call x3, Pallas kernels, body(): pl.pallas_call(functools.partial(step_kernel, step, cfg), out_shape=tuple...  59.3 us
    pallas_call x4, Pallas kernels, weights(): pl.pallas_call(functools.partial(kernel, shares), out_shape=tuple(outs),...  16 us
    ppermute x4, starting transfers between devices, swapped(): lax.ppermute(value, axis, [(source, source ^ distance) for source in rang...  8.39 us
    all_gather x3, blocking collectives, body(): gathered = lax.all_gather(part, 'tok', axis=0, tiled=False)  5.98 us
  transfers between devices with their start and end apart: 9, of which 1 were waited for; matrix products, arithmetic and copies ran while one was open for 0% of the time, Pallas kernels for 17%

profile of v11, /device:TPU:0, one launch (start us, length us, event | category | flops | bytes accessed | tf_op | source)
XLA Modules:
  0.0 94.0 jit_solution(10511721212172824923)
XLA Ops:
  0.6 0.5 collective-permute-start.1
  1.2 3.7 %collective-permute-start = (f32[1,32,64]{2,1,0:T(8,128)}, f32[1,32,64]{2,1,0:T(8,128)S(1)}, u32[]{:S(2)}, u32[]{:S(2)}) collective-permute-start(f32[1,32,64]{2,1,0:T(8,128)} %param.10), channel_id=1, source_target_pairs={{0,16},{2,18},{4,20},{6,22},{8,24},{10,26},{12,28},{14,30},{16,0},... | collective-permute-start | bytes 24584 | tf_op jit(solution)/shard_map/ppermute | solution.py:407
  4.8 0.2 collective-permute-start.4
  5.0 0.3 collective-permute-start.5
  5.3 0.2 collective-permute-start.7
  5.5 4.5 %weights.4 = (f32[1536,128]{1,0:T(8,128)S(1)}, f32[128,128]{1,0:T(8,128)S(1)}, bf16[1536,128]{1,0:T(8,128)(2,1)S(1)}) custom-call(bf16[64,1536]{1,0:T(8,128)(2,1)} %refs_0_.4, bf16[19,1536]{1,0:T(8,128)(2,1)} %refs_1_.4, bf16[3,768,3072]{2,1,0:T(8,128)(2,1)} %refs_5_.6, bf16[768,3072]{1,0:T(8,128)(2,1)} %refs_6_.3), custom_call_target="tpu_custom_call" | custom-call | flops 603979776 | bytes 4718592 | tf_op jit(solution)/shard_map/weights/pallas_call | solution.py:430
  10.0 0.1 pad_maximum_fusion.3
  10.1 1.6 %collective-permute-start.2 = (f32[1,32,128]{2,1,0:T(8,128)S(1)}, f32[1,32,128]{2,1,0:T(8,128)S(1)}, u32[]{:S(2)}, u32[]{:S(2)}) collective-permute-start(f32[1,32,128]{2,1,0:T(8,128)S(1)} %pad_maximum_fusion.3), channel_id=1, source_target_pairs={{0,8},{2,10},{4,12},{6,14},{8,0},{10,2},{12,4},{14,6},{16,24},{18,... | collective-permute-start | bytes 49160 | tf_op jit(solution)/shard_map/ppermute | solution.py:407
  11.7 4.4 %weights.5 = (f32[768,128]{1,0:T(8,128)S(1)}, f32[768,64]{1,0:T(8,128)S(1)}, f32[64,128]{1,0:T(8,128)S(1)}) custom-call(bf16[64,1536]{1,0:T(8,128)(2,1)} %bitcast.8, bf16[1536,128]{1,0:T(8,128)(2,1)S(1)} %get-tuple-element.52.refs_1_, bf16[3,768,3072]{2,1,0:T(8,128)(2,1)} %refs_5_.6, bf16[768,3072]{1,0:T(8,128)(2,1)} %refs_6_.3, ...), custom_call_target="tpu_custom_call" | custom-call | flops 603979776 | bytes 4718592 | tf_op jit(solution)/shard_map/weights/pallas_call | solution.py:430
  16.2 1.6 %collective-permute-start.3 = (f32[2,32,128]{2,1,0:T(8,128)S(1)}, f32[2,32,128]{2,1,0:T(8,128)S(1)}, u32[]{:S(2)}, u32[]{:S(2)}) collective-permute-start(f32[2,32,128]{2,1,0:T(8,128)S(1)} %pad_maximum_fusion.2), channel_id=1, source_target_pairs={{0,4},{2,6},{4,0},{6,2},{8,12},{10,14},{12,8},{14,10},{16,20},{18,... | collective-permute-start | bytes 98312 | tf_op jit(solution)/shard_map/ppermute | solution.py:407
  17.8 3.6 %weights.6 = (bf16[768,128]{1,0:T(8,128)(2,1)S(1)}, bf16[128,768]{1,0:T(8,128)(2,1)S(1)}, bf16[128,256]{1,0:T(8,128)(2,1)S(1)}, bf16[1536,128]{1,0:T(8,128)(2,1)S(1)}) custom-call(bf16[64,1536]{1,0:T(8,128)(2,1)S(1)} %collective-permute-done.4.refs_0_, bf16[19,1536]{1,0:T(8,128)(2,1)S(1)} %collective-permute-done.5.refs_1_, ...), custom_call_target="tpu_custom_call" | custom-call | flops 603979776 | bytes 4718592 | tf_op jit(solution)/shard_map/weights/pallas_call | solution.py:430
  21.4 0.0 copy-start.1
  21.4 0.0 copy-start.2
  21.5 1.6 %collective-permute-start.6 = (f32[4,32,128]{2,1,0:T(8,128)S(1)}, f32[4,32,128]{2,1,0:T(8,128)S(1)}, u32[]{:S(2)}, u32[]{:S(2)}) collective-permute-start(f32[4,32,128]{2,1,0:T(8,128)S(1)} %pad_maximum_fusion.1), channel_id=1, source_target_pairs={{0,2},{2,0},{4,6},{6,4},{8,10},{10,8},{12,14},{14,12},{16,18},{18,... | collective-permute-start | bytes 196616 | tf_op jit(solution)/shard_map/ppermute | solution.py:407
  23.0 3.4 %weights.7 = (bf16[768,128]{1,0:T(8,128)(2,1)S(1)}, bf16[128,768]{1,0:T(8,128)(2,1)S(1)}, bf16[64,256]{1,0:T(8,128)(2,1)S(1)}) custom-call(bf16[64,1536]{1,0:T(8,128)(2,1)S(1)} %collective-permute-done.7.refs_0_, bf16[1536,128]{1,0:T(8,128)(2,1)S(1)} %get-tuple-element.66.refs_1_, f32[768,128]{1,0:T(8,128)S(1)} %get-tuple-element.67.refs_2_, ...), custom_call_target="tpu_custom_call" | custom-call | flops 603979776 | bytes 4718592 | tf_op jit(solution)/shard_map/weights/pallas_call | solution.py:430
  26.5 0.1 collective-permute-start.8
  26.6 1.3 %collective-permute-done.8.refs_3_ = f32[8,32,128]{2,1,0:T(8,128)S(1)} collective-permute-done((f32[8,32,128]{2,1,0:T(8,128)S(1)}, f32[8,32,128]{2,1,0:T(8,128)S(1)}, u32[]{:S(2)}, u32[]{:S(2)}) %collective-permute-start.8) | collective-permute-done | bytes 131104 | tf_op jit(solution)/shard_map/ppermute | solution.py:410
  28.0 33.4 %step0.1 = (f32[64,896]{1,0:T(8,128)S(1)}, f32[64,896]{1,0:T(8,128)S(1)}, f32[64,896]{1,0:T(8,128)S(1)}) custom-call(s32[16]{0:T(128)S(1)} %copy-done.2, s32[16]{0:T(128)S(1)} %copy-done.3, f32[8,32,128]{2,1,0:T(8,128)S(1)} %pad_maximum_fusion.refs_2_, f32[8,32,128]{2,1,0:T(8,128)S(1)} %collective-permute-done.8.refs_3_, ...), custom_call_target="tpu_custom_call" | custom-call | flops 2919235584 | bytes 786432 | tf_op jit(solution)/shard_map/step0/pallas_call | solution.py:519
  61.3 2.1 %all-gather = f32[128,896]{1,0:T(8,128)S(1)} all-gather(f32[64,896]{1,0:T(8,128)S(1)} %get-tuple-element.81), channel_id=2, replica_groups=mesh['queue'=16,'tok'=2] {'tok'}, dimensions={0}, use_global_device_ids=true | all-gather | bytes 688128 | tf_op jit(solution)/shard_map/all_gather | solution.py:542
  63.5 19.6 %step1.1 = (f32[64,512]{1,0:T(8,128)S(1)}, f32[64,512]{1,0:T(8,128)S(1)}, f32[64,512]{1,0:T(8,128)S(1)}, f32[32,64]{1,0:T(8,128)S(1)}) custom-call(s32[16]{0:T(128)S(1)} %copy-done.2, s32[16]{0:T(128)S(1)} %copy-done.3, f32[2,64,896]{2,1,0:T(8,128)S(1)} %bitcast.4, f32[64,896]{1,0:T(8,128)S(1)} %get-tuple-element.82.refs_3_, ...), custom_call_target="tpu_custom_call" | custom-call | flops 1862270976 | bytes 786432 | tf_op jit(solution)/shard_map/step1/pallas_call | solution.py:519
  83.1 2.0 %all-gather.1 = f32[128,512]{1,0:T(8,128)S(1)} all-gather(f32[64,512]{1,0:T(8,128)S(1)} %get-tuple-element.84), channel_id=3, replica_groups=mesh['queue'=16,'tok'=2] {'tok'}, dimensions={0}, use_global_device_ids=true | all-gather | bytes 393216 | tf_op jit(solution)/shard_map/all_gather | solution.py:542
  85.1 6.3 %step2.1 = (f32[64,128]{1,0:T(8,128)S(1)}, f32[64,128]{1,0:T(8,128)S(1)}, f32[64,128]{1,0:T(8,128)S(1)}, f32[32,64]{1,0:T(8,128)S(1)}) custom-call(s32[16]{0:T(128)S(1)} %copy-done.2, s32[16]{0:T(128)S(1)} %copy-done.3, f32[2,64,512]{2,1,0:T(8,128)S(1)} %bitcast.5, f32[64,512]{1,0:T(8,128)S(1)} %get-tuple-element.85.refs_3_, ...), custom_call_target="tpu_custom_call" | custom-call | flops 805306368 | bytes 786432 | tf_op jit(solution)/shard_map/step2/pallas_call | solution.py:519
  91.4 1.9 %all-gather.2 = f32[128,128]{1,0:T(8,128)S(1)} all-gather(f32[64,128]{1,0:T(8,128)S(1)} %get-tuple-element.87), channel_id=4, replica_groups=mesh['queue'=16,'tok'=2] {'tok'}, dimensions={0}, use_global_device_ids=true | all-gather | bytes 98304 | tf_op jit(solution)/shard_map/all_gather | solution.py:542
  93.3 0.7 last.1
  (19 shorter events, 0.1 us)
Async XLA Ops:
  0.6 9.4 %copy-start.4 = (f32[1,32,64]{2,1,0:T(8,128)S(1)}, f32[1,32,64]{2,1,0:T(8,128)}, u32[]{:S(2)}) copy-start(f32[1,32,64]{2,1,0:T(8,128)} %param.10) | copy-start | bytes 24580
  0.6 9.4 %collective-permute-start.1 = (f32[3,32,64]{2,1,0:T(8,128)}, f32[3,32,64]{2,1,0:T(8,128)S(1)}, u32[]{:S(2)}, u32[]{:S(2)}) collective-permute-start(f32[3,32,64]{2,1,0:T(8,128)} %refs_5_.8), channel_id=1, source_target_pairs={{0,1},{1,0},{2,3},{3,2},{4,5},{5,4},{6,7},{7,6},{8,9},{9,8},{10,11... | collective-permute-start | bytes 73736 | tf_op jit(solution)/shard_map/ppermute | solution.py:410
  1.2 8.8 %collective-permute-start = (f32[1,32,64]{2,1,0:T(8,128)}, f32[1,32,64]{2,1,0:T(8,128)S(1)}, u32[]{:S(2)}, u32[]{:S(2)}) collective-permute-start(f32[1,32,64]{2,1,0:T(8,128)} %param.10), channel_id=1, source_target_pairs={{0,16},{2,18},{4,20},{6,22},{8,24},{10,26},{12,28},{14,30},{16,0},... | collective-permute-start | bytes 24584 | tf_op jit(solution)/shard_map/ppermute | solution.py:407
  4.8 12.9 %collective-permute-start.4 = (bf16[64,1536]{1,0:T(8,128)(2,1)}, bf16[64,1536]{1,0:T(8,128)(2,1)S(1)}, u32[]{:S(2)}, u32[]{:S(2)}) collective-permute-start(bf16[64,1536]{1,0:T(8,128)(2,1)} %refs_0_.4), channel_id=1, source_target_pairs={{0,1},{1,0},{2,3},{3,2},{4,5},{5,4},{6,7},{7,6},{8,9},{9,8},{10,11... | collective-permute-start | bytes 589832 | tf_op jit(solution)/shard_map/ppermute | solution.py:410
  5.0 12.8 %collective-permute-start.5 = (bf16[19,1536]{1,0:T(8,128)(2,1)}, bf16[19,1536]{1,0:T(8,128)(2,1)S(1)}, u32[]{:S(2)}, u32[]{:S(2)}) collective-permute-start(bf16[19,1536]{1,0:T(8,128)(2,1)} %refs_1_.4), channel_id=1, source_target_pairs={{0,1},{1,0},{2,3},{3,2},{4,5},{5,4},{6,7},{7,6},{8,9},{9,8},{10,11... | collective-permute-start | bytes 175112 | tf_op jit(solution)/shard_map/ppermute | solution.py:410
  5.3 17.7 %collective-permute-start.7 = (bf16[64,1536]{1,0:T(8,128)(2,1)}, bf16[64,1536]{1,0:T(8,128)(2,1)S(1)}, u32[]{:S(2)}, u32[]{:S(2)}) collective-permute-start(bf16[64,1536]{1,0:T(8,128)(2,1)} %bitcast.7), channel_id=1, source_target_pairs={{0,1},{1,0},{2,3},{3,2},{4,5},{5,4},{6,7},{7,6},{8,9},{9,8},{10,11... | collective-permute-start | bytes 589832 | tf_op jit(solution)/shard_map/ppermute | solution.py:410
  10.1 6.0 %collective-permute-start.2 = (f32[1,32,128]{2,1,0:T(8,128)S(1)}, f32[1,32,128]{2,1,0:T(8,128)S(1)}, u32[]{:S(2)}, u32[]{:S(2)}) collective-permute-start(f32[1,32,128]{2,1,0:T(8,128)S(1)} %pad_maximum_fusion.3), channel_id=1, source_target_pairs={{0,8},{2,10},{4,12},{6,14},{8,0},{10,2},{12,4},{14,6},{16,24},{18,... | collective-permute-start | bytes 49160 | tf_op jit(solution)/shard_map/ppermute | solution.py:407
  16.2 5.3 %collective-permute-start.3 = (f32[2,32,128]{2,1,0:T(8,128)S(1)}, f32[2,32,128]{2,1,0:T(8,128)S(1)}, u32[]{:S(2)}, u32[]{:S(2)}) collective-permute-start(f32[2,32,128]{2,1,0:T(8,128)S(1)} %pad_maximum_fusion.2), channel_id=1, source_target_pairs={{0,4},{2,6},{4,0},{6,2},{8,12},{10,14},{12,8},{14,10},{16,20},{18,... | collective-permute-start | bytes 98312 | tf_op jit(solution)/shard_map/ppermute | solution.py:407
  21.4 6.5 %copy-start = (f32[3,32,64]{2,1,0:T(8,128)S(1)}, f32[3,32,64]{2,1,0:T(8,128)}, u32[]{:S(2)}) copy-start(f32[3,32,64]{2,1,0:T(8,128)} %refs_5_.8) | copy-start | bytes 73732
  21.4 6.5 %copy-start.1 = (f32[2,768]{1,0:T(2,128)S(1)}, f32[2,768]{1,0:T(2,128)}, u32[]{:S(2)}) copy-start(f32[2,768]{1,0:T(2,128)} %refs_5_.9) | copy-start | bytes 18436
  21.4 6.5 %copy-start.2 = (s32[16]{0:T(128)S(1)}, s32[16]{0:T(128)}, u32[]{:S(2)}) copy-start(s32[16]{0:T(128)} %refs_0_.7) | copy-start | bytes 196
  21.5 6.5 %copy-start.3 = (s32[16]{0:T(128)S(1)}, s32[16]{0:T(128)}, u32[]{:S(2)}) copy-start(s32[16]{0:T(128)} %refs_1_.7) | copy-start | bytes 196
  21.5 5.0 %collective-permute-start.6 = (f32[4,32,128]{2,1,0:T(8,128)S(1)}, f32[4,32,128]{2,1,0:T(8,128)S(1)}, u32[]{:S(2)}, u32[]{:S(2)}) collective-permute-start(f32[4,32,128]{2,1,0:T(8,128)S(1)} %pad_maximum_fusion.1), channel_id=1, source_target_pairs={{0,2},{2,0},{4,6},{6,4},{8,10},{10,8},{12,14},{14,12},{16,18},{18,... | collective-permute-start | bytes 196616 | tf_op jit(solution)/shard_map/ppermute | solution.py:407
  26.5 1.4 %collective-permute-start.8 = (f32[8,32,128]{2,1,0:T(8,128)S(1)}, f32[8,32,128]{2,1,0:T(8,128)S(1)}, u32[]{:S(2)}, u32[]{:S(2)}) collective-permute-start(f32[8,32,128]{2,1,0:T(8,128)S(1)} %pad_maximum_fusion.refs_2_), channel_id=1, source_target_pairs={{0,1},{1,0},{2,3},{3,2},{4,5},{5,4},{6,7},{7,6},{8,9},{9,8},{10,11... | collective-permute-start | bytes 393224 | tf_op jit(solution)/shard_map/ppermute | solution.py:410

commit v12 on v10

--- a/solution.py
+++ b/solution.py
@@ -105,9 +105,9 @@
         if own:
             total_ref[spot, :] = total
         elif chunk < per:
-            mq_ref[where, :] = halves(total, 1)
+            mq_ref[where, :] = total.astype(BF16)
         else:
-            mk_ref[:, where] = halves(total.T, 0)
+            mk_ref[:, where] = total.T.astype(BF16)
 
 
 def values_kernel(rows, shares, right_ref, down_ref, *refs):
@@ -131,7 +131,7 @@
         if own:
             (mv_ref if place < per else wo_ref)[where, :] = total
         elif place < per:
-            mv_ref[where, :] = halves(total, 1)
+            mv_ref[where, :] = total.astype(BF16)
         else:
             wo_ref[:, where] = halves(total.T, 0)
 
@@ -223,7 +223,6 @@
     aug = jnp.where(last_row, EPS * mean_t, aug_t).T
     eps_c = aug[:, base - 1 : base]
     aug_b = aug.astype(BF16)
-    both = jnp.concatenate([aug_b, aug_b], axis=1)
 
     hpart_ref[...] = dot(gv_ref[...], both_q)
     xq_ref[...] = state[:, queries]
@@ -233,11 +232,11 @@
     head_of = lambda axis: lax.broadcasted_iota(jnp.int32, (span, span), axis) // HD
     average = jnp.where(head_of(0) == head_of(1), 1.0 / HD, 0.0).astype(BF16)
     for at in range(0, width, span):
-        raw = dot(both, mk_ref[:, at : at + span])
+        raw = dot(aug_b, mk_ref[:, at : at + span])
         spread = dot((raw * raw).astype(BF16), average)
         kbuf[:, at : at + span] = (raw * lax.rsqrt(spread + eps_c) * gain[:, at : at + span]).astype(BF16)
-    vbuf[...] = (dot(mv_ref[...], both_t) * lax.rsqrt(mean_t)).astype(BF16)
-    raw = dot(mq_ref[...], both_q).reshape(heads, HD, query_lanes)
+    vbuf[...] = (dot(mv_ref[...], aug_tb) * lax.rsqrt(mean_t)).astype(BF16)
+    raw = dot(mq_ref[...], aug_qb).reshape(heads, HD, query_lanes)
     spread = jnp.sum(raw * raw, axis=1, keepdims=True) * (1.0 / HD)
     qbuf[...] = (raw * lax.rsqrt(spread + EPS * mean_q)[:, :, :]).reshape(width, query_lanes).astype(BF16)
 
@@ -453,15 +452,15 @@
 
     def other_keys(*after):
         outs = [
-            shape((width, 2 * base), BF16),
-            shape((2 * base, width), BF16),
+            shape((width, base), BF16),
+            shape((base, width), BF16),
             shape((base, 2 * base), BF16),
             shape((channels, 2 * base), BF16),
         ]
         return weights(keys_part, others, outs + turned_tables(parts - 1), (), after, *tables, *done[0][:3])
 
     def other_values(*after):
-        outs = [shape((width, 2 * base), BF16), shape((2 * channels, width), BF16)]
+        outs = [shape((width, base), BF16), shape((2 * channels, width), BF16)]
         return weights(values_part, others, outs, (), after, *done[2][4:], *done[1])
 
     state = latent

time: 93.5 us -> 94 us (level)
  no operation moved by 1% of the time
where the time goes in v12:
time: 94 us; the launch traced here: 93.4 us
  Pallas kernels  75.2 us (80%)
  starting transfers between devices  9.92 us (11%)
  blocking collectives  5.98 us (6%)
  waiting for transfers between devices  1.36 us (1%)
    pallas_call x3, Pallas kernels, body(): pl.pallas_call(functools.partial(step_kernel, step, cfg), out_shape=tuple...  58.5 us
    pallas_call x4, Pallas kernels, weights(): pl.pallas_call(functools.partial(kernel, shares), out_shape=tuple(outs),...  16 us
    ppermute x4, starting transfers between devices, swapped(): lax.ppermute(value, axis, [(source, source ^ distance) for source in rang...  8.83 us
    all_gather x3, blocking collectives, body(): gathered = lax.all_gather(part, 'tok', axis=0, tiled=False)  5.98 us
  transfers between devices with their start and end apart: 9, of which 1 were waited for; matrix products, arithmetic and copies ran while one was open for 0% of the time, Pallas kernels for 17%

profile of v12, /device:TPU:0, one launch (start us, length us, event | category | flops | bytes accessed | tf_op | source)
XLA Modules:
  0.0 93.4 jit_solution(17636047143864933826)
XLA Ops:
  0.6 4.1 %collective-permute-start = (f32[1,32,64]{2,1,0:T(8,128)}, f32[1,32,64]{2,1,0:T(8,128)S(1)}, u32[]{:S(2)}, u32[]{:S(2)}) collective-permute-start(f32[1,32,64]{2,1,0:T(8,128)} %param.10), channel_id=1, source_target_pairs={{0,16},{2,18},{4,20},{6,22},{8,24},{10,26},{12,28},{14,30},{16,0},... | collective-permute-start | bytes 24584 | tf_op jit(solution)/shard_map/ppermute | solution.py:400
  4.7 0.5 collective-permute-start.5
  5.3 0.5 collective-permute-start.4
  5.8 4.6 %weights.4 = (f32[1536,128]{1,0:T(8,128)S(1)}, f32[128,128]{1,0:T(8,128)S(1)}, f32[64,128]{1,0:T(8,128)S(1)}, bf16[1536,128]{1,0:T(8,128)(2,1)S(1)}, bf16[1536,64]{1,0:T(8,128)(2,1)S(1)}) custom-call(bf16[64,1536]{1,0:T(8,128)(2,1)} %refs_0_.4, bf16[19,1536]{1,0:T(8,128)(2,1)} %refs_1_.4, bf16[64,1536]{1,0:T(8,128)(2,1)} %bitcast.8, ...), custom_call_target="tpu_custom_call" | custom-call | flops 603979776 | bytes 4718592 | tf_op jit(solution)/shard_map/weights/pallas_call | solution.py:422
  10.4 0.1 pad_maximum_fusion.3
  10.5 1.6 %collective-permute-start.2 = (f32[1,32,128]{2,1,0:T(8,128)S(1)}, f32[1,32,128]{2,1,0:T(8,128)S(1)}, u32[]{:S(2)}, u32[]{:S(2)}) collective-permute-start(f32[1,32,128]{2,1,0:T(8,128)S(1)} %pad_maximum_fusion.3), channel_id=1, source_target_pairs={{0,8},{2,10},{4,12},{6,14},{8,0},{10,2},{12,4},{14,6},{16,24},{18,... | collective-permute-start | bytes 49160 | tf_op jit(solution)/shard_map/ppermute | solution.py:400
  12.1 4.3 %weights.5 = (f32[768,128]{1,0:T(8,128)S(1)}, f32[768,64]{1,0:T(8,128)S(1)}) custom-call(bf16[1536,128]{1,0:T(8,128)(2,1)S(1)} %get-tuple-element.58.refs_0_, bf16[1536,64]{1,0:T(8,128)(2,1)S(1)} %get-tuple-element.59.refs_1_, bf16[3,768,3072]{2,1,0:T(8,128)(2,1)} %refs_4_.3, bf16[768,3072]{1,0:T(8,128)(2,1)} %refs_5_.4, ...), custom_call_target="tpu_custom_call" | custom-call | flops 603979776 | bytes 4718592 | tf_op jit(solution)/shard_map/weights/pallas_call | solution.py:422
  16.4 1.6 %collective-permute-start.3 = (f32[2,32,128]{2,1,0:T(8,128)S(1)}, f32[2,32,128]{2,1,0:T(8,128)S(1)}, u32[]{:S(2)}, u32[]{:S(2)}) collective-permute-start(f32[2,32,128]{2,1,0:T(8,128)S(1)} %pad_maximum_fusion.2), channel_id=1, source_target_pairs={{0,4},{2,6},{4,0},{6,2},{8,12},{10,14},{12,8},{14,10},{16,20},{18,... | collective-permute-start | bytes 98312 | tf_op jit(solution)/shard_map/ppermute | solution.py:400
  18.0 3.7 %weights.6 = (bf16[768,128]{1,0:T(8,128)(2,1)S(1)}, bf16[128,768]{1,0:T(8,128)(2,1)S(1)}, bf16[128,256]{1,0:T(8,128)(2,1)S(1)}, bf16[64,256]{1,0:T(8,128)(2,1)S(...) custom-call(bf16[64,1536]{1,0:T(8,128)(2,1)S(1)} %collective-permute-done.4.refs_0_, ...), custom_call_target="tpu_custom_call" | custom-call | flops 603979776 | bytes 4718592 | tf_op jit(solution)/shard_map/weights/pallas_call | solution.py:422
  21.7 0.0 copy-start
  21.7 0.0 copy-start.1
  21.7 0.0 copy-start.2
  21.7 0.0 copy-start.3
  21.8 1.6 %collective-permute-start.7 = (f32[4,32,128]{2,1,0:T(8,128)S(1)}, f32[4,32,128]{2,1,0:T(8,128)S(1)}, u32[]{:S(2)}, u32[]{:S(2)}) collective-permute-start(f32[4,32,128]{2,1,0:T(8,128)S(1)} %pad_maximum_fusion.1), channel_id=1, source_target_pairs={{0,2},{2,0},{4,6},{6,4},{8,10},{10,8},{12,14},{14,12},{16,18},{18,... | collective-permute-start | bytes 196616 | tf_op jit(solution)/shard_map/ppermute | solution.py:400
  23.3 3.4 %weights.7 = (bf16[768,128]{1,0:T(8,128)(2,1)S(1)}, bf16[128,768]{1,0:T(8,128)(2,1)S(1)}) custom-call(bf16[1536,128]{1,0:T(8,128)(2,1)S(1)} %get-tuple-element.75.refs_0_, bf16[1536,64]{1,0:T(8,128)(2,1)S(1)} %get-tuple-element.76.refs_1_, f32[768,128]{1,0:T(8,128)S(1)} %get-tuple-element.77.refs_2_, f32[768,64]{1,0:T(8,128)S(1)} %get-tuple-element.78.refs_3_, ...), custom_call_target="tpu_custom_call" | custom-call | flops 603979776 | bytes 4718592 | tf_op jit(solution)/shard_map/weights/pallas_call | solution.py:422
  26.7 0.1 collective-permute-start.8
  26.8 1.3 %collective-permute-done.8.refs_3_ = f32[8,32,128]{2,1,0:T(8,128)S(1)} collective-permute-done((f32[8,32,128]{2,1,0:T(8,128)S(1)}, f32[8,32,128]{2,1,0:T(8,128)S(1)}, u32[]{:S(2)}, u32[]{:S(2)}) %collective-permute-start.8) | collective-permute-done | bytes 131104 | tf_op jit(solution)/shard_map/ppermute | solution.py:403
  28.2 33.2 %step0.1 = (f32[64,896]{1,0:T(8,128)S(1)}, f32[64,896]{1,0:T(8,128)S(1)}, f32[64,896]{1,0:T(8,128)S(1)}) custom-call(s32[16]{0:T(128)S(1)} %copy-done.2, s32[16]{0:T(128)S(1)} %copy-done.3, f32[8,32,128]{2,1,0:T(8,128)S(1)} %pad_maximum_fusion.refs_2_, f32[8,32,128]{2,1,0:T(8,128)S(1)} %collective-permute-done.8.refs_3_, ...), custom_call_target="tpu_custom_call" | custom-call | flops 2919235584 | bytes 786432 | tf_op jit(solution)/shard_map/step0/pallas_call | solution.py:507
  61.4 2.1 %all-gather = f32[128,896]{1,0:T(8,128)S(1)} all-gather(f32[64,896]{1,0:T(8,128)S(1)} %get-tuple-element.89), channel_id=2, replica_groups=mesh['queue'=16,'tok'=2] {'tok'}, dimensions={0}, use_global_device_ids=true | all-gather | bytes 688128 | tf_op jit(solution)/shard_map/all_gather | solution.py:530
  63.5 19.3 %step1.1 = (f32[64,512]{1,0:T(8,128)S(1)}, f32[64,512]{1,0:T(8,128)S(1)}, f32[64,512]{1,0:T(8,128)S(1)}, f32[32,64]{1,0:T(8,128)S(1)}) custom-call(s32[16]{0:T(128)S(1)} %copy-done.2, s32[16]{0:T(128)S(1)} %copy-done.3, f32[2,64,896]{2,1,0:T(8,128)S(1)} %bitcast.4, f32[64,896]{1,0:T(8,128)S(1)} %get-tuple-element.90.refs_3_, ...), custom_call_target="tpu_custom_call" | custom-call | flops 1862270976 | bytes 786432 | tf_op jit(solution)/shard_map/step1/pallas_call | solution.py:507
  82.8 2.0 %all-gather.1 = f32[128,512]{1,0:T(8,128)S(1)} all-gather(f32[64,512]{1,0:T(8,128)S(1)} %get-tuple-element.92), channel_id=3, replica_groups=mesh['queue'=16,'tok'=2] {'tok'}, dimensions={0}, use_global_device_ids=true | all-gather | bytes 393216 | tf_op jit(solution)/shard_map/all_gather | solution.py:530
  84.8 6.0 %step2.1 = (f32[64,128]{1,0:T(8,128)S(1)}, f32[64,128]{1,0:T(8,128)S(1)}, f32[64,128]{1,0:T(8,128)S(1)}, f32[32,64]{1,0:T(8,128)S(1)}) custom-call(s32[16]{0:T(128)S(1)} %copy-done.2, s32[16]{0:T(128)S(1)} %copy-done.3, f32[2,64,512]{2,1,0:T(8,128)S(1)} %bitcast.5, f32[64,512]{1,0:T(8,128)S(1)} %get-tuple-element.93.refs_3_, ...), custom_call_target="tpu_custom_call" | custom-call | flops 805306368 | bytes 786432 | tf_op jit(solution)/shard_map/step2/pallas_call | solution.py:507
  90.8 1.9 %all-gather.2 = f32[128,128]{1,0:T(8,128)S(1)} all-gather(f32[64,128]{1,0:T(8,128)S(1)} %get-tuple-element.95), channel_id=4, replica_groups=mesh['queue'=16,'tok'=2] {'tok'}, dimensions={0}, use_global_device_ids=true | all-gather | bytes 98304 | tf_op jit(solution)/shard_map/all_gather | solution.py:530
  92.7 0.7 last.1
  (19 shorter events, 0.1 us)
Async XLA Ops:
  0.6 9.8 %copy-start.4 = (f32[1,32,64]{2,1,0:T(8,128)S(1)}, f32[1,32,64]{2,1,0:T(8,128)}, u32[]{:S(2)}) copy-start(f32[1,32,64]{2,1,0:T(8,128)} %param.10) | copy-start | bytes 24580
  0.6 9.7 %collective-permute-start = (f32[1,32,64]{2,1,0:T(8,128)}, f32[1,32,64]{2,1,0:T(8,128)S(1)}, u32[]{:S(2)}, u32[]{:S(2)}) collective-permute-start(f32[1,32,64]{2,1,0:T(8,128)} %param.10), channel_id=1, source_target_pairs={{0,16},{2,18},{4,20},{6,22},{8,24},{10,26},{12,28},{14,30},{16,0},... | collective-permute-start | bytes 24584 | tf_op jit(solution)/shard_map/ppermute | solution.py:400
  4.7 5.6 %collective-permute-start.1 = (f32[3,32,64]{2,1,0:T(8,128)}, f32[3,32,64]{2,1,0:T(8,128)S(1)}, u32[]{:S(2)}, u32[]{:S(2)}) collective-permute-start(f32[3,32,64]{2,1,0:T(8,128)} %refs_5_.6), channel_id=1, source_target_pairs={{0,1},{1,0},{2,3},{3,2},{4,5},{5,4},{6,7},{7,6},{8,9},{9,8},{10,11... | collective-permute-start | bytes 73736 | tf_op jit(solution)/shard_map/ppermute | solution.py:403
  4.7 13.3 %collective-permute-start.5 = (bf16[19,1536]{1,0:T(8,128)(2,1)}, bf16[19,1536]{1,0:T(8,128)(2,1)S(1)}, u32[]{:S(2)}, u32[]{:S(2)}) collective-permute-start(bf16[19,1536]{1,0:T(8,128)(2,1)} %refs_1_.4), channel_id=1, source_target_pairs={{0,1},{1,0},{2,3},{3,2},{4,5},{5,4},{6,7},{7,6},{8,9},{9,8},{10,11... | collective-permute-start | bytes 175112 | tf_op jit(solution)/shard_map/ppermute | solution.py:403
  5.3 12.8 %collective-permute-start.6 = (bf16[64,1536]{1,0:T(8,128)(2,1)}, bf16[64,1536]{1,0:T(8,128)(2,1)S(1)}, u32[]{:S(2)}, u32[]{:S(2)}) collective-permute-start(bf16[64,1536]{1,0:T(8,128)(2,1)} %bitcast.7), channel_id=1, source_target_pairs={{0,1},{1,0},{2,3},{3,2},{4,5},{5,4},{6,7},{7,6},{8,9},{9,8},{10,11... | collective-permute-start | bytes 589832 | tf_op jit(solution)/shard_map/ppermute | solution.py:403
  5.3 12.8 %collective-permute-start.4 = (bf16[64,1536]{1,0:T(8,128)(2,1)}, bf16[64,1536]{1,0:T(8,128)(2,1)S(1)}, u32[]{:S(2)}, u32[]{:S(2)}) collective-permute-start(bf16[64,1536]{1,0:T(8,128)(2,1)} %refs_0_.4), channel_id=1, source_target_pairs={{0,1},{1,0},{2,3},{3,2},{4,5},{5,4},{6,7},{7,6},{8,9},{9,8},{10,11... | collective-permute-start | bytes 589832 | tf_op jit(solution)/shard_map/ppermute | solution.py:403
  10.5 5.9 %collective-permute-start.2 = (f32[1,32,128]{2,1,0:T(8,128)S(1)}, f32[1,32,128]{2,1,0:T(8,128)S(1)}, u32[]{:S(2)}, u32[]{:S(2)}) collective-permute-start(f32[1,32,128]{2,1,0:T(8,128)S(1)} %pad_maximum_fusion.3), channel_id=1, source_target_pairs={{0,8},{2,10},{4,12},{6,14},{8,0},{10,2},{12,4},{14,6},{16,24},{18,... | collective-permute-start | bytes 49160 | tf_op jit(solution)/shard_map/ppermute | solution.py:400
  16.4 5.3 %collective-permute-start.3 = (f32[2,32,128]{2,1,0:T(8,128)S(1)}, f32[2,32,128]{2,1,0:T(8,128)S(1)}, u32[]{:S(2)}, u32[]{:S(2)}) collective-permute-start(f32[2,32,128]{2,1,0:T(8,128)S(1)} %pad_maximum_fusion.2), channel_id=1, source_target_pairs={{0,4},{2,6},{4,0},{6,2},{8,12},{10,14},{12,8},{14,10},{16,20},{18,... | collective-permute-start | bytes 98312 | tf_op jit(solution)/shard_map/ppermute | solution.py:400
  21.7 6.5 %copy-start = (f32[3,32,64]{2,1,0:T(8,128)S(1)}, f32[3,32,64]{2,1,0:T(8,128)}, u32[]{:S(2)}) copy-start(f32[3,32,64]{2,1,0:T(8,128)} %refs_5_.6) | copy-start | bytes 73732
  21.7 6.4 %copy-start.1 = (f32[2,768]{1,0:T(2,128)S(1)}, f32[2,768]{1,0:T(2,128)}, u32[]{:S(2)}) copy-start(f32[2,768]{1,0:T(2,128)} %refs_5_.7) | copy-start | bytes 18436
  21.7 6.4 %copy-start.2 = (s32[16]{0:T(128)S(1)}, s32[16]{0:T(128)}, u32[]{:S(2)}) copy-start(s32[16]{0:T(128)} %refs_0_.7) | copy-start | bytes 196
  21.7 6.4 %copy-start.3 = (s32[16]{0:T(128)S(1)}, s32[16]{0:T(128)}, u32[]{:S(2)}) copy-start(s32[16]{0:T(128)} %refs_1_.7) | copy-start | bytes 196
  21.8 4.9 %collective-permute-start.7 = (f32[4,32,128]{2,1,0:T(8,128)S(1)}, f32[4,32,128]{2,1,0:T(8,128)S(1)}, u32[]{:S(2)}, u32[]{:S(2)}) collective-permute-start(f32[4,32,128]{2,1,0:T(8,128)S(1)} %pad_maximum_fusion.1), channel_id=1, source_target_pairs={{0,2},{2,0},{4,6},{6,4},{8,10},{10,8},{12,14},{14,12},{16,18},{18,... | collective-permute-start | bytes 196616 | tf_op jit(solution)/shard_map/ppermute | solution.py:400
  26.7 1.4 %collective-permute-start.8 = (f32[8,32,128]{2,1,0:T(8,128)S(1)}, f32[8,32,128]{2,1,0:T(8,128)S(1)}, u32[]{:S(2)}, u32[]{:S(2)}) collective-permute-start(f32[8,32,128]{2,1,0:T(8,128)S(1)} %pad_maximum_fusion.refs_2_), channel_id=1, source_target_pairs={{0,1},{1,0},{2,3},{3,2},{4,5},{5,4},{6,7},{7,6},{8,9},{9,8},{10,11... | collective-permute-start | bytes 393224 | tf_op jit(solution)/shard_map/ppermute | solution.py:403

commit v13 on v11

--- a/solution.py
+++ b/solution.py
@@ -418,7 +418,7 @@
     in_hbm = lambda array: pltpu.with_memory_space_constraint(array, pltpu.HBM)
     table = tuple(in_hbm(piece) for piece in table)
     qkv_weight, out_weight = in_hbm(qkv_weight), in_hbm(out_weight)
-    rows = 384 if width % 384 == 0 else 256
+    rows = 768 if width % 768 == 0 else 256
     chunks = 2 * width // rows
 
     def weights(kernel, shares, outs, held, after, *operands):

time: 94.1 us -> 93.4 us (level)
    pallas_call x3, Pallas kernels: 59.3 us -> 58.3 us  [body(): pl.pallas_call(functools.partial(step_kernel, step, cfg), out_shape=tuple...]
where the time goes in v13:
time: 93.4 us; the launch traced here: 93.1 us
  Pallas kernels  75.1 us (80%)
  starting transfers between devices  9.65 us (10%)
  blocking collectives  5.98 us (6%)
  waiting for transfers between devices  1.36 us (1%)
    pallas_call x3, Pallas kernels, body(): pl.pallas_call(functools.partial(step_kernel, step, cfg), out_shape=tuple...  58.3 us
    pallas_call x4, Pallas kernels, weights(): pl.pallas_call(functools.partial(kernel, shares), out_shape=tuple(outs),...  16.1 us
    ppermute x4, starting transfers between devices, swapped(): lax.ppermute(value, axis, [(source, source ^ distance) for source in rang...  8.39 us
    all_gather x3, blocking collectives, body(): gathered = lax.all_gather(part, 'tok', axis=0, tiled=False)  5.98 us
  transfers between devices with their start and end apart: 9, of which 1 were waited for; matrix products, arithmetic and copies ran while one was open for 0% of the time, Pallas kernels for 17%

profile of v13, /device:TPU:0, one launch (start us, length us, event | category | flops | bytes accessed | tf_op | source)
XLA Modules:
  0.0 93.1 jit_solution(14756695689502268976)
XLA Ops:
  0.6 0.5 collective-permute-start.1
  1.2 3.7 %collective-permute-start = (f32[1,32,64]{2,1,0:T(8,128)}, f32[1,32,64]{2,1,0:T(8,128)S(1)}, u32[]{:S(2)}, u32[]{:S(2)}) collective-permute-start(f32[1,32,64]{2,1,0:T(8,128)} %param.10), channel_id=1, source_target_pairs={{0,16},{2,18},{4,20},{6,22},{8,24},{10,26},{12,28},{14,30},{16,0},... | collective-permute-start | bytes 24584 | tf_op jit(solution)/shard_map/ppermute | solution.py:407
  4.8 0.2 collective-permute-start.4
  5.0 0.3 collective-permute-start.5
  5.3 0.2 collective-permute-start.7
  5.5 4.6 %weights.4 = (f32[1536,128]{1,0:T(8,128)S(1)}, f32[128,128]{1,0:T(8,128)S(1)}, bf16[1536,128]{1,0:T(8,128)(2,1)S(1)}) custom-call(bf16[64,1536]{1,0:T(8,128)(2,1)} %refs_0_.4, bf16[19,1536]{1,0:T(8,128)(2,1)} %refs_1_.4, bf16[3,768,3072]{2,1,0:T(8,128)(2,1)} %refs_5_.6, bf16[768,3072]{1,0:T(8,128)(2,1)} %refs_6_.3), custom_call_target="tpu_custom_call" | custom-call | flops 603979776 | bytes 4718592 | tf_op jit(solution)/shard_map/weights/pallas_call | solution.py:430
  10.1 0.1 pad_maximum_fusion.3
  10.2 1.6 %collective-permute-start.2 = (f32[1,32,128]{2,1,0:T(8,128)S(1)}, f32[1,32,128]{2,1,0:T(8,128)S(1)}, u32[]{:S(2)}, u32[]{:S(2)}) collective-permute-start(f32[1,32,128]{2,1,0:T(8,128)S(1)} %pad_maximum_fusion.3), channel_id=1, source_target_pairs={{0,8},{2,10},{4,12},{6,14},{8,0},{10,2},{12,4},{14,6},{16,24},{18,... | collective-permute-start | bytes 49160 | tf_op jit(solution)/shard_map/ppermute | solution.py:407
  11.8 4.5 %weights.5 = (f32[768,128]{1,0:T(8,128)S(1)}, f32[768,64]{1,0:T(8,128)S(1)}, f32[64,128]{1,0:T(8,128)S(1)}) custom-call(bf16[64,1536]{1,0:T(8,128)(2,1)} %bitcast.8, bf16[1536,128]{1,0:T(8,128)(2,1)S(1)} %get-tuple-element.52.refs_1_, bf16[3,768,3072]{2,1,0:T(8,128)(2,1)} %refs_5_.6, bf16[768,3072]{1,0:T(8,128)(2,1)} %refs_6_.3, ...), custom_call_target="tpu_custom_call" | custom-call | flops 603979776 | bytes 4718592 | tf_op jit(solution)/shard_map/weights/pallas_call | solution.py:430
  16.3 1.6 %collective-permute-start.3 = (f32[2,32,128]{2,1,0:T(8,128)S(1)}, f32[2,32,128]{2,1,0:T(8,128)S(1)}, u32[]{:S(2)}, u32[]{:S(2)}) collective-permute-start(f32[2,32,128]{2,1,0:T(8,128)S(1)} %pad_maximum_fusion.2), channel_id=1, source_target_pairs={{0,4},{2,6},{4,0},{6,2},{8,12},{10,14},{12,8},{14,10},{16,20},{18,... | collective-permute-start | bytes 98312 | tf_op jit(solution)/shard_map/ppermute | solution.py:407
  17.9 3.6 %weights.6 = (bf16[768,128]{1,0:T(8,128)(2,1)S(1)}, bf16[128,768]{1,0:T(8,128)(2,1)S(1)}, bf16[128,256]{1,0:T(8,128)(2,1)S(1)}, bf16[1536,128]{1,0:T(8,128)(2,1)S(1)}) custom-call(bf16[64,1536]{1,0:T(8,128)(2,1)S(1)} %collective-permute-done.4.refs_0_, bf16[19,1536]{1,0:T(8,128)(2,1)S(1)} %collective-permute-done.5.refs_1_, ...), custom_call_target="tpu_custom_call" | custom-call | flops 603979776 | bytes 4718592 | tf_op jit(solution)/shard_map/weights/pallas_call | solution.py:430
  21.5 0.0 copy-start
  21.5 0.0 copy-start.1
  21.6 1.6 %collective-permute-start.6 = (f32[4,32,128]{2,1,0:T(8,128)S(1)}, f32[4,32,128]{2,1,0:T(8,128)S(1)}, u32[]{:S(2)}, u32[]{:S(2)}) collective-permute-start(f32[4,32,128]{2,1,0:T(8,128)S(1)} %pad_maximum_fusion.1), channel_id=1, source_target_pairs={{0,2},{2,0},{4,6},{6,4},{8,10},{10,8},{12,14},{14,12},{16,18},{18,... | collective-permute-start | bytes 196616 | tf_op jit(solution)/shard_map/ppermute | solution.py:407
  23.2 3.4 %weights.7 = (bf16[768,128]{1,0:T(8,128)(2,1)S(1)}, bf16[128,768]{1,0:T(8,128)(2,1)S(1)}, bf16[64,256]{1,0:T(8,128)(2,1)S(1)}) custom-call(bf16[64,1536]{1,0:T(8,128)(2,1)S(1)} %collective-permute-done.7.refs_0_, bf16[1536,128]{1,0:T(8,128)(2,1)S(1)} %get-tuple-element.66.refs_1_, f32[768,128]{1,0:T(8,128)S(1)} %get-tuple-element.67.refs_2_, ...), custom_call_target="tpu_custom_call" | custom-call | flops 603979776 | bytes 4718592 | tf_op jit(solution)/shard_map/weights/pallas_call | solution.py:430
  26.6 0.1 collective-permute-start.8
  26.7 1.3 %collective-permute-done.8.refs_3_ = f32[8,32,128]{2,1,0:T(8,128)S(1)} collective-permute-done((f32[8,32,128]{2,1,0:T(8,128)S(1)}, f32[8,32,128]{2,1,0:T(8,128)S(1)}, u32[]{:S(2)}, u32[]{:S(2)}) %collective-permute-start.8) | collective-permute-done | bytes 131104 | tf_op jit(solution)/shard_map/ppermute | solution.py:410
  28.0 33.0 %step0.1 = (f32[64,896]{1,0:T(8,128)S(1)}, f32[64,896]{1,0:T(8,128)S(1)}, f32[64,896]{1,0:T(8,128)S(1)}) custom-call(s32[16]{0:T(128)S(1)} %copy-done.2, s32[16]{0:T(128)S(1)} %copy-done.3, f32[8,32,128]{2,1,0:T(8,128)S(1)} %pad_maximum_fusion.refs_2_, f32[8,32,128]{2,1,0:T(8,128)S(1)} %collective-permute-done.8.refs_3_, ...), custom_call_target="tpu_custom_call" | custom-call | flops 2919235584 | bytes 786432 | tf_op jit(solution)/shard_map/step0/pallas_call | solution.py:519
  61.1 2.1 %all-gather = f32[128,896]{1,0:T(8,128)S(1)} all-gather(f32[64,896]{1,0:T(8,128)S(1)} %get-tuple-element.81), channel_id=2, replica_groups=mesh['queue'=16,'tok'=2] {'tok'}, dimensions={0}, use_global_device_ids=true | all-gather | bytes 688128 | tf_op jit(solution)/shard_map/all_gather | solution.py:542
  63.2 19.3 %step1.1 = (f32[64,512]{1,0:T(8,128)S(1)}, f32[64,512]{1,0:T(8,128)S(1)}, f32[64,512]{1,0:T(8,128)S(1)}, f32[32,64]{1,0:T(8,128)S(1)}) custom-call(s32[16]{0:T(128)S(1)} %copy-done.2, s32[16]{0:T(128)S(1)} %copy-done.3, f32[2,64,896]{2,1,0:T(8,128)S(1)} %bitcast.4, f32[64,896]{1,0:T(8,128)S(1)} %get-tuple-element.82.refs_3_, ...), custom_call_target="tpu_custom_call" | custom-call | flops 1862270976 | bytes 786432 | tf_op jit(solution)/shard_map/step1/pallas_call | solution.py:519
  82.5 2.0 %all-gather.1 = f32[128,512]{1,0:T(8,128)S(1)} all-gather(f32[64,512]{1,0:T(8,128)S(1)} %get-tuple-element.84), channel_id=3, replica_groups=mesh['queue'=16,'tok'=2] {'tok'}, dimensions={0}, use_global_device_ids=true | all-gather | bytes 393216 | tf_op jit(solution)/shard_map/all_gather | solution.py:542
  84.5 6.0 %step2.1 = (f32[64,128]{1,0:T(8,128)S(1)}, f32[64,128]{1,0:T(8,128)S(1)}, f32[64,128]{1,0:T(8,128)S(1)}, f32[32,64]{1,0:T(8,128)S(1)}) custom-call(s32[16]{0:T(128)S(1)} %copy-done.2, s32[16]{0:T(128)S(1)} %copy-done.3, f32[2,64,512]{2,1,0:T(8,128)S(1)} %bitcast.5, f32[64,512]{1,0:T(8,128)S(1)} %get-tuple-element.85.refs_3_, ...), custom_call_target="tpu_custom_call" | custom-call | flops 805306368 | bytes 786432 | tf_op jit(solution)/shard_map/step2/pallas_call | solution.py:519
  90.5 1.9 %all-gather.2 = f32[128,128]{1,0:T(8,128)S(1)} all-gather(f32[64,128]{1,0:T(8,128)S(1)} %get-tuple-element.87), channel_id=4, replica_groups=mesh['queue'=16,'tok'=2] {'tok'}, dimensions={0}, use_global_device_ids=true | all-gather | bytes 98304 | tf_op jit(solution)/shard_map/all_gather | solution.py:542
  92.4 0.7 last.1
  (19 shorter events, 0.1 us)
Async XLA Ops:
  0.6 9.5 %copy-start.4 = (f32[1,32,64]{2,1,0:T(8,128)S(1)}, f32[1,32,64]{2,1,0:T(8,128)}, u32[]{:S(2)}) copy-start(f32[1,32,64]{2,1,0:T(8,128)} %param.10) | copy-start | bytes 24580
  0.6 9.5 %collective-permute-start.1 = (f32[3,32,64]{2,1,0:T(8,128)}, f32[3,32,64]{2,1,0:T(8,128)S(1)}, u32[]{:S(2)}, u32[]{:S(2)}) collective-permute-start(f32[3,32,64]{2,1,0:T(8,128)} %refs_5_.8), channel_id=1, source_target_pairs={{0,1},{1,0},{2,3},{3,2},{4,5},{5,4},{6,7},{7,6},{8,9},{9,8},{10,11... | collective-permute-start | bytes 73736 | tf_op jit(solution)/shard_map/ppermute | solution.py:410
  1.2 8.9 %collective-permute-start = (f32[1,32,64]{2,1,0:T(8,128)}, f32[1,32,64]{2,1,0:T(8,128)S(1)}, u32[]{:S(2)}, u32[]{:S(2)}) collective-permute-start(f32[1,32,64]{2,1,0:T(8,128)} %param.10), channel_id=1, source_target_pairs={{0,16},{2,18},{4,20},{6,22},{8,24},{10,26},{12,28},{14,30},{16,0},... | collective-permute-start | bytes 24584 | tf_op jit(solution)/shard_map/ppermute | solution.py:407
  4.8 13.1 %collective-permute-start.4 = (bf16[64,1536]{1,0:T(8,128)(2,1)}, bf16[64,1536]{1,0:T(8,128)(2,1)S(1)}, u32[]{:S(2)}, u32[]{:S(2)}) collective-permute-start(bf16[64,1536]{1,0:T(8,128)(2,1)} %refs_0_.4), channel_id=1, source_target_pairs={{0,1},{1,0},{2,3},{3,2},{4,5},{5,4},{6,7},{7,6},{8,9},{9,8},{10,11... | collective-permute-start | bytes 589832 | tf_op jit(solution)/shard_map/ppermute | solution.py:410
  5.0 12.9 %collective-permute-start.5 = (bf16[19,1536]{1,0:T(8,128)(2,1)}, bf16[19,1536]{1,0:T(8,128)(2,1)S(1)}, u32[]{:S(2)}, u32[]{:S(2)}) collective-permute-start(bf16[19,1536]{1,0:T(8,128)(2,1)} %refs_1_.4), channel_id=1, source_target_pairs={{0,1},{1,0},{2,3},{3,2},{4,5},{5,4},{6,7},{7,6},{8,9},{9,8},{10,11... | collective-permute-start | bytes 175112 | tf_op jit(solution)/shard_map/ppermute | solution.py:410
  5.3 17.8 %collective-permute-start.7 = (bf16[64,1536]{1,0:T(8,128)(2,1)}, bf16[64,1536]{1,0:T(8,128)(2,1)S(1)}, u32[]{:S(2)}, u32[]{:S(2)}) collective-permute-start(bf16[64,1536]{1,0:T(8,128)(2,1)} %bitcast.7), channel_id=1, source_target_pairs={{0,1},{1,0},{2,3},{3,2},{4,5},{5,4},{6,7},{7,6},{8,9},{9,8},{10,11... | collective-permute-start | bytes 589832 | tf_op jit(solution)/shard_map/ppermute | solution.py:410
  10.2 6.1 %collective-permute-start.2 = (f32[1,32,128]{2,1,0:T(8,128)S(1)}, f32[1,32,128]{2,1,0:T(8,128)S(1)}, u32[]{:S(2)}, u32[]{:S(2)}) collective-permute-start(f32[1,32,128]{2,1,0:T(8,128)S(1)} %pad_maximum_fusion.3), channel_id=1, source_target_pairs={{0,8},{2,10},{4,12},{6,14},{8,0},{10,2},{12,4},{14,6},{16,24},{18,... | collective-permute-start | bytes 49160 | tf_op jit(solution)/shard_map/ppermute | solution.py:407
  16.3 5.2 %collective-permute-start.3 = (f32[2,32,128]{2,1,0:T(8,128)S(1)}, f32[2,32,128]{2,1,0:T(8,128)S(1)}, u32[]{:S(2)}, u32[]{:S(2)}) collective-permute-start(f32[2,32,128]{2,1,0:T(8,128)S(1)} %pad_maximum_fusion.2), channel_id=1, source_target_pairs={{0,4},{2,6},{4,0},{6,2},{8,12},{10,14},{12,8},{14,10},{16,20},{18,... | collective-permute-start | bytes 98312 | tf_op jit(solution)/shard_map/ppermute | solution.py:407
  21.5 6.5 %copy-start = (f32[3,32,64]{2,1,0:T(8,128)S(1)}, f32[3,32,64]{2,1,0:T(8,128)}, u32[]{:S(2)}) copy-start(f32[3,32,64]{2,1,0:T(8,128)} %refs_5_.8) | copy-start | bytes 73732
  21.5 6.5 %copy-start.1 = (f32[2,768]{1,0:T(2,128)S(1)}, f32[2,768]{1,0:T(2,128)}, u32[]{:S(2)}) copy-start(f32[2,768]{1,0:T(2,128)} %refs_5_.9) | copy-start | bytes 18436
  21.6 6.5 %copy-start.2 = (s32[16]{0:T(128)S(1)}, s32[16]{0:T(128)}, u32[]{:S(2)}) copy-start(s32[16]{0:T(128)} %refs_0_.7) | copy-start | bytes 196
  21.6 6.5 %copy-start.3 = (s32[16]{0:T(128)S(1)}, s32[16]{0:T(128)}, u32[]{:S(2)}) copy-start(s32[16]{0:T(128)} %refs_1_.7) | copy-start | bytes 196
  21.6 5.0 %collective-permute-start.6 = (f32[4,32,128]{2,1,0:T(8,128)S(1)}, f32[4,32,128]{2,1,0:T(8,128)S(1)}, u32[]{:S(2)}, u32[]{:S(2)}) collective-permute-start(f32[4,32,128]{2,1,0:T(8,128)S(1)} %pad_maximum_fusion.1), channel_id=1, source_target_pairs={{0,2},{2,0},{4,6},{6,4},{8,10},{10,8},{12,14},{14,12},{16,18},{18,... | collective-permute-start | bytes 196616 | tf_op jit(solution)/shard_map/ppermute | solution.py:407
  26.6 1.4 %collective-permute-start.8 = (f32[8,32,128]{2,1,0:T(8,128)S(1)}, f32[8,32,128]{2,1,0:T(8,128)S(1)}, u32[]{:S(2)}, u32[]{:S(2)}) collective-permute-start(f32[8,32,128]{2,1,0:T(8,128)S(1)} %pad_maximum_fusion.refs_2_), channel_id=1, source_target_pairs={{0,1},{1,0},{2,3},{3,2},{4,5},{5,4},{6,7},{7,6},{8,9},{9,8},{10,11... | collective-permute-start | bytes 393224 | tf_op jit(solution)/shard_map/ppermute | solution.py:410
